TPU v7x, 512 devices: a whole 4x8x8 slice. The times are simulated.
512 devices in a mesh: band: 8 (over x, core), tile: 64 (over z, y).
Axes of the slice: x: 4, y: 8, z: 8, core: 2. Of those that a mesh axis runs over, the one named last changes fastest.
Arguments:
- coarse_blocks: bfloat16 [512, 4480], P('band'), may hold values from -6 to 6
- block_anchor: int32 [8, 64], replicated, may hold values from 0 to 511
- nest_width: int32 [8], P('band'), may hold values from 128 to 256, as said below
- sigmas: float32 [3], replicated, as said below
- noise: float32 [8, 4, 256, 256], P('band', None, 'tile'), may hold values from -6 to 6
- w_context: bfloat16 [256, 70], replicated, may hold values from -0.75 to 0.75
- w_in: bfloat16 [9, 128, 4], replicated, may hold values from -1 to 1
- w_sigma: float32 [128], replicated, may hold values from -4 to 4
- w_enc: bfloat16 [9, 128, 128], replicated, may hold values from -0.1875 to 0.1875
- w_down: bfloat16 [9, 256, 128], replicated, may hold values from -0.1875 to 0.1875
- w_mid: bfloat16 [9, 256, 256], replicated, may hold values from -0.125 to 0.125
- w_dec: bfloat16 [9, 128, 384], replicated, may hold values from -0.109375 to 0.109375
- w_out: bfloat16 [9, 4, 128], replicated, may hold values from -0.75 to 0.75
Outputs:
- downscaled: float32 [8, 4, 256, 256], P('band', None, 'tile')
Inputs may be any that keep to these rules, and one draw needn't show every extreme that they name: `nest_width`: one nest uses all 256 columns. `sigmas`: the levels fall strictly from each entry to the next.
All inputs are finite; a program needn't handle non-finite values.
Results may differ from a plain program's by a relative error of at most 0.014.
Values may be sent and summed in bfloat16 or wider, within the bound.
No kernel may reach another device: no remote copies, remote signals or barrier semaphores. Data moves between devices by JAX's collectives and lax.ppermute only.
A program may use at most 64 MiB of HBM per device.

v0:
```python
import math

import jax
import jax.numpy as jnp
from jax import lax
from jax.sharding import PartitionSpec as P

K = 96
STEPS = 2


SIGMA_DATA = 0.5


def with_halo(x, sides, width):
    for axis, dim in sides:
        size, length = (lax.axis_size(axis), x.shape[dim])
        up = [(i, (i + 1) % size) for i in range(size - 1)]
        down = [(j, i) for i, j in up]
        last = lax.slice_in_dim(x, length - width, length, axis=dim)
        first = lax.slice_in_dim(x, 0, width, axis=dim)
        before = lax.ppermute(last, axis, up)
        after = lax.ppermute(first, axis, down)
        x = jnp.concatenate([before, x, after], axis=dim)
    return x


def from_behind(x, axis, by):
    size = lax.axis_size(axis)
    pairs = [(i, i + by) for i in range(size) if 0 <= i + by < size]
    return lax.ppermute(x, axis, pairs)


def conv_taps(padded, weight, out_rows, out_cols, stride):
    channels = padded.shape[0]
    summed = jnp.zeros((weight.shape[1], out_rows, out_cols), jnp.float32)
    for tap_index in range(9):
        row_off = tap_index // 3
        col_off = tap_index % 3
        window = lax.slice(
            padded,
            (0, row_off, col_off),
            (
                channels,
                row_off + stride * (out_rows - 1) + 1,
                col_off + stride * (out_cols - 1) + 1,
            ),
            (1, stride, stride),
        )
        summed = summed + jnp.einsum(
            "oi,irc->orc", weight[tap_index], window, preferred_element_type=jnp.float32
        )
    return summed


def pad_cols(field_in):
    return jnp.pad(field_in, ((0, 0), (0, 0), (1, 1)))


def arrange(arrived, own_start, band_size):
    rolled = jnp.roll(arrived, -(own_start % band_size), axis=1)
    return rolled.reshape(arrived.shape[0] * band_size, arrived.shape[2])


def per_device(
    coarse_blocks,
    block_anchor,
    nest_width,
    sigmas,
    noise,
    w_context,
    w_in,
    w_sigma,
    w_enc,
    w_down,
    w_mid,
    w_dec,
    w_out,
):
    band_size = lax.axis_size("band")
    band_index = lax.axis_index("band")
    tile_index = lax.axis_index("tile")
    tile_rows = noise.shape[2]
    tile_cols = noise.shape[3]
    half_rows = tile_rows // 2
    half_cols = tile_cols // 2
    block_count = coarse_blocks.shape[0]
    coarse_chans = w_context.shape[1]
    hidden = w_context.shape[0]
    cell_count = coarse_blocks.shape[1] // coarse_chans
    slot_count = (K + band_size - 1) // band_size
    starts = lax.dynamic_index_in_dim(block_anchor, tile_index, 1, keepdims=False)
    own_start = lax.dynamic_index_in_dim(starts, band_index, 0, keepdims=False)
    offsets = (band_index - starts) % band_size
    positions = offsets[None, :] + jnp.arange(slot_count, dtype=jnp.int32)[:, None] * band_size
    is_valid = positions < K
    local_rows = jnp.where(
        is_valid, (starts[None, :] + positions) % (block_count * band_size) // band_size, 0
    )
    keep_mask = is_valid.astype(jnp.bfloat16)[:, :, None]
    outgoing = coarse_blocks[local_rows] * keep_mask
    arrived = lax.all_to_all(outgoing, "band", split_axis=1, concat_axis=1, tiled=True)
    ordered = arrange(arrived, own_start, band_size).reshape(K, coarse_chans, cell_count)
    features = jax.nn.silu(
        jnp.einsum("hc,kcb->khb", w_context, ordered, preferred_element_type=jnp.float32)
    ).astype(jnp.bfloat16)
    group_size = K // half_rows
    pooled = jnp.sum(
        features.reshape(half_rows, group_size, hidden, cell_count), axis=1, dtype=jnp.float32
    ) * (1.0 / math.sqrt(group_size))
    context_map = jnp.repeat(jnp.transpose(pooled, (1, 0, 2)), half_cols // cell_count, axis=2)
    width_now = nest_width[0]
    colmask = (jnp.arange(tile_cols, dtype=jnp.int32) < width_now).astype(jnp.float32)[
        None, None, :
    ]
    halfmask = (jnp.arange(half_cols, dtype=jnp.int32) * 2 < width_now).astype(jnp.float32)[
        None, None, :
    ]
    field_now = sigmas[0] * noise[0] * colmask
    for step_index in range(STEPS):
        sigma_now = sigmas[step_index]
        sigma_next = sigmas[step_index + 1]
        scale_in = 1.0 / jnp.sqrt(sigma_now * sigma_now + SIGMA_DATA * SIGMA_DATA)
        scaled = (field_now * scale_in).astype(jnp.bfloat16)
        embedded = w_sigma[:, None, None] * jnp.log(sigma_now)
        rim_field = with_halo(scaled, (("tile", 1),), 1)
        first_act = (
            jax.nn.silu(conv_taps(pad_cols(rim_field), w_in, tile_rows, tile_cols, 1) + embedded)
            * colmask
        ).astype(jnp.bfloat16)
        padded_first = pad_cols(with_halo(first_act, (("tile", 1),), 1))
        second = (
            jax.nn.silu(conv_taps(padded_first, w_enc, tile_rows, tile_cols, 1)) * colmask
        ).astype(jnp.bfloat16)
        above_row = from_behind(second[:, tile_rows - 1 :, :], "tile", 1)
        stacked = pad_cols(jnp.concatenate([above_row, second], axis=1))
        third_act = (
            jax.nn.silu(conv_taps(stacked, w_down, half_rows, half_cols, 2) + context_map)
            * halfmask
        ).astype(jnp.bfloat16)
        mid_field = pad_cols(with_halo(third_act, (("tile", 1),), 1))
        fourth = (
            jax.nn.silu(conv_taps(mid_field, w_mid, half_rows, half_cols, 1)) * halfmask
        ).astype(jnp.bfloat16)
        upward = jnp.repeat(jnp.repeat(fourth, 2, axis=1), 2, axis=2)
        joined = jnp.concatenate([second, upward], axis=0)
        dec_field = pad_cols(with_halo(joined, (("tile", 1),), 1))
        fifth_act = (
            jax.nn.silu(conv_taps(dec_field, w_dec, tile_rows, tile_cols, 1)) * colmask
        ).astype(jnp.bfloat16)
        out_field = pad_cols(with_halo(fifth_act, (("tile", 1),), 1))
        output_net = conv_taps(out_field, w_out, tile_rows, tile_cols, 1)
        total_var = sigma_now * sigma_now + SIGMA_DATA * SIGMA_DATA
        denoised = (
            SIGMA_DATA * SIGMA_DATA / total_var * field_now
            + sigma_now * SIGMA_DATA / jnp.sqrt(total_var) * output_net
        )
        field_now = (
            field_now + (sigma_next - sigma_now) / sigma_now * (field_now - denoised)
        ) * colmask
    return field_now[None]


def solution(mesh):
    return jax.shard_map(
        per_device,
        mesh=mesh,
        in_specs=(
            P("band", None),
            P(),
            P("band"),
            P(),
            P("band", None, "tile", None),
            P(),
            P(),
            P(),
            P(),
            P(),
            P(),
            P(),
            P(),
        ),
        out_specs=P("band", None, "tile", None),
        check_vma=False,
    )
```

profile of v0, /device:TPU:260, one launch (start us, length us, event | category | flops | bytes accessed | tf_op | source)
XLA Modules:
  0.0 201.2 jit_solution(11055624791948746910)
XLA Ops:
  5.0 4.5 %collective-permute-start.1 = (bf16[4,1,256]{2,0,1:T(4,128)(2,1)S(1)}, bf16[4,1,256]{2,0,1:T(4,128)(2,1)S(1)}, u32[]{:S(2)}, u32[]{:S(2)}) collective-permute-start(bf16[4,1,256]{2,0,1:T(4,128)(2,1)S(1)} %get-tuple-element.24), channel_id=1, source_target_pairs={{1,0},{2,1},{3,2},{4,3},{5,4},{6,5},{7,6},{8,7},{9,8},{10,9},{11,1... | collective-permute-start | bytes 6152 | tf_op jit(solution)/shard_map/ppermute | solution.py:23
  9.5 1.9 collective-permute-start
  15.9 2.4 %collective-permute-done = bf16[4,1,256]{2,0,1:T(4,128)(2,1)S(1)} collective-permute-done((bf16[4,1,256]{2,0,1:T(4,128)(2,1)S(1)}, bf16[4,1,256]{2,0,1:T(4,128)(2,1)S(1)}, u32[]{:S(2)}, u32[]{:S(2)}) %collective-permute-start) | collective-permute-done | bytes 2080 | tf_op jit(solution)/shard_map/ppermute | solution.py:22
  22.2 4.9 %collective-permute-start.3 = (bf16[128,1,256]{0,2,1:T(8,128)(2,1)S(1)}, bf16[128,1,256]{0,2,1:T(8,128)(2,1)S(1)}, u32[]{:S(2)}, u32[]{:S(2)}) collective-permute-start(bf16[128,1,256]{0,2,1:T(8,128)(2,1)S(1)} %get-tuple-element.16), channel_id=1, source_target_pairs={{1,0},{2,1},{3,2},{4,3},{5,4},{6,5},{7,6},{8,7},{9,8},{10,9},{11,1... | collective-permute-start | bytes 196616 | tf_op jit(solution)/shard_map/ppermute | solution.py:23
  27.1 1.9 collective-permute-start.2
  30.3 4.9 %all-to-all-start = ((bf16[12,8,4480]{2,0,1:T(8,128)(2,1)}), bf16[12,8,4480]{2,0,1:T(8,128)(2,1)S(1)}, u32[]{:S(2)}, u32[]{:S(2)}) async-start(bf16[12,8,4480]{2,0,1:T(8,128)(2,1)} %copy_multiply_fusion), calls=%async_computation | async-start | bytes 2293760 | tf_op jit(solution)/shard_map/all_to_all | solution.py:102
  40.9 2.1 %collective-permute-start.4 = (bf16[128,1,256]{0,2,1:T(8,128)(2,1)S(1)}, bf16[128,1,256]{0,2,1:T(8,128)(2,1)S(1)}, u32[]{:S(2)}, u32[]{:S(2)}) collective-permute-start(bf16[128,1,256]{0,2,1:T(8,128)(2,1)S(1)} %slice.842), channel_id=1, source_target_pairs={{0,1},{1,2},{2,3},{3,4},{4,5},{5,6},{6,7},{7,8},{8,9},{9,10},{10,1... | collective-permute-start | bytes 196616 | tf_op jit(solution)/shard_map/ppermute | solution.py:31
  43.0 7.7 %collective-permute-done.4 = bf16[128,1,256]{0,2,1:T(8,128)(2,1)S(1)} collective-permute-done((bf16[128,1,256]{0,2,1:T(8,128)(2,1)S(1)}, bf16[128,1,256]{0,2,1:T(8,128)(2,1)S(1)}, u32[]{:S(2)}, u32[]{:S(2)}) %collective-permute-start.4) | collective-permute-done | bytes 65568 | tf_op jit(solution)/shard_map/ppermute | solution.py:31
  59.1 2.2 %reshape_reshape.3 = bf16[96,70,64]{2,1,0:T(8,128)(2,1)} reshape(bf16[12,8,4480]{2,1,0:T(8,128)(2,1)S(1)} %copy.57) | data formatting | bytes 1720320 | tf_op jit(solution)/shard_map/reshape;reshape | solution.py:103
  61.4 3.4 %fusion.3 = bf16[96,256,64]{1,2,0:T(8,128)(2,1)S(1)} fusion(bf16[96,70,64]{2,1,0:T(8,128)(2,1)} %reshape_reshape.3, bf16[256,70]{0,1:T(8,128)(2,1)S(1)} %copy-done.15), kind=kOutput, calls=%fused_computation.7 | convolution fusion | flops 228065280 | bytes 4041728 | tf_op jit(solution)/shard_map/hc,kcb->khb/dot_general | solution.py:105
  65.9 3.9 %collective-permute-start.6 = (bf16[256,1,128]{0,2,1:T(8,128)(2,1)S(1)}, bf16[256,1,128]{0,2,1:T(8,128)(2,1)S(1)}, u32[]{:S(2)}, u32[]{:S(2)}) collective-permute-start(bf16[256,1,128]{0,2,1:T(8,128)(2,1)S(1)} %get-tuple-element.20), channel_id=1, source_target_pairs={{1,0},{2,1},{3,2},{4,3},{5,4},{6,5},{7,6},{8,7},{9,8},{10,9},{11,1... | collective-permute-start | bytes 196616 | tf_op jit(solution)/shard_map/ppermute | solution.py:23
  69.8 2.1 %collective-permute-start.5 = (bf16[256,1,128]{0,2,1:T(8,128)(2,1)S(1)}, bf16[256,1,128]{0,2,1:T(8,128)(2,1)S(1)}, u32[]{:S(2)}, u32[]{:S(2)}) collective-permute-start(bf16[256,1,128]{0,2,1:T(8,128)(2,1)S(1)} %get-tuple-element.19), channel_id=1, source_target_pairs={{0,1},{1,2},{2,3},{3,4},{4,5},{5,6},{6,7},{7,8},{8,9},{9,10},{10,1... | collective-permute-start | bytes 196616 | tf_op jit(solution)/shard_map/ppermute | solution.py:22
  72.2 7.1 %collective-permute-done.5 = bf16[256,1,128]{0,2,1:T(8,128)(2,1)S(1)} collective-permute-done((bf16[256,1,128]{0,2,1:T(8,128)(2,1)S(1)}, bf16[256,1,128]{0,2,1:T(8,128)(2,1)S(1)}, u32[]{:S(2)}, u32[]{:S(2)}) %collective-permute-start.5) | collective-permute-done | bytes 65568 | tf_op jit(solution)/shard_map/ppermute | solution.py:22
  82.1 2.1 %collective-permute-start.8 = (bf16[384,1,256]{0,2,1:T(8,128)(2,1)S(1)}, bf16[384,1,256]{0,2,1:T(8,128)(2,1)S(1)}, u32[]{:S(2)}, u32[]{:S(2)}) collective-permute-start(bf16[384,1,256]{0,2,1:T(8,128)(2,1)S(1)} %get-tuple-element.8), channel_id=1, source_target_pairs={{1,0},{2,1},{3,2},{4,3},{5,4},{6,5},{7,6},{8,7},{9,8},{10,9},{11,1... | collective-permute-start | bytes 589832 | tf_op jit(solution)/shard_map/ppermute | solution.py:23
  84.2 4.1 %collective-permute-start.7 = (bf16[384,1,256]{0,2,1:T(8,128)(2,1)S(1)}, bf16[384,1,256]{0,2,1:T(8,128)(2,1)S(1)}, u32[]{:S(2)}, u32[]{:S(2)}) collective-permute-start(bf16[384,1,256]{0,2,1:T(8,128)(2,1)S(1)} %get-tuple-element.7), channel_id=1, source_target_pairs={{0,1},{1,2},{2,3},{3,4},{4,5},{5,6},{6,7},{7,8},{8,9},{9,10},{10,1... | collective-permute-start | bytes 589832 | tf_op jit(solution)/shard_map/ppermute | solution.py:22
  89.8 5.2 %collective-permute-done.7 = bf16[384,1,256]{0,2,1:T(8,128)(2,1)S(1)} collective-permute-done((bf16[384,1,256]{0,2,1:T(8,128)(2,1)S(1)}, bf16[384,1,256]{0,2,1:T(8,128)(2,1)S(1)}, u32[]{:S(2)}, u32[]{:S(2)}) %collective-permute-start.7) | collective-permute-done | bytes 196640 | tf_op jit(solution)/shard_map/ppermute | solution.py:22
  98.9 1.9 collective-permute-start.10
  100.8 3.9 %collective-permute-start.9 = (bf16[128,1,256]{0,2,1:T(8,128)(2,1)S(1)}, bf16[128,1,256]{0,2,1:T(8,128)(2,1)S(1)}, u32[]{:S(2)}, u32[]{:S(2)}) collective-permute-start(bf16[128,1,256]{0,2,1:T(8,128)(2,1)S(1)} %get-tuple-element.13), channel_id=1, source_target_pairs={{0,1},{1,2},{2,3},{3,4},{4,5},{5,6},{6,7},{7,8},{8,9},{9,10},{10,1... | collective-permute-start | bytes 196616 | tf_op jit(solution)/shard_map/ppermute | solution.py:22
  113.4 4.0 %collective-permute-start.12 = (bf16[4,1,256]{2,0,1:T(4,128)(2,1)S(1)}, bf16[4,1,256]{2,0,1:T(4,128)(2,1)S(1)}, u32[]{:S(2)}, u32[]{:S(2)}) collective-permute-start(bf16[4,1,256]{2,0,1:T(4,128)(2,1)S(1)} %get-tuple-element.22), channel_id=1, source_target_pairs={{1,0},{2,1},{3,2},{4,3},{5,4},{6,5},{7,6},{8,7},{9,8},{10,9},{11,1... | collective-permute-start | bytes 6152 | tf_op jit(solution)/shard_map/ppermute | solution.py:23
  119.4 6.9 %collective-permute-done.11 = bf16[4,1,256]{2,0,1:T(4,128)(2,1)S(1)} collective-permute-done((bf16[4,1,256]{2,0,1:T(4,128)(2,1)S(1)}, bf16[4,1,256]{2,0,1:T(4,128)(2,1)S(1)}, u32[]{:S(2)}, u32[]{:S(2)}) %collective-permute-start.11) | collective-permute-done | bytes 2080 | tf_op jit(solution)/shard_map/ppermute | solution.py:22
  131.4 3.9 %collective-permute-start.13 = (bf16[128,1,256]{0,2,1:T(8,128)(2,1)S(1)}, bf16[128,1,256]{0,2,1:T(8,128)(2,1)S(1)}, u32[]{:S(2)}, u32[]{:S(2)}) collective-permute-start(bf16[128,1,256]{0,2,1:T(8,128)(2,1)S(1)} %get-tuple-element.11), channel_id=1, source_target_pairs={{0,1},{1,2},{2,3},{3,4},{4,5},{5,6},{6,7},{7,8},{8,9},{9,10},{10,1... | collective-permute-start | bytes 196616 | tf_op jit(solution)/shard_map/ppermute | solution.py:22
  135.7 5.2 %collective-permute-done.13 = bf16[128,1,256]{0,2,1:T(8,128)(2,1)S(1)} collective-permute-done((bf16[128,1,256]{0,2,1:T(8,128)(2,1)S(1)}, bf16[128,1,256]{0,2,1:T(8,128)(2,1)S(1)}, u32[]{:S(2)}, u32[]{:S(2)}) %collective-permute-start.13) | collective-permute-done | bytes 65568 | tf_op jit(solution)/shard_map/ppermute | solution.py:22
  143.3 2.1 %collective-permute-start.15 = (bf16[128,1,256]{0,2,1:T(8,128)(2,1)S(1)}, bf16[128,1,256]{0,2,1:T(8,128)(2,1)S(1)}, u32[]{:S(2)}, u32[]{:S(2)}) collective-permute-start(bf16[128,1,256]{0,2,1:T(8,128)(2,1)S(1)} %slice.881), channel_id=1, source_target_pairs={{0,1},{1,2},{2,3},{3,4},{4,5},{5,6},{6,7},{7,8},{8,9},{9,10},{10,1... | collective-permute-start | bytes 196616 | tf_op jit(solution)/shard_map/ppermute | solution.py:31
  145.3 7.6 %collective-permute-done.15 = bf16[128,1,256]{0,2,1:T(8,128)(2,1)S(1)} collective-permute-done((bf16[128,1,256]{0,2,1:T(8,128)(2,1)S(1)}, bf16[128,1,256]{0,2,1:T(8,128)(2,1)S(1)}, u32[]{:S(2)}, u32[]{:S(2)}) %collective-permute-start.15) | collective-permute-done | bytes 65568 | tf_op jit(solution)/shard_map/ppermute | solution.py:31
  156.5 1.9 collective-permute-start.17
  158.4 3.9 %collective-permute-start.16 = (bf16[256,1,128]{0,2,1:T(8,128)(2,1)S(1)}, bf16[256,1,128]{0,2,1:T(8,128)(2,1)S(1)}, u32[]{:S(2)}, u32[]{:S(2)}) collective-permute-start(bf16[256,1,128]{0,2,1:T(8,128)(2,1)S(1)} %get-tuple-element.17), channel_id=1, source_target_pairs={{0,1},{1,2},{2,3},{3,4},{4,5},{5,6},{6,7},{7,8},{8,9},{9,10},{10,1... | collective-permute-start | bytes 196616 | tf_op jit(solution)/shard_map/ppermute | solution.py:22
  162.6 5.2 %collective-permute-done.16 = bf16[256,1,128]{0,2,1:T(8,128)(2,1)S(1)} collective-permute-done((bf16[256,1,128]{0,2,1:T(8,128)(2,1)S(1)}, bf16[256,1,128]{0,2,1:T(8,128)(2,1)S(1)}, u32[]{:S(2)}, u32[]{:S(2)}) %collective-permute-start.16) | collective-permute-done | bytes 65568 | tf_op jit(solution)/shard_map/ppermute | solution.py:22
  170.6 2.1 %collective-permute-start.19 = (bf16[384,1,256]{0,2,1:T(8,128)(2,1)S(1)}, bf16[384,1,256]{0,2,1:T(8,128)(2,1)S(1)}, u32[]{:S(2)}, u32[]{:S(2)}) collective-permute-start(bf16[384,1,256]{0,2,1:T(8,128)(2,1)S(1)} %get-tuple-element.6), channel_id=1, source_target_pairs={{1,0},{2,1},{3,2},{4,3},{5,4},{6,5},{7,6},{8,7},{9,8},{10,9},{11,1... | collective-permute-start | bytes 589832 | tf_op jit(solution)/shard_map/ppermute | solution.py:23
  172.7 4.1 %collective-permute-start.18 = (bf16[384,1,256]{0,2,1:T(8,128)(2,1)S(1)}, bf16[384,1,256]{0,2,1:T(8,128)(2,1)S(1)}, u32[]{:S(2)}, u32[]{:S(2)}) collective-permute-start(bf16[384,1,256]{0,2,1:T(8,128)(2,1)S(1)} %get-tuple-element.5), channel_id=1, source_target_pairs={{0,1},{1,2},{2,3},{3,4},{4,5},{5,6},{6,7},{7,8},{8,9},{9,10},{10,1... | collective-permute-start | bytes 589832 | tf_op jit(solution)/shard_map/ppermute | solution.py:22
  178.3 5.2 %collective-permute-done.18 = bf16[384,1,256]{0,2,1:T(8,128)(2,1)S(1)} collective-permute-done((bf16[384,1,256]{0,2,1:T(8,128)(2,1)S(1)}, bf16[384,1,256]{0,2,1:T(8,128)(2,1)S(1)}, u32[]{:S(2)}, u32[]{:S(2)}) %collective-permute-start.18) | collective-permute-done | bytes 196640 | tf_op jit(solution)/shard_map/ppermute | solution.py:22
  189.3 3.9 %collective-permute-start.20 = (bf16[128,1,256]{0,2,1:T(8,128)(2,1)S(1)}, bf16[128,1,256]{0,2,1:T(8,128)(2,1)S(1)}, u32[]{:S(2)}, u32[]{:S(2)}) collective-permute-start(bf16[128,1,256]{0,2,1:T(8,128)(2,1)S(1)} %get-tuple-element.9), channel_id=1, source_target_pairs={{0,1},{1,2},{2,3},{3,4},{4,5},{5,6},{6,7},{7,8},{8,9},{9,10},{10,1... | collective-permute-start | bytes 196616 | tf_op jit(solution)/shard_map/ppermute | solution.py:22
  196.1 2.7 %collective-permute-done.20 = bf16[128,1,256]{0,2,1:T(8,128)(2,1)S(1)} collective-permute-done((bf16[128,1,256]{0,2,1:T(8,128)(2,1)S(1)}, bf16[128,1,256]{0,2,1:T(8,128)(2,1)S(1)}, u32[]{:S(2)}, u32[]{:S(2)}) %collective-permute-start.20) | collective-permute-done | bytes 65568 | tf_op jit(solution)/shard_map/ppermute | solution.py:22
  (232 shorter events, 62.0 us)
Async XLA Ops:
  0.0 14.7 %copy-start = (bf16[64,4480]{1,0:T(8,128)(2,1)S(1)}, bf16[64,4480]{1,0:T(8,128)(2,1)}, u32[]{:S(2)}) copy-start(bf16[64,4480]{1,0:T(8,128)(2,1)} %param.13) | copy-start | bytes 1720324
  5.0 10.9 %collective-permute-start.1 = (bf16[4,1,256]{2,0,1:T(4,128)(2,1)S(1)}, bf16[4,1,256]{2,0,1:T(4,128)(2,1)S(1)}, u32[]{:S(2)}, u32[]{:S(2)}) collective-permute-start(bf16[4,1,256]{2,0,1:T(4,128)(2,1)S(1)} %get-tuple-element.24), channel_id=1, source_target_pairs={{1,0},{2,1},{3,2},{4,3},{5,4},{6,5},{7,6},{8,7},{9,8},{10,9},{11,1... | collective-permute-start | bytes 6152 | tf_op jit(solution)/shard_map/ppermute | solution.py:23
  9.5 8.8 %collective-permute-start = (bf16[4,1,256]{2,0,1:T(4,128)(2,1)S(1)}, bf16[4,1,256]{2,0,1:T(4,128)(2,1)S(1)}, u32[]{:S(2)}, u32[]{:S(2)}) collective-permute-start(bf16[4,1,256]{2,0,1:T(4,128)(2,1)S(1)} %get-tuple-element.23), channel_id=1, source_target_pairs={{0,1},{1,2},{2,3},{3,4},{4,5},{5,6},{6,7},{7,8},{8,9},{9,10},{10,1... | collective-permute-start | bytes 6152 | tf_op jit(solution)/shard_map/ppermute | solution.py:22
  22.2 16.3 %collective-permute-start.3 = (bf16[128,1,256]{0,2,1:T(8,128)(2,1)S(1)}, bf16[128,1,256]{0,2,1:T(8,128)(2,1)S(1)}, u32[]{:S(2)}, u32[]{:S(2)}) collective-permute-start(bf16[128,1,256]{0,2,1:T(8,128)(2,1)S(1)} %get-tuple-element.16), channel_id=1, source_target_pairs={{1,0},{2,1},{3,2},{4,3},{5,4},{6,5},{7,6},{8,7},{9,8},{10,9},{11,1... | collective-permute-start | bytes 196616 | tf_op jit(solution)/shard_map/ppermute | solution.py:23
  27.1 11.4 %collective-permute-start.2 = (bf16[128,1,256]{0,2,1:T(8,128)(2,1)S(1)}, bf16[128,1,256]{0,2,1:T(8,128)(2,1)S(1)}, u32[]{:S(2)}, u32[]{:S(2)}) collective-permute-start(bf16[128,1,256]{0,2,1:T(8,128)(2,1)S(1)} %get-tuple-element.15), channel_id=1, source_target_pairs={{0,1},{1,2},{2,3},{3,4},{4,5},{5,6},{6,7},{7,8},{8,9},{9,10},{10,1... | collective-permute-start | bytes 196616 | tf_op jit(solution)/shard_map/ppermute | solution.py:22
  30.3 28.1 %all-to-all-start = ((bf16[12,8,4480]{2,0,1:T(8,128)(2,1)}), bf16[12,8,4480]{2,0,1:T(8,128)(2,1)S(1)}, u32[]{:S(2)}, u32[]{:S(2)}) async-start(bf16[12,8,4480]{2,0,1:T(8,128)(2,1)} %copy_multiply_fusion), calls=%async_computation | async-start | bytes 2293760 | tf_op jit(solution)/shard_map/all_to_all | solution.py:102
  40.8 11.1 %copy-start.2 = (bf16[9,256,128]{2,1,0:T(8,128)(2,1)S(1)}, bf16[9,256,128]{2,1,0:T(8,128)(2,1)}, u32[]{:S(2)}) copy-start(bf16[9,256,128]{2,1,0:T(8,128)(2,1)} %param.22) | copy-start | bytes 1769476
  40.9 9.8 %collective-permute-start.4 = (bf16[128,1,256]{0,2,1:T(8,128)(2,1)S(1)}, bf16[128,1,256]{0,2,1:T(8,128)(2,1)S(1)}, u32[]{:S(2)}, u32[]{:S(2)}) collective-permute-start(bf16[128,1,256]{0,2,1:T(8,128)(2,1)S(1)} %slice.842), channel_id=1, source_target_pairs={{0,1},{1,2},{2,3},{3,4},{4,5},{5,6},{6,7},{7,8},{8,9},{9,10},{10,1... | collective-permute-start | bytes 196616 | tf_op jit(solution)/shard_map/ppermute | solution.py:31
  42.9 38.3 %copy-start.16 = (f32[128]{0:T(128)}, f32[128]{0:T(128)S(1)}, u32[]{:S(2)}) copy-start(f32[128]{0:T(128)S(1)} %compare_convert_fusion) | copy-start | bytes 1540
  65.6 14.0 %copy-start.9 = (f32[256,2,128]{0,2,1:T(8,128)}, f32[256,2,128]{0,2,1:T(8,128)S(1)}, u32[]{:S(2)}) copy-start(f32[256,2,128]{0,2,1:T(8,128)S(1)} %reshape.251) | copy-start | bytes 786436
  65.6 13.7 %copy-start.1 = (bf16[9,256,256]{2,1,0:T(8,128)(2,1)S(1)}, bf16[9,256,256]{2,1,0:T(8,128)(2,1)}, u32[]{:S(2)}) copy-start(bf16[9,256,256]{2,1,0:T(8,128)(2,1)} %param.23) | copy-start | bytes 3538948
  65.9 6.3 %collective-permute-start.6 = (bf16[256,1,128]{0,2,1:T(8,128)(2,1)S(1)}, bf16[256,1,128]{0,2,1:T(8,128)(2,1)S(1)}, u32[]{:S(2)}, u32[]{:S(2)}) collective-permute-start(bf16[256,1,128]{0,2,1:T(8,128)(2,1)S(1)} %get-tuple-element.20), channel_id=1, source_target_pairs={{1,0},{2,1},{3,2},{4,3},{5,4},{6,5},{7,6},{8,7},{9,8},{10,9},{11,1... | collective-permute-start | bytes 196616 | tf_op jit(solution)/shard_map/ppermute | solution.py:23
  69.8 9.5 %collective-permute-start.5 = (bf16[256,1,128]{0,2,1:T(8,128)(2,1)S(1)}, bf16[256,1,128]{0,2,1:T(8,128)(2,1)S(1)}, u32[]{:S(2)}, u32[]{:S(2)}) collective-permute-start(bf16[256,1,128]{0,2,1:T(8,128)(2,1)S(1)} %get-tuple-element.19), channel_id=1, source_target_pairs={{0,1},{1,2},{2,3},{3,4},{4,5},{5,6},{6,7},{7,8},{8,9},{9,10},{10,1... | collective-permute-start | bytes 196616 | tf_op jit(solution)/shard_map/ppermute | solution.py:22
  82.1 13.3 %copy-start.5 = (bf16[9,128,384]{2,1,0:T(8,128)(2,1)S(1)}, bf16[9,128,384]{2,1,0:T(8,128)(2,1)}, u32[]{:S(2)}) copy-start(bf16[9,128,384]{2,1,0:T(8,128)(2,1)} %param.24) | copy-start | bytes 2654212
  82.1 7.7 %collective-permute-start.8 = (bf16[384,1,256]{0,2,1:T(8,128)(2,1)S(1)}, bf16[384,1,256]{0,2,1:T(8,128)(2,1)S(1)}, u32[]{:S(2)}, u32[]{:S(2)}) collective-permute-start(bf16[384,1,256]{0,2,1:T(8,128)(2,1)S(1)} %get-tuple-element.8), channel_id=1, source_target_pairs={{1,0},{2,1},{3,2},{4,3},{5,4},{6,5},{7,6},{8,7},{9,8},{10,9},{11,1... | collective-permute-start | bytes 589832 | tf_op jit(solution)/shard_map/ppermute | solution.py:23
  84.2 10.9 %collective-permute-start.7 = (bf16[384,1,256]{0,2,1:T(8,128)(2,1)S(1)}, bf16[384,1,256]{0,2,1:T(8,128)(2,1)S(1)}, u32[]{:S(2)}, u32[]{:S(2)}) collective-permute-start(bf16[384,1,256]{0,2,1:T(8,128)(2,1)S(1)} %get-tuple-element.7), channel_id=1, source_target_pairs={{0,1},{1,2},{2,3},{3,4},{4,5},{5,6},{6,7},{7,8},{8,9},{9,10},{10,1... | collective-permute-start | bytes 589832 | tf_op jit(solution)/shard_map/ppermute | solution.py:22
  98.5 12.0 %copy-start.14 = (bf16[9,4,128]{2,1,0:T(4,128)(2,1)S(1)}, bf16[9,4,128]{2,1,0:T(4,128)(2,1)}, u32[]{:S(2)}) copy-start(bf16[9,4,128]{2,1,0:T(4,128)(2,1)} %param.25) | copy-start | bytes 27652
  98.9 10.2 %collective-permute-start.10 = (bf16[128,1,256]{0,2,1:T(8,128)(2,1)S(1)}, bf16[128,1,256]{0,2,1:T(8,128)(2,1)S(1)}, u32[]{:S(2)}, u32[]{:S(2)}) collective-permute-start(bf16[128,1,256]{0,2,1:T(8,128)(2,1)S(1)} %get-tuple-element.14), channel_id=1, source_target_pairs={{1,0},{2,1},{3,2},{4,3},{5,4},{6,5},{7,6},{8,7},{9,8},{10,9},{11,1... | collective-permute-start | bytes 196616 | tf_op jit(solution)/shard_map/ppermute | solution.py:23
  100.8 9.5 %collective-permute-start.9 = (bf16[128,1,256]{0,2,1:T(8,128)(2,1)S(1)}, bf16[128,1,256]{0,2,1:T(8,128)(2,1)S(1)}, u32[]{:S(2)}, u32[]{:S(2)}) collective-permute-start(bf16[128,1,256]{0,2,1:T(8,128)(2,1)S(1)} %get-tuple-element.13), channel_id=1, source_target_pairs={{0,1},{1,2},{2,3},{3,4},{4,5},{5,6},{6,7},{7,8},{8,9},{9,10},{10,1... | collective-permute-start | bytes 196616 | tf_op jit(solution)/shard_map/ppermute | solution.py:22
  113.4 6.0 %collective-permute-start.12 = (bf16[4,1,256]{2,0,1:T(4,128)(2,1)S(1)}, bf16[4,1,256]{2,0,1:T(4,128)(2,1)S(1)}, u32[]{:S(2)}, u32[]{:S(2)}) collective-permute-start(bf16[4,1,256]{2,0,1:T(4,128)(2,1)S(1)} %get-tuple-element.22), channel_id=1, source_target_pairs={{1,0},{2,1},{3,2},{4,3},{5,4},{6,5},{7,6},{8,7},{9,8},{10,9},{11,1... | collective-permute-start | bytes 6152 | tf_op jit(solution)/shard_map/ppermute | solution.py:23
  117.5 8.8 %collective-permute-start.11 = (bf16[4,1,256]{2,0,1:T(4,128)(2,1)S(1)}, bf16[4,1,256]{2,0,1:T(4,128)(2,1)S(1)}, u32[]{:S(2)}, u32[]{:S(2)}) collective-permute-start(bf16[4,1,256]{2,0,1:T(4,128)(2,1)S(1)} %get-tuple-element.21), channel_id=1, source_target_pairs={{0,1},{1,2},{2,3},{3,4},{4,5},{5,6},{6,7},{7,8},{8,9},{9,10},{10,1... | collective-permute-start | bytes 6152 | tf_op jit(solution)/shard_map/ppermute | solution.py:22
  129.5 6.2 %collective-permute-start.14 = (bf16[128,1,256]{0,2,1:T(8,128)(2,1)S(1)}, bf16[128,1,256]{0,2,1:T(8,128)(2,1)S(1)}, u32[]{:S(2)}, u32[]{:S(2)}) collective-permute-start(bf16[128,1,256]{0,2,1:T(8,128)(2,1)S(1)} %get-tuple-element.12), channel_id=1, source_target_pairs={{1,0},{2,1},{3,2},{4,3},{5,4},{6,5},{7,6},{8,7},{9,8},{10,9},{11,1... | collective-permute-start | bytes 196616 | tf_op jit(solution)/shard_map/ppermute | solution.py:23
  131.4 9.5 %collective-permute-start.13 = (bf16[128,1,256]{0,2,1:T(8,128)(2,1)S(1)}, bf16[128,1,256]{0,2,1:T(8,128)(2,1)S(1)}, u32[]{:S(2)}, u32[]{:S(2)}) collective-permute-start(bf16[128,1,256]{0,2,1:T(8,128)(2,1)S(1)} %get-tuple-element.11), channel_id=1, source_target_pairs={{0,1},{1,2},{2,3},{3,4},{4,5},{5,6},{6,7},{7,8},{8,9},{9,10},{10,1... | collective-permute-start | bytes 196616 | tf_op jit(solution)/shard_map/ppermute | solution.py:22
  143.3 11.2 %copy-start.3 = (bf16[9,256,128]{2,1,0:T(8,128)(2,1)S(1)}, bf16[9,256,128]{2,1,0:T(8,128)(2,1)}, u32[]{:S(2)}) copy-start(bf16[9,256,128]{2,1,0:T(8,128)(2,1)} %param.22) | copy-start | bytes 1769476
  143.3 9.6 %collective-permute-start.15 = (bf16[128,1,256]{0,2,1:T(8,128)(2,1)S(1)}, bf16[128,1,256]{0,2,1:T(8,128)(2,1)S(1)}, u32[]{:S(2)}, u32[]{:S(2)}) collective-permute-start(bf16[128,1,256]{0,2,1:T(8,128)(2,1)S(1)} %slice.881), channel_id=1, source_target_pairs={{0,1},{1,2},{2,3},{3,4},{4,5},{5,6},{6,7},{7,8},{8,9},{9,10},{10,1... | collective-permute-start | bytes 196616 | tf_op jit(solution)/shard_map/ppermute | solution.py:31
  156.5 6.2 %collective-permute-start.17 = (bf16[256,1,128]{0,2,1:T(8,128)(2,1)S(1)}, bf16[256,1,128]{0,2,1:T(8,128)(2,1)S(1)}, u32[]{:S(2)}, u32[]{:S(2)}) collective-permute-start(bf16[256,1,128]{0,2,1:T(8,128)(2,1)S(1)} %get-tuple-element.18), channel_id=1, source_target_pairs={{1,0},{2,1},{3,2},{4,3},{5,4},{6,5},{7,6},{8,7},{9,8},{10,9},{11,1... | collective-permute-start | bytes 196616 | tf_op jit(solution)/shard_map/ppermute | solution.py:23
  158.4 9.5 %collective-permute-start.16 = (bf16[256,1,128]{0,2,1:T(8,128)(2,1)S(1)}, bf16[256,1,128]{0,2,1:T(8,128)(2,1)S(1)}, u32[]{:S(2)}, u32[]{:S(2)}) collective-permute-start(bf16[256,1,128]{0,2,1:T(8,128)(2,1)S(1)} %get-tuple-element.17), channel_id=1, source_target_pairs={{0,1},{1,2},{2,3},{3,4},{4,5},{5,6},{6,7},{7,8},{8,9},{9,10},{10,1... | collective-permute-start | bytes 196616 | tf_op jit(solution)/shard_map/ppermute | solution.py:22
  170.6 13.3 %copy-start.6 = (bf16[9,128,384]{2,1,0:T(8,128)(2,1)S(1)}, bf16[9,128,384]{2,1,0:T(8,128)(2,1)}, u32[]{:S(2)}) copy-start(bf16[9,128,384]{2,1,0:T(8,128)(2,1)} %param.24) | copy-start | bytes 2654212
  170.6 7.7 %collective-permute-start.19 = (bf16[384,1,256]{0,2,1:T(8,128)(2,1)S(1)}, bf16[384,1,256]{0,2,1:T(8,128)(2,1)S(1)}, u32[]{:S(2)}, u32[]{:S(2)}) collective-permute-start(bf16[384,1,256]{0,2,1:T(8,128)(2,1)S(1)} %get-tuple-element.6), channel_id=1, source_target_pairs={{1,0},{2,1},{3,2},{4,3},{5,4},{6,5},{7,6},{8,7},{9,8},{10,9},{11,1... | collective-permute-start | bytes 589832 | tf_op jit(solution)/shard_map/ppermute | solution.py:23
  172.7 10.9 %collective-permute-start.18 = (bf16[384,1,256]{0,2,1:T(8,128)(2,1)S(1)}, bf16[384,1,256]{0,2,1:T(8,128)(2,1)S(1)}, u32[]{:S(2)}, u32[]{:S(2)}) collective-permute-start(bf16[384,1,256]{0,2,1:T(8,128)(2,1)S(1)} %get-tuple-element.5), channel_id=1, source_target_pairs={{0,1},{1,2},{2,3},{3,4},{4,5},{5,6},{6,7},{7,8},{8,9},{9,10},{10,1... | collective-permute-start | bytes 589832 | tf_op jit(solution)/shard_map/ppermute | solution.py:22
  187.4 8.7 %collective-permute-start.21 = (bf16[128,1,256]{0,2,1:T(8,128)(2,1)S(1)}, bf16[128,1,256]{0,2,1:T(8,128)(2,1)S(1)}, u32[]{:S(2)}, u32[]{:S(2)}) collective-permute-start(bf16[128,1,256]{0,2,1:T(8,128)(2,1)S(1)} %get-tuple-element.10), channel_id=1, source_target_pairs={{1,0},{2,1},{3,2},{4,3},{5,4},{6,5},{7,6},{8,7},{9,8},{10,9},{11,1... | collective-permute-start | bytes 196616 | tf_op jit(solution)/shard_map/ppermute | solution.py:23
  189.3 9.5 %collective-permute-start.20 = (bf16[128,1,256]{0,2,1:T(8,128)(2,1)S(1)}, bf16[128,1,256]{0,2,1:T(8,128)(2,1)S(1)}, u32[]{:S(2)}, u32[]{:S(2)}) collective-permute-start(bf16[128,1,256]{0,2,1:T(8,128)(2,1)S(1)} %get-tuple-element.9), channel_id=1, source_target_pairs={{0,1},{1,2},{2,3},{3,4},{4,5},{5,6},{6,7},{7,8},{8,9},{9,10},{10,1... | collective-permute-start | bytes 196616 | tf_op jit(solution)/shard_map/ppermute | solution.py:22
  (10 other events, 21.8 us)
where the time goes:
time: 203 us; the launch traced here: 201 us
  starting transfers between devices  69.9 us (34%)
  waiting for transfers between devices  60.4 us (30%)
  matrix products  35.4 us (17%)
  local copies, waits for them, and re-layouts  15.1 us (7%)
  between operations  14.2 us (7%)
  other arithmetic  6.27 us (3%)
    ppermute x10, waiting for transfers between devices, with_halo(): before = lax.ppermute(last, axis, up)  41.2 us
    dot_general x108, matrix products, conv_taps(): jnp.einsum('oi,irc->orc', weight[tap_index], window, preferred_element_ty...  31.9 us
    ppermute x10, starting transfers between devices, with_halo(): before = lax.ppermute(last, axis, up)  31.8 us
    ppermute x10, starting transfers between devices, with_halo(): after = lax.ppermute(first, axis, down)  29 us
    ppermute x2, waiting for transfers between devices, from_behind(): return lax.ppermute(x, axis, pairs)  15.2 us
    slice x18, local copies, waits for them, and re-layouts, conv_taps(): lax.slice(padded, (0, row_off, col_off), (channels, row_off + stride * (o...  5.66 us
    all_to_all x1, starting transfers between devices, per_device(): lax.all_to_all(outgoing, 'band', split_axis=1, concat_axis=1, tiled=True)  4.93 us
    ppermute x2, starting transfers between devices, from_behind(): return lax.ppermute(x, axis, pairs)  4.1 us
  transfers between devices with their start and end apart: 23, of which 16 were waited for; matrix products, arithmetic and copies ran while one was open for 8% of the time, Pallas kernels for 0%

commit v1 on v0

v1 whole, which is shorter than its diff:
```python
import functools
import math

import jax
import jax.numpy as jnp
from jax import lax
from jax.experimental import pallas as pl
from jax.experimental.pallas import tpu as pltpu
from jax.sharding import PartitionSpec as P

K = 96
SIGMA_DATA = 0.5
BF = jnp.bfloat16
F32 = jnp.float32
HALF = 128
ROWS = 256
NT = (((1,), (1,)), ((), ()))
TN = (((0,), (1,)), ((), ()))

STEP_ROWS = (
    dict(scaled=(-15, 31), first=(-14, 29), second=(-13, 27), third=(-6, 13), fourth=(-5, 11), fifth=(-8, 19), out=(-7, 17)),
    dict(scaled=(-7, 17), first=(-6, 15), second=(-5, 13), third=(-2, 6), fourth=(-1, 4), fifth=(-1, 6), out=(0, 4)),
)


def silu(v):
    h = 0.5 * v
    return h + h * jnp.tanh(h)


def dot_nt(a, b):
    return lax.dot_general(a, b, NT, preferred_element_type=F32)


def encode_kernel(anchor_ref, blocks_ref, w_ref, out_ref, enc_ref):
    band = lax.axis_index("band")
    tile = lax.axis_index("tile")
    count = enc_ref.shape[0]
    cells = enc_ref.shape[1]

    def encode(i, carry):
        part = blocks_ref[pl.ds(pl.multiple_of(i * 512, 512), 512), :]
        v = silu(dot_nt(part, w_ref[...])).astype(BF).astype(F32)
        enc_ref[pl.ds(i * 8, 8)] = v.reshape(8, cells, 256)
        return carry

    lax.fori_loop(0, count // 8, encode, 0)

    def window(k, carry):
        nest = k // 2
        part = k % 2
        anchor = anchor_ref[nest, tile]
        begin = anchor + (band - anchor + 512) % 8 + part * 48
        row = (begin % 512) // 8
        total = enc_ref[row]
        for m in range(1, 6):
            total = total + enc_ref[(row + m) % count]
        out_ref[nest, pl.ds(pl.multiple_of(part * cells, cells), cells), :] = total.astype(BF)
        return carry

    lax.fori_loop(0, 16, window, 0)


def pair_weight(w, a):
    zero = jnp.zeros_like(w(a, 0))
    own = jnp.concatenate(
        [jnp.concatenate([w(a, 1), w(a, 2)], 1), jnp.concatenate([w(a, 0), w(a, 1)], 1)], 0
    )
    rim = jnp.concatenate(
        [jnp.concatenate([w(a, 0), zero], 1), jnp.concatenate([zero, w(a, 2)], 1)], 0
    )
    return own, rim


def prep_kernel(w_enc, w_down, w_mid, w_dec, enc_o, down_o, mid_o, dec2_o, even_o, odd_o):
    for a in range(3):
        own, rim = pair_weight(lambda i, b: w_enc[3 * i + b], a)
        enc_o[:, 512 * a : 512 * a + 256] = own
        enc_o[:, 512 * a + 256 : 512 * a + 512] = rim
        own, rim = pair_weight(lambda i, b: w_dec[3 * i + b, :, 0:128], a)
        dec2_o[:, 512 * a : 512 * a + 256] = own
        dec2_o[:, 512 * a + 256 : 512 * a + 512] = rim
        down_o[:, 256 * a : 256 * a + 128] = w_down[3 * a + 1]
        down_o[:, 256 * a + 128 : 256 * a + 256] = w_down[3 * a + 2]
        down_o[:, 768 + 128 * a : 896 + 128 * a] = w_down[3 * a]
        for b in range(3):
            mid_o[:, 768 * a + 256 * b : 768 * a + 256 * b + 256] = w_mid[3 * a + b]

    def up(a, b):
        return w_dec[3 * a + b, :, 128:384].astype(F32)

    for o_ref, sets in ((even_o, ((0,), (1, 2))), (odd_o, ((0, 1), (2,)))):
        for k, taps in enumerate(sets):
            col = [sum(up(a, b) for a in taps) for b in range(3)]
            zero = jnp.zeros_like(col[0])
            o_ref[:, 768 * k : 768 * k + 256] = jnp.concatenate([col[0], zero], 0).astype(BF)
            o_ref[:, 768 * k + 256 : 768 * k + 512] = jnp.concatenate(
                [col[1] + col[2], col[0] + col[1]], 0
            ).astype(BF)
            o_ref[:, 768 * k + 512 : 768 * k + 768] = jnp.concatenate([zero, col[2]], 0).astype(BF)


def main_kernel(
    width_ref, coef_ref,
    far_up, near_up, own, near_down, far_down,
    cond_far_up, cond_up, cond_own, cond_down, cond_far_down,
    bias_ref, w_in, w_enc, w_down, w_mid, w_dec2, w_even, w_odd, w_out,
    out_ref,
    state, spread, firstc, firste, secondc, seconde, third, thirdl, thirdr, fourth, fourthl, fourthr,
    fifthc, fifthe, prod, picked,
):
    tile = lax.axis_index("tile")
    base = tile * 4
    width = width_ref[0]
    lane = lax.broadcasted_iota(jnp.int32, (HALF, 256), 1)
    pair = lax.broadcasted_iota(jnp.int32, (HALF, 256), 0)
    colmask = (2 * pair + lane // 128 < width).astype(F32)
    halfmask = (2 * pair < width).astype(F32)
    natural = (lax.broadcasted_iota(jnp.int32, (8, 256), 1) < width).astype(F32)

    def fine_ok(rho):
        row = base + rho
        return jnp.logical_and(row >= 0, row < ROWS).astype(F32)

    def half_ok(h):
        row = tile * 2 + h
        return jnp.logical_and(row >= 0, row < ROWS // 2).astype(F32)

    def slide(x, by):
        rows = x.shape[0]
        edge = 0 if by == 1 else HALF - 1
        where = lax.broadcasted_iota(jnp.int32, x.shape, 0) % HALF
        return jnp.where(where == edge, 0.0, pltpu.roll(x, by % rows, 0))

    def keep_pairs(y, center, rim, at, n, mask, lo):
        y = jnp.concatenate(
            [y[k * HALF : (k + 1) * HALF] * (mask * fine_ok(lo + at + k)) for k in range(n)], 0
        )
        side = jnp.concatenate([slide(y[:, 128:], 1), slide(y[:, :128], -1)], 1).astype(BF)
        y = y.astype(BF)
        for k in range(n):
            center[at + k] = y[k * HALF : (k + 1) * HALF]
            rim[at + k] = side[k * HALF : (k + 1) * HALF]

    def keep_half(y, center, left, right, at, n, lo):
        y = jnp.concatenate(
            [y[k * HALF : (k + 1) * HALF] * (halfmask * half_ok(lo + at + k)) for k in range(n)], 0
        )
        sides = (slide(y, 1).astype(BF), slide(y, -1).astype(BF))
        y = y.astype(BF)
        for k in range(n):
            cut = slice(k * HALF, (k + 1) * HALF)
            center[at + k] = y[cut]
            left[at + k] = sides[0][cut]
            right[at + k] = sides[1][cut]

    def stacked(ref, at, n, step=1):
        return jnp.concatenate([ref[at + step * k] for k in range(n)], 0)

    def chunks(total, size, body):
        full = total // size
        if full == 1:
            body(0, size)
        elif full:
            lax.fori_loop(0, full, lambda i, c: (body(i * size, size), c)[1], 0)
        if total % size:
            body(full * size, total % size)

    pieces = ((far_up, -16, 12), (near_up, -4, 4), (own, 0, 4), (near_down, 4, 4), (far_down, 8, 12))
    start = coef_ref[0, 0]
    empty = jnp.zeros((4, 256), F32)
    for ref, lo, n in pieces:
        for k in range(n):
            rho = lo + k
            if -15 <= rho <= 15:
                value = jnp.concatenate([ref[4 * k : 4 * k + 4, :], empty], 0)
                state[8 * (rho + 15) : 8 * (rho + 16), :] = start * value * (natural * fine_ok(rho))

    col = lax.broadcasted_iota(jnp.int32, (256, 512), 0)
    place = lax.broadcasted_iota(jnp.int32, (256, 512), 1)
    pick = (col == 2 * (place % 128) + place // 128 - 1).astype(F32).astype(BF)
    weave_j = lax.broadcasted_iota(jnp.int32, (HALF, 256), 0)
    weave_c = lax.broadcasted_iota(jnp.int32, (HALF, 256), 1)
    weave = [(weave_c == 2 * weave_j + p).astype(F32) for p in range(2)]
    repeat = (
        lax.broadcasted_iota(jnp.int32, (HALF, 64), 0) // 2 == lax.broadcasted_iota(jnp.int32, (HALF, 64), 1)
    ).astype(F32).astype(BF)

    conds = (
        (cond_far_up, 0), (cond_far_up, 1), (cond_far_up, 2), (cond_far_up, 3),
        (cond_up, 0), (cond_up, 1), (cond_own, 0), (cond_own, 1), (cond_down, 0), (cond_down, 1),
        (cond_far_down, 0), (cond_far_down, 1), (cond_far_down, 2), (cond_far_down, 3),
    )

    for step in range(2):
        rows = STEP_ROWS[step]
        state_lo = rows["scaled"][0]
        scale, keep, mix, move = (coef_ref[step, 1 + i] for i in range(4))
        bias = bias_ref[step : step + 1, :]

        n_scaled = rows["scaled"][1]
        scaled = (state[0 : 8 * n_scaled, :] * scale).astype(BF)
        spread[0 : 8 * n_scaled, :] = jnp.dot(scaled, pick, preferred_element_type=F32)
        lo, total = rows["first"]

        def first_rows(at, n):
            cols = []
            for k in range(n):
                cols.append(
                    jnp.concatenate(
                        [
                            spread[pl.ds(pl.multiple_of((at + k + a) * 8, 8), 8), 128 * q : 128 * q + 128]
                            for a in range(3)
                            for q in range(4)
                        ],
                        0,
                    )
                )
            x = jnp.concatenate(cols, 1).astype(BF)
            y = lax.dot_general(x, w_in[...], TN, preferred_element_type=F32)
            keep_pairs(silu(y + bias), firstc, firste, at, n, colmask, lo)

        chunks(total, 5, first_rows)

        lo, total = rows["second"]

        def second_rows(at, n):
            x = jnp.concatenate(
                [stacked(ref, at + a, n) for a in range(3) for ref in (firstc, firste)], 1
            )
            keep_pairs(silu(dot_nt(x, w_enc[...])), secondc, seconde, at, n, colmask, rows["second"][0])

        chunks(total, 9 if step == 0 else 13, second_rows)

        second_lo = rows["second"][0]
        third_lo, total = rows["third"]

        def third_rows(at, n):
            begin = 2 * third_lo - 1 - second_lo + 2 * at
            x = jnp.concatenate(
                [stacked(secondc, begin + a, n, 2) for a in range(3)]
                + [
                    jnp.concatenate([seconde[begin + a + 2 * k][:, :128] for k in range(n)], 0)
                    for a in range(3)
                ],
                1,
            )
            y = dot_nt(x, w_down[...])
            add = []
            for k in range(n):
                ref, r = conds[third_lo + at + k + 6]
                add.append(jnp.dot(repeat, ref[64 * r : 64 * r + 64, :], preferred_element_type=F32))
            y = y + jnp.concatenate(add, 0)
            keep_half(silu(y), third, thirdl, thirdr, at, n, third_lo)

        for at in range(0, total, 7):
            third_rows(at, min(7, total - at))

        fourth_lo, total = rows["fourth"]

        def fourth_rows(at, n):
            begin = fourth_lo - 1 - third_lo + at
            x = jnp.concatenate(
                [stacked(ref, begin + a, n) for a in range(3) for ref in (thirdl, third, thirdr)], 1
            )
            keep_half(silu(dot_nt(x, w_mid[...])), fourth, fourthl, fourthr, at, n, fourth_lo)

        for at in range(0, total, 6):
            fourth_rows(at, min(6, total - at))

        fifth_lo, total = rows["fifth"]

        def fifth_rows(at, n):
            rho = fifth_lo + at
            odd = rho % 2
            begin = rho - 1 - second_lo
            h = (rho - odd) // 2 - fourth_lo - (0 if odd else 1)
            x = jnp.concatenate(
                [stacked(ref, begin + a, n, 2) for a in range(3) for ref in (secondc, seconde)], 1
            )
            z = jnp.concatenate(
                [stacked(ref, h + a, n) for a in range(2) for ref in (fourthl, fourth, fourthr)], 1
            )
            y = dot_nt(x, w_dec2[...]) + dot_nt(z, (w_odd if odd else w_even)[...])
            y = silu(y)
            for k in range(n):
                part = y[k * HALF : (k + 1) * HALF]
                keep_pairs(part, fifthc, fifthe, at + 2 * k, 1, colmask, fifth_lo)

        for parity in range(2):
            n_rows = (total - parity + 1) // 2
            for at in range(0, n_rows, 5):
                fifth_rows(parity + 2 * at, min(5, n_rows - at))

        def out_rows(at, n):
            x = jnp.concatenate([stacked(fifthc, at, n), stacked(fifthe, at, n)], 1)
            prod[:, at * HALF : (at + n) * HALF] = dot_nt(w_out[...], x)

        for at in range(0, total, 10):
            out_rows(at, min(10, total - at))
        out_lo, total = rows["out"]
        for k in range(total):
            for p in range(2):
                picked[p, 8 * k : 8 * k + 8, :] = sum(
                    prod[16 * a + 8 * p : 16 * a + 8 * p + 8, (k + a) * HALF : (k + a + 1) * HALF]
                    for a in range(3)
                )
        net = sum(
            jnp.dot(
                picked[p, 0 : 8 * total, :], weave[p], preferred_element_type=F32, precision=lax.Precision.HIGHEST
            )
            for p in range(2)
        )
        skip = 8 * (out_lo - state_lo)
        now = state[skip : skip + 8 * total, :]
        denoised = keep * now + mix * net
        now = now + move * (now - denoised)
        for k in range(total):
            value = now[8 * k : 8 * k + 8] * (natural * fine_ok(out_lo + k))
            if step == 0:
                state[8 * k : 8 * k + 8, :] = value
            else:
                out_ref[:, k, :] = value[0:4]


def shift(x, by):
    n = lax.axis_size("tile")
    return lax.ppermute(x, "tile", [(i, i + by) for i in range(n) if 0 <= i + by < n])


def turn(x, by):
    n = lax.axis_size("tile")
    return lax.ppermute(x, "tile", [(i, (i + by) % n) for i in range(n)])


VMEM = pl.BlockSpec(memory_space=pltpu.VMEM)
SMEM = pl.BlockSpec(memory_space=pltpu.SMEM)
PARAMS = pltpu.CompilerParams(vmem_limit_bytes=56 << 20)


def pair_map(count):
    return [[q - p if 0 <= q - p <= 2 else None for q in range(count)] for p in range(2)]


def small_weights(w_in, w_out):
    pad_in = jnp.pad(w_in.reshape(3, 3, 128, 4), ((0, 0), (0, 0), (0, 0), (0, 4)))
    zero = jnp.zeros((128, 8), BF)
    rows = []
    for p in range(2):
        cols = [
            pad_in[a, q - p] if 0 <= q - p <= 2 else zero for a in range(3) for q in range(4)
        ]
        rows.append(jnp.concatenate(cols, 1))
    packed_in = jnp.concatenate(rows, 0)
    pad_out = jnp.pad(w_out.reshape(3, 3, 4, 128), ((0, 0), (0, 0), (0, 4), (0, 0)))
    zero = jnp.zeros((8, 128), BF)
    rows = []
    for a in range(3):
        for p in range(2):
            cols = [q - p for q in (1, 2, 0, 3)]
            rows.append(jnp.concatenate([pad_out[a, b] if 0 <= b <= 2 else zero for b in cols], 1))
    return packed_in, jnp.concatenate(rows, 0)


def prep_call(w_enc, w_down, w_mid, w_dec):
    shapes = ((256, 1536), (256, 1152), (256, 2304), (256, 1536), (256, 1536), (256, 1536))
    return pl.pallas_call(
        prep_kernel,
        out_shape=[jax.ShapeDtypeStruct(s, BF) for s in shapes],
        in_specs=[VMEM] * 4,
        out_specs=[VMEM] * 6,
        compiler_params=PARAMS,
        name="prep",
    )(w_enc, w_down, w_mid, w_dec)


def main_call(width, coef, noise_parts, cond_parts, bias, weights):
    def rowbuf(n):
        return pltpu.VMEM((n, HALF, 256), BF)

    return pl.pallas_call(
        main_kernel,
        out_shape=jax.ShapeDtypeStruct((4, 4, 256), F32),
        in_specs=[SMEM, SMEM] + [VMEM] * 19,
        out_specs=VMEM,
        scratch_shapes=[
            pltpu.VMEM((31 * 8, 256), F32),
            pltpu.VMEM((31 * 8, 512), F32),
            rowbuf(29), rowbuf(29), rowbuf(27), rowbuf(27),
            rowbuf(13), rowbuf(13), rowbuf(13), rowbuf(11), rowbuf(11), rowbuf(11),
            rowbuf(19), rowbuf(19),
            pltpu.VMEM((48, 19 * HALF), F32),
            pltpu.VMEM((2, 17 * 8, HALF), F32),
        ],
        compiler_params=PARAMS,
        name="steps",
    )(width, coef, *noise_parts, *cond_parts, bias, *weights)


def coefficients(sigmas, w_sigma):
    now = sigmas[:2]
    var = now * now + SIGMA_DATA * SIGMA_DATA
    coef = jnp.stack(
        [
            jnp.broadcast_to(sigmas[0], (2,)),
            1.0 / jnp.sqrt(var),
            SIGMA_DATA * SIGMA_DATA / var,
            now * SIGMA_DATA / jnp.sqrt(var),
            (sigmas[1:] - now) / now,
        ],
        1,
    )
    bias = jnp.log(now)[:, None] * jnp.concatenate([w_sigma, w_sigma])[None, :]
    return coef, bias


def per_device(
    coarse_blocks, block_anchor, nest_width, sigmas, noise,
    w_context, w_in, w_sigma, w_enc, w_down, w_mid, w_dec, w_out,
):
    coef, bias = coefficients(sigmas, w_sigma)
    packed_in, packed_out = small_weights(w_in, w_out)

    chans = w_context.shape[1]
    cells = coarse_blocks.shape[1] // chans
    count = coarse_blocks.shape[0]
    blocks = coarse_blocks.reshape(count, chans, cells).transpose(0, 2, 1).reshape(count * cells, chans)
    partial = pl.pallas_call(
        encode_kernel,
        out_shape=jax.ShapeDtypeStruct((8, 2 * cells, 256), BF),
        in_specs=[SMEM, VMEM, VMEM],
        out_specs=VMEM,
        scratch_shapes=[pltpu.VMEM((count, cells, 256), F32)],
        compiler_params=PARAMS,
        name="encode",
    )(block_anchor, blocks, w_context)
    arrived = lax.all_to_all(partial, "band", 0, 0, tiled=True)

    own = noise[0].transpose(1, 0, 2).reshape(16, 256)
    near_up = turn(own, 1)
    near_down = turn(own, -1)
    three = jnp.concatenate([near_up, own, near_down], 0)
    far_up = turn(three, 3)
    far_down = turn(three, -3)

    enc, down, mid, dec2, even, odd = prep_call(w_enc, w_down, w_mid, w_dec)

    cond = (jnp.sum(arrived.astype(F32), axis=0) * (1.0 / math.sqrt(K // 2))).astype(BF)
    cond_up = shift(cond, 1)
    cond_down = shift(cond, -1)
    cond_far_up = shift(jnp.concatenate([cond_up, cond], 0), 2)
    cond_far_down = shift(jnp.concatenate([cond, cond_down], 0), -2)

    out = main_call(
        nest_width, coef,
        (far_up, near_up, own, near_down, far_down),
        (cond_far_up, cond_up, cond, cond_down, cond_far_down),
        bias,
        (packed_in, enc, down, mid, dec2, even, odd, packed_out),
    )
    return out[None]


def solution(mesh):
    return jax.shard_map(
        per_device,
        mesh=mesh,
        in_specs=(
            P("band", None), P(), P("band"), P(), P("band", None, "tile", None),
            P(), P(), P(), P(), P(), P(), P(), P(),
        ),
        out_specs=P("band", None, "tile", None),
        check_vma=False,
    )
```

time: 203 us -> 104 us (0.51)
  the two profiles are of different devices: /device:TPU:260 before, /device:TPU:8 now
where the time goes in v1:
time: 104 us
  starting transfers between devices  40.3 us (39%)
  Pallas kernels  37.7 us (36%)
  waiting for transfers between devices  14.8 us (14%)
  local copies, waits for them, and re-layouts  8.13 us (8%)
  other arithmetic  1.48 us (1%)
    pallas_call x1, Pallas kernels, main_call(): pl.pallas_call(main_kernel, out_shape=jax.ShapeDtypeStruct((4, 4, 256), F...  28.4 us
    ppermute x4, starting transfers between devices, turn(): return lax.ppermute(x, 'tile', [(i, (i + by) % n) for i in range(n)])  18.7 us
    ppermute x4, starting transfers between devices, shift(): lax.ppermute(x, 'tile', [(i, i + by) for i in range(n) if 0 <= i + by < n])  18 us
    all_to_all x1, waiting for transfers between devices, per_device(): arrived = lax.all_to_all(partial, 'band', 0, 0, tiled=True)  8.05 us
    pallas_call x1, Pallas kernels, per_device(): pl.pallas_call(encode_kernel, out_shape=jax.ShapeDtypeStruct((8, 2 * cell...  5.17 us
    pallas_call x1, Pallas kernels, prep_call(): pl.pallas_call(prep_kernel, out_shape=[jax.ShapeDtypeStruct(s, BF) for s...  4.21 us
    ppermute x4, waiting for transfers between devices, shift(): lax.ppermute(x, 'tile', [(i, i + by) for i in range(n) if 0 <= i + by < n])  4.2 us
    all_to_all x1, starting transfers between devices, per_device(): arrived = lax.all_to_all(partial, 'band', 0, 0, tiled=True)  3.62 us
  transfers between devices with their start and end apart: 9, of which 3 were waited for; matrix products, arithmetic and copies ran while one was open for 8% of the time, Pallas kernels for 9%

profile of v1, /device:TPU:8, one launch (start us, length us, event | category | flops | bytes accessed | tf_op | source)
XLA Modules:
  0.0 103.5 jit_solution(5188050729898220163)
XLA Ops:
  0.0 0.7 copy.26
  0.7 7.7 %collective-permute-start.1 = (f32[16,256]{1,0:T(8,128)S(1)}, f32[16,256]{1,0:T(8,128)S(1)}, u32[]{:S(2)}, u32[]{:S(2)}) collective-permute-start(f32[16,256]{1,0:T(8,128)S(1)} %reshape.17.own), channel_id=1, source_target_pairs={{0,63},{1,0},{2,1},{3,2},{4,3},{5,4},{6,5},{7,6},{8,7},{9,8},{10,9... | collective-permute-start | bytes 49160 | tf_op jit(solution)/shard_map/ppermute | solution.py:333
  8.5 1.9 %collective-permute-start = (f32[16,256]{1,0:T(8,128)S(1)}, f32[16,256]{1,0:T(8,128)S(1)}, u32[]{:S(2)}, u32[]{:S(2)}) collective-permute-start(f32[16,256]{1,0:T(8,128)S(1)} %reshape.17.own), channel_id=1, source_target_pairs={{0,1},{1,2},{2,3},{3,4},{4,5},{5,6},{6,7},{7,8},{8,9},{9,10},{10,1... | collective-permute-start | bytes 49160 | tf_op jit(solution)/shard_map/ppermute | solution.py:333
  10.4 1.5 %copy.28.w_ref = bf16[256,70]{1,0:T(8,128)(2,1)} copy(bf16[256,70]{0,1:T(8,128)(2,1)} %param.18) | data formatting | bytes 71680 | tf_op args[5]
  11.9 1.9 %reshape.18 = bf16[64,70,64]{2,1,0:T(8,128)(2,1)S(1)} reshape(bf16[64,4480]{1,0:T(8,128)(2,1)} %param.13) | data formatting | bytes 1146880 | tf_op jit(solution)/shard_map/reshape | solution.py:427
  13.8 1.5 %copy.27 = bf16[64,64,70]{2,1,0:T(8,128)(2,1)} copy(bf16[64,64,70]{1,2,0:T(8,128)(2,1)S(1)} %bitcast.54) | data formatting | bytes 1146880 | tf_op jit(solution)/shard_map/transpose | solution.py:427
  15.3 5.2 %encode.1 = bf16[8,128,256]{2,1,0:T(8,128)(2,1)} custom-call(s32[8,64]{1,0:T(8,128)} %anchor_ref.1, bf16[4096,70]{1,0:T(8,128)(2,1)} %bitcast.55, bf16[256,70]{1,0:T(8,128)(2,1)} %copy.28.w_ref), custom_call_target="tpu_custom_call" | custom-call | tf_op jit(solution)/shard_map/encode/pallas_call | solution.py:428
  20.5 3.6 %all-to-all-start = ((bf16[8,128,256]{2,1,0:T(8,128)(2,1)}), bf16[8,128,256]{2,1,0:T(8,128)(2,1)S(1)}, u32[]{:S(2)}, u32[]{:S(2)}) async-start(bf16[8,128,256]{2,1,0:T(8,128)(2,1)} %encode.1), calls=%async_computation | async-start | bytes 1048576 | tf_op jit(solution)/shard_map/all_to_all | solution.py:437
  24.1 0.3 copy.29
  24.4 0.1 slice_bitcast_fusion
  24.5 0.2 concatenate.47
  24.7 0.2 concatenate.46
  25.0 0.6 pad_maximum_fusion.2.w_in
  25.7 0.6 broadcast_multiply_fusion.bias_ref
  26.3 8.0 %all-to-all-done = bf16[8,128,256]{2,1,0:T(8,128)(2,1)S(1)} async-done(((bf16[8,128,256]{2,1,0:T(8,128)(2,1)}), bf16[8,128,256]{2,1,0:T(8,128)(2,1)S(1)}, u32[]{:S(2)}, u32[]{:S(2)}) %all-to-all-start) | async-done | bytes 524320 | tf_op jit(solution)/shard_map/all_to_all | solution.py:437
  34.5 9.4 %collective-permute-start.6 = (bf16[128,256]{1,0:T(8,128)(2,1)S(1)}, bf16[128,256]{1,0:T(8,128)(2,1)S(1)}, u32[]{:S(2)}, u32[]{:S(2)}) collective-permute-start(bf16[128,256]{1,0:T(8,128)(2,1)S(1)} %multiply_convert_fusion.cond_own), channel_id=1, source_target_pairs={{1,0},{2,1},{3,2},{4,3},{5,4},{6,5},{7,6},{8,7},{9,8},{10,9},{11,1... | collective-permute-start | bytes 196616 | tf_op jit(solution)/shard_map/ppermute | solution.py:328
  43.9 1.9 %collective-permute-start.4 = (bf16[128,256]{1,0:T(8,128)(2,1)S(1)}, bf16[128,256]{1,0:T(8,128)(2,1)S(1)}, u32[]{:S(2)}, u32[]{:S(2)}) collective-permute-start(bf16[128,256]{1,0:T(8,128)(2,1)S(1)} %multiply_convert_fusion.cond_own), channel_id=1, source_target_pairs={{0,1},{1,2},{2,3},{3,4},{4,5},{5,6},{6,7},{7,8},{8,9},{9,10},{10,1... | collective-permute-start | bytes 196616 | tf_op jit(solution)/shard_map/ppermute | solution.py:328
  45.8 4.2 %collective-permute-done.4.cond_up = bf16[128,256]{1,0:T(8,128)(2,1)S(1)} collective-permute-done((bf16[128,256]{1,0:T(8,128)(2,1)S(1)}, bf16[128,256]{1,0:T(8,128)(2,1)S(1)}, u32[]{:S(2)}, u32[]{:S(2)}) %collective-permute-start.4) | collective-permute-done | bytes 65568 | tf_op jit(solution)/shard_map/ppermute | solution.py:328
  50.0 1.3 %collective-permute-start.7 = (bf16[256,256]{1,0:T(8,128)(2,1)S(1)}, bf16[256,256]{1,0:T(8,128)(2,1)S(1)}, u32[]{:S(2)}, u32[]{:S(2)}) collective-permute-start(bf16[256,256]{1,0:T(8,128)(2,1)S(1)} %get-tuple-element.26), channel_id=1, source_target_pairs={{2,0},{3,1},{4,2},{5,3},{6,4},{7,5},{8,6},{9,7},{10,8},{11,9},{12,... | collective-permute-start | bytes 393224 | tf_op jit(solution)/shard_map/ppermute | solution.py:328
  51.3 5.5 %collective-permute-start.5 = (bf16[256,256]{1,0:T(8,128)(2,1)S(1)}, bf16[256,256]{1,0:T(8,128)(2,1)S(1)}, u32[]{:S(2)}, u32[]{:S(2)}) collective-permute-start(bf16[256,256]{1,0:T(8,128)(2,1)S(1)} %get-tuple-element.27), channel_id=1, source_target_pairs={{0,2},{1,3},{2,4},{3,5},{4,6},{5,7},{6,8},{7,9},{8,10},{9,11},{10,... | collective-permute-start | bytes 393224 | tf_op jit(solution)/shard_map/ppermute | solution.py:328
  56.8 5.6 %collective-permute-start.3 = (f32[48,256]{1,0:T(8,128)S(1)}, f32[48,256]{1,0:T(8,128)S(1)}, u32[]{:S(2)}, u32[]{:S(2)}) collective-permute-start(f32[48,256]{1,0:T(8,128)S(1)} %constant_dynamic-update-slice_fusion), channel_id=1, source_target_pairs={{0,61},{1,62},{2,63},{3,0},{4,1},{5,2},{6,3},{7,4},{8,5},{9,6},{10... | collective-permute-start | bytes 147464 | tf_op jit(solution)/shard_map/ppermute | solution.py:333
  62.5 3.4 %collective-permute-start.2 = (f32[48,256]{1,0:T(8,128)S(1)}, f32[48,256]{1,0:T(8,128)S(1)}, u32[]{:S(2)}, u32[]{:S(2)}) collective-permute-start(f32[48,256]{1,0:T(8,128)S(1)} %constant_dynamic-update-slice_fusion), channel_id=1, source_target_pairs={{0,3},{1,4},{2,5},{3,6},{4,7},{5,8},{6,9},{7,10},{8,11},{9,12},{10... | collective-permute-start | bytes 147464 | tf_op jit(solution)/shard_map/ppermute | solution.py:333
  66.6 0.1 copy.24
  66.7 0.1 copy.23
  66.8 0.1 copy.25
  66.8 0.1 copy.22
  66.9 4.2 %prep.1 = (bf16[256,1536]{1,0:T(8,128)(2,1)}, bf16[256,1152]{1,0:T(8,128)(2,1)}, bf16[256,2304]{1,0:T(8,128)(2,1)}, bf16[256,1536]{1,0:T(8,128)(2,1)}, bf16[256,...) custom-call(bf16[9,128,128]{2,1,0:T(8,128)(2,1)} %w_enc.1, bf16[9,256,128]{2,1,0:T(8,128)(2,1)} %w_down.1, ...), custom_call_target="tpu_custom_call" | custom-call | tf_op jit(solution)/shard_map/prep/pallas_call | solution.py:367
  71.2 0.6 stack.19.coef_ref
  71.9 2.6 %collective-permute-done.2.far_up = f32[48,256]{1,0:T(8,128)S(1)} collective-permute-done((f32[48,256]{1,0:T(8,128)S(1)}, f32[48,256]{1,0:T(8,128)S(1)}, u32[]{:S(2)}, u32[]{:S(2)}) %collective-permute-start.2) | collective-permute-done | bytes 49184 | tf_op jit(solution)/shard_map/ppermute | solution.py:333
  74.5 0.6 copy-done.10
  75.1 0.1 copy-done.4
  75.2 28.4 %steps.1 = f32[4,4,256]{2,1,0:T(4,128)} custom-call(s32[1]{0:T(128)S(6)} %copy.37.width_ref, f32[2,5]{1,0:T(2,128)} %stack.19.coef_ref, f32[48,256]{1,0:T(8,128)} %copy-done.10, f32[16,256]{1,0:T(8,128)} %copy-done.8, f32[16,256]{1,0:T(8,128)} %copy-done.3, f32[16,256]{1,0:T(8,128)} %copy-done.7, f32[48,256]{1,0:T(8,128)} %copy-done.9, ...), custom_call_target="tpu_custom_call" | custom-call | tf_op jit(solution)/shard_map/steps/pallas_call | solution.py:381
  (53 shorter events, 0.4 us)
Async XLA Ops:
  0.7 45.1 %copy-start.3 = (f32[16,256]{1,0:T(8,128)}, f32[16,256]{1,0:T(8,128)S(1)}, u32[]{:S(2)}) copy-start(f32[16,256]{1,0:T(8,128)S(1)} %reshape.17.own) | copy-start | bytes 49156
  0.7 56.1 %collective-permute-start.1 = (f32[16,256]{1,0:T(8,128)S(1)}, f32[16,256]{1,0:T(8,128)S(1)}, u32[]{:S(2)}, u32[]{:S(2)}) collective-permute-start(f32[16,256]{1,0:T(8,128)S(1)} %reshape.17.own), channel_id=1, source_target_pairs={{0,63},{1,0},{2,1},{3,2},{4,3},{5,4},{6,5},{7,6},{8,7},{9,8},{10,9... | collective-permute-start | bytes 49160 | tf_op jit(solution)/shard_map/ppermute | solution.py:333
  8.5 17.8 %collective-permute-start = (f32[16,256]{1,0:T(8,128)S(1)}, f32[16,256]{1,0:T(8,128)S(1)}, u32[]{:S(2)}, u32[]{:S(2)}) collective-permute-start(f32[16,256]{1,0:T(8,128)S(1)} %reshape.17.own), channel_id=1, source_target_pairs={{0,1},{1,2},{2,3},{3,4},{4,5},{5,6},{6,7},{7,8},{8,9},{9,10},{10,1... | collective-permute-start | bytes 49160 | tf_op jit(solution)/shard_map/ppermute | solution.py:333
  15.3 8.8 %copy-start.11 = (bf16[9,128,4]{1,2,0:T(4,128)(2,1)S(1)}, bf16[9,128,4]{1,2,0:T(4,128)(2,1)}, u32[]{:S(2)}) copy-start(bf16[9,128,4]{1,2,0:T(4,128)(2,1)} %param.19) | copy-start | bytes 27652
  20.5 4.4 %copy-start.13 = (f32[3]{0:T(128)S(1)}, f32[3]{0:T(128)}, u32[]{:S(2)}) copy-start(f32[3]{0:T(128)} %param.16) | copy-start | bytes 40
  20.5 4.5 %copy-start.12 = (bf16[9,4,128]{2,1,0:T(4,128)(2,1)S(1)}, bf16[9,4,128]{2,1,0:T(4,128)(2,1)}, u32[]{:S(2)}) copy-start(bf16[9,4,128]{2,1,0:T(4,128)(2,1)} %param.25) | copy-start | bytes 27652
  20.5 13.9 %all-to-all-start = ((bf16[8,128,256]{2,1,0:T(8,128)(2,1)}), bf16[8,128,256]{2,1,0:T(8,128)(2,1)S(1)}, u32[]{:S(2)}, u32[]{:S(2)}) async-start(bf16[8,128,256]{2,1,0:T(8,128)(2,1)} %encode.1), calls=%async_computation | async-start | bytes 1048576 | tf_op jit(solution)/shard_map/all_to_all | solution.py:437
  24.1 1.5 %copy-start.14 = (f32[128]{0:T(128)S(1)}, f32[128]{0:T(128)}, u32[]{:S(2)}) copy-start(f32[128]{0:T(128)} %param.20) | copy-start | bytes 1540
  26.3 44.8 %copy-start.8 = (f32[16,256]{1,0:T(8,128)}, f32[16,256]{1,0:T(8,128)S(1)}, u32[]{:S(2)}) copy-start(f32[16,256]{1,0:T(8,128)S(1)} %collective-permute-done.near_up) | copy-start | bytes 49156
  34.5 36.7 %copy-start = (bf16[128,256]{1,0:T(8,128)(2,1)}, bf16[128,256]{1,0:T(8,128)(2,1)S(1)}, u32[]{:S(2)}) copy-start(bf16[128,256]{1,0:T(8,128)(2,1)S(1)} %multiply_convert_fusion.cond_own) | copy-start | bytes 196612
  34.5 11.3 %collective-permute-start.6 = (bf16[128,256]{1,0:T(8,128)(2,1)S(1)}, bf16[128,256]{1,0:T(8,128)(2,1)S(1)}, u32[]{:S(2)}, u32[]{:S(2)}) collective-permute-start(bf16[128,256]{1,0:T(8,128)(2,1)S(1)} %multiply_convert_fusion.cond_own), channel_id=1, source_target_pairs={{1,0},{2,1},{3,2},{4,3},{5,4},{6,5},{7,6},{8,7},{9,8},{10,9},{11,1... | collective-permute-start | bytes 196616 | tf_op jit(solution)/shard_map/ppermute | solution.py:328
  43.9 6.2 %collective-permute-start.4 = (bf16[128,256]{1,0:T(8,128)(2,1)S(1)}, bf16[128,256]{1,0:T(8,128)(2,1)S(1)}, u32[]{:S(2)}, u32[]{:S(2)}) collective-permute-start(bf16[128,256]{1,0:T(8,128)(2,1)S(1)} %multiply_convert_fusion.cond_own), channel_id=1, source_target_pairs={{0,1},{1,2},{2,3},{3,4},{4,5},{5,6},{6,7},{7,8},{8,9},{9,10},{10,1... | collective-permute-start | bytes 196616 | tf_op jit(solution)/shard_map/ppermute | solution.py:328
  45.8 25.3 %copy-start.1 = (bf16[128,256]{1,0:T(8,128)(2,1)}, bf16[128,256]{1,0:T(8,128)(2,1)S(1)}, u32[]{:S(2)}) copy-start(bf16[128,256]{1,0:T(8,128)(2,1)S(1)} %collective-permute-done.6.cond_down) | copy-start | bytes 196612
  50.0 21.2 %copy-start.2 = (bf16[128,256]{1,0:T(8,128)(2,1)}, bf16[128,256]{1,0:T(8,128)(2,1)S(1)}, u32[]{:S(2)}) copy-start(bf16[128,256]{1,0:T(8,128)(2,1)S(1)} %collective-permute-done.4.cond_up) | copy-start | bytes 196612
  50.0 24.4 %collective-permute-start.7 = (bf16[256,256]{1,0:T(8,128)(2,1)S(1)}, bf16[256,256]{1,0:T(8,128)(2,1)S(1)}, u32[]{:S(2)}, u32[]{:S(2)}) collective-permute-start(bf16[256,256]{1,0:T(8,128)(2,1)S(1)} %get-tuple-element.26), channel_id=1, source_target_pairs={{2,0},{3,1},{4,2},{5,3},{6,4},{7,5},{8,6},{9,7},{10,8},{11,9},{12,... | collective-permute-start | bytes 393224 | tf_op jit(solution)/shard_map/ppermute | solution.py:328
  51.3 23.1 %collective-permute-start.5 = (bf16[256,256]{1,0:T(8,128)(2,1)S(1)}, bf16[256,256]{1,0:T(8,128)(2,1)S(1)}, u32[]{:S(2)}, u32[]{:S(2)}) collective-permute-start(bf16[256,256]{1,0:T(8,128)(2,1)S(1)} %get-tuple-element.27), channel_id=1, source_target_pairs={{0,2},{1,3},{2,4},{3,5},{4,6},{5,7},{6,8},{7,9},{8,10},{9,11},{10,... | collective-permute-start | bytes 393224 | tf_op jit(solution)/shard_map/ppermute | solution.py:328
  56.8 14.4 %copy-start.7 = (f32[16,256]{1,0:T(8,128)}, f32[16,256]{1,0:T(8,128)S(1)}, u32[]{:S(2)}) copy-start(f32[16,256]{1,0:T(8,128)S(1)} %collective-permute-done.1.near_down) | copy-start | bytes 49156
  56.8 15.0 %collective-permute-start.3 = (f32[48,256]{1,0:T(8,128)S(1)}, f32[48,256]{1,0:T(8,128)S(1)}, u32[]{:S(2)}, u32[]{:S(2)}) collective-permute-start(f32[48,256]{1,0:T(8,128)S(1)} %constant_dynamic-update-slice_fusion), channel_id=1, source_target_pairs={{0,61},{1,62},{2,63},{3,0},{4,1},{5,2},{6,3},{7,4},{8,5},{9,6},{10... | collective-permute-start | bytes 147464 | tf_op jit(solution)/shard_map/ppermute | solution.py:333
  62.5 12.0 %collective-permute-start.2 = (f32[48,256]{1,0:T(8,128)S(1)}, f32[48,256]{1,0:T(8,128)S(1)}, u32[]{:S(2)}, u32[]{:S(2)}) collective-permute-start(f32[48,256]{1,0:T(8,128)S(1)} %constant_dynamic-update-slice_fusion), channel_id=1, source_target_pairs={{0,3},{1,4},{2,5},{3,6},{4,7},{5,8},{6,9},{7,10},{8,11},{9,12},{10... | collective-permute-start | bytes 147464 | tf_op jit(solution)/shard_map/ppermute | solution.py:333
  65.9 5.3 %copy-start.6 = (bf16[48,512]{1,0:T(8,128)(2,1)}, bf16[48,512]{1,0:T(8,128)(2,1)S(1)}, u32[]{:S(2)}) copy-start(bf16[48,512]{1,0:T(8,128)(2,1)S(1)} %constant_dynamic-update-slice_fusion.3.w_out) | copy-start | bytes 147460
  71.9 2.6 %copy-start.9 = (f32[48,256]{1,0:T(8,128)}, f32[48,256]{1,0:T(8,128)S(1)}, u32[]{:S(2)}) copy-start(f32[48,256]{1,0:T(8,128)S(1)} %collective-permute-done.3.far_down) | copy-start | bytes 147460
  74.4 0.6 copy-start.10
  74.4 0.7 copy-start.4
  74.5 0.7 copy-start.5

commit v2 on v1

v2 whole, which is shorter than its diff:
```python
import functools
import math

import jax
import jax.numpy as jnp
from jax import lax
from jax.experimental import pallas as pl
from jax.experimental.pallas import tpu as pltpu
from jax.sharding import PartitionSpec as P

K = 96
SIGMA_DATA = 0.5
BF = jnp.bfloat16
F32 = jnp.float32
HALF = 128
ROWS = 256
NT = (((1,), (1,)), ((), ()))
TN = (((0,), (1,)), ((), ()))

STEP_ROWS = (
    dict(scaled=(-15, 31), first=(-14, 29), second=(-13, 27), third=(-6, 13), fourth=(-5, 11), fifth=(-8, 19), out=(-7, 17)),
    dict(scaled=(-7, 17), first=(-6, 15), second=(-5, 13), third=(-2, 6), fourth=(-1, 4), fifth=(-1, 6), out=(0, 4)),
)


def silu(v):
    h = 0.5 * v
    return h + h * jnp.tanh(h)


def dot_nt(a, b):
    return lax.dot_general(a, b, NT, preferred_element_type=F32)


def encode_kernel(anchor_ref, blocks_ref, w_ref, out_ref, enc_ref, flat, wide):
    band = lax.axis_index("band")
    tile = lax.axis_index("tile")
    count, cells = enc_ref.shape[:2]
    chans = w_ref.shape[0]
    tiles = blocks_ref.shape[1] // 128
    group = 8 * tiles

    flat[count * tiles :, :] = jnp.zeros((flat.shape[0] - count * tiles, 128), F32)
    for g in range(count // 16):
        for t in range(tiles):
            v = blocks_ref[16 * g : 16 * g + 16, 128 * t : 128 * t + 128].astype(F32)
            flat[2 * g * group + 8 * t : 2 * g * group + 8 * t + 8, :] = v[:8]
            flat[(2 * g + 1) * group + 8 * t : (2 * g + 1) * group + 8 * t + 8, :] = v[8:]

    w = w_ref[...].astype(F32)
    for half in range(2):
        wide[half, 0:chans, :] = w[:, 128 * half : 128 * half + 128]
        wide[half, chans:80, :] = jnp.zeros((80 - chans, 128), F32)
    weight = jnp.concatenate(
        [
            jnp.concatenate([wide[half, pl.ds(odd, 40, stride=2), :] for half in range(2)], 1)
            for odd in range(2)
        ],
        0,
    ).astype(BF)
    first = lax.broadcasted_iota(jnp.int32, (40, 128), 1) < 64

    def encode(g, carry):
        begin = pl.multiple_of(g * group, 8)
        cols = []
        for k in range(4):
            one = flat[pl.ds(begin + 2 * k, 40, stride=8), :]
            two = flat[pl.ds(begin + 2 * k + 1, 40, stride=8), :]
            even = jnp.where(first, one, pltpu.roll(two, 64, 1))
            odd = jnp.where(first, pltpu.roll(one, 64, 1), two)
            cols.append(jnp.concatenate([even, odd], 0))
        x = jnp.concatenate(cols, 1).astype(BF)
        v = lax.dot_general(x, weight, (((0,), (0,)), ((), ())), preferred_element_type=F32)
        v = silu(v).astype(BF).astype(F32)
        enc_ref[pl.ds(g * 8, 8)] = v.reshape(8, cells, 256)
        return carry

    lax.fori_loop(0, count // 8, encode, 0)

    def window(k, carry):
        nest = k // 2
        part = k % 2
        anchor = anchor_ref[nest, tile]
        begin = anchor + (band - anchor + 512) % 8 + part * 48
        row = (begin % 512) // 8
        total = enc_ref[row]
        for m in range(1, 6):
            total = total + enc_ref[(row + m) % count]
        out_ref[nest, pl.ds(pl.multiple_of(part * cells, cells), cells), :] = total.astype(BF)
        return carry

    lax.fori_loop(0, 16, window, 0)


def pair_weight(w, a):
    zero = jnp.zeros_like(w(a, 0))
    own = jnp.concatenate(
        [jnp.concatenate([w(a, 1), w(a, 2)], 1), jnp.concatenate([w(a, 0), w(a, 1)], 1)], 0
    )
    rim = jnp.concatenate(
        [jnp.concatenate([w(a, 0), zero], 1), jnp.concatenate([zero, w(a, 2)], 1)], 0
    )
    return own, rim


def prep_kernel(w_enc, w_down, w_mid, w_dec, enc_o, down_o, mid_o, dec2_o, even_o, odd_o):
    for a in range(3):
        own, rim = pair_weight(lambda i, b: w_enc[3 * i + b], a)
        enc_o[:, 512 * a : 512 * a + 256] = own
        enc_o[:, 512 * a + 256 : 512 * a + 512] = rim
        own, rim = pair_weight(lambda i, b: w_dec[3 * i + b, :, 0:128], a)
        dec2_o[:, 512 * a : 512 * a + 256] = own
        dec2_o[:, 512 * a + 256 : 512 * a + 512] = rim
        down_o[:, 256 * a : 256 * a + 128] = w_down[3 * a + 1]
        down_o[:, 256 * a + 128 : 256 * a + 256] = w_down[3 * a + 2]
        down_o[:, 768 + 128 * a : 896 + 128 * a] = w_down[3 * a]
        for b in range(3):
            mid_o[:, 768 * a + 256 * b : 768 * a + 256 * b + 256] = w_mid[3 * a + b]

    def up(a, b):
        return w_dec[3 * a + b, :, 128:384].astype(F32)

    for o_ref, sets in ((even_o, ((0,), (1, 2))), (odd_o, ((0, 1), (2,)))):
        for k, taps in enumerate(sets):
            col = [sum(up(a, b) for a in taps) for b in range(3)]
            zero = jnp.zeros_like(col[0])
            o_ref[:, 768 * k : 768 * k + 256] = jnp.concatenate([col[0], zero], 0).astype(BF)
            o_ref[:, 768 * k + 256 : 768 * k + 512] = jnp.concatenate(
                [col[1] + col[2], col[0] + col[1]], 0
            ).astype(BF)
            o_ref[:, 768 * k + 512 : 768 * k + 768] = jnp.concatenate([zero, col[2]], 0).astype(BF)


class Field:
    def __init__(self, width):
        self.tile = lax.axis_index("tile")
        lane = lax.broadcasted_iota(jnp.int32, (HALF, 256), 1)
        pair = lax.broadcasted_iota(jnp.int32, (HALF, 256), 0)
        self.colmask = (2 * pair + lane // 128 < width).astype(F32)
        self.halfmask = (2 * pair < width).astype(F32)
        self.natural = (lax.broadcasted_iota(jnp.int32, (8, 256), 1) < width).astype(F32)

    def fine_ok(self, rho):
        row = self.tile * 4 + rho
        return jnp.logical_and(row >= 0, row < ROWS).astype(F32)

    def half_ok(self, h):
        row = self.tile * 2 + h
        return jnp.logical_and(row >= 0, row < ROWS // 2).astype(F32)

    def keep_pairs(self, y, center, rim, at, n, lo):
        y = jnp.concatenate(
            [y[k * HALF : (k + 1) * HALF] * (self.colmask * self.fine_ok(lo + at + k)) for k in range(n)], 0
        )
        side = jnp.concatenate([slide(y[:, 128:], 1), slide(y[:, :128], -1)], 1).astype(BF)
        y = y.astype(BF)
        for k in range(n):
            center[at + k] = y[k * HALF : (k + 1) * HALF]
            rim[at + k] = side[k * HALF : (k + 1) * HALF]

    def keep_half(self, y, center, left, right, at, n, lo):
        y = jnp.concatenate(
            [y[k * HALF : (k + 1) * HALF] * (self.halfmask * self.half_ok(lo + at + k)) for k in range(n)], 0
        )
        sides = (slide(y, 1).astype(BF), slide(y, -1).astype(BF))
        y = y.astype(BF)
        for k in range(n):
            cut = slice(k * HALF, (k + 1) * HALF)
            center[at + k] = y[cut]
            left[at + k] = sides[0][cut]
            right[at + k] = sides[1][cut]


def slide(x, by):
    rows = x.shape[0]
    edge = 0 if by == 1 else HALF - 1
    where = lax.broadcasted_iota(jnp.int32, x.shape, 0) % HALF
    return jnp.where(where == edge, 0.0, pltpu.roll(x, by % rows, 0))


def stacked(ref, at, n, step=1):
    return jnp.concatenate([ref[at + step * k] for k in range(n)], 0)


def chunks(total, size, body):
    full = total // size
    if full == 1:
        body(0, size)
    elif full:
        lax.fori_loop(0, full, lambda i, c: (body(i * size, size), c)[1], 0)
    if total % size:
        body(full * size, total % size)


def encoder(field, rows, state, scale, bias, w_in, w_enc, spread, firstc, firste, secondc, seconde, size):
    col = lax.broadcasted_iota(jnp.int32, (256, 512), 0)
    place = lax.broadcasted_iota(jnp.int32, (256, 512), 1)
    pick = (col == 2 * (place % 128) + place // 128 - 1).astype(F32).astype(BF)
    n_scaled = rows["scaled"][1]
    scaled = (state[0 : 8 * n_scaled, :] * scale).astype(BF)
    spread[0 : 8 * n_scaled, :] = jnp.dot(scaled, pick, preferred_element_type=F32)
    first_lo, total = rows["first"]

    def first_rows(at, n):
        cols = []
        for k in range(n):
            cols.append(
                jnp.concatenate(
                    [
                        spread[pl.ds(pl.multiple_of((at + k + a) * 8, 8), 8), 128 * q : 128 * q + 128]
                        for a in range(3)
                        for q in range(4)
                    ],
                    0,
                )
            )
        x = jnp.concatenate(cols, 1).astype(BF)
        y = lax.dot_general(x, w_in[...], TN, preferred_element_type=F32)
        field.keep_pairs(silu(y + bias), firstc, firste, at, n, first_lo)

    chunks(total, 5, first_rows)
    second_lo, total = rows["second"]

    def second_rows(at, n):
        x = jnp.concatenate([stacked(ref, at + a, n) for a in range(3) for ref in (firstc, firste)], 1)
        field.keep_pairs(silu(dot_nt(x, w_enc[...])), secondc, seconde, at, n, second_lo)

    chunks(total, size, second_rows)


def first_kernel(
    width_ref, coef_ref, own, up3, down3, near_up, near_down, bias_ref, w_in, w_enc,
    state_ref, secondc, seconde,
    state, spread, firstc, firste,
):
    field = Field(width_ref[0])
    rows = STEP_ROWS[0]
    start = coef_ref[0, 0]
    empty = jnp.zeros((4, 256), F32)
    pieces = {-3: up3, 0: own, 3: down3}
    for tile_off in range(-4, 4):
        if tile_off in pieces:
            value = pieces[tile_off][...]
        else:
            ref = near_up if (tile_off + 1) % 3 == 0 else near_down
            slot = (tile_off + (1 if ref is near_up else -1)) // 3 + 1
            begin = 128 + 16 * slot
            value = ref[begin : begin + 16, :].astype(F32) + ref[begin + 48 : begin + 64, :].astype(F32)
        for r in range(4):
            rho = 4 * tile_off + r
            if rho >= -15:
                row = jnp.concatenate([value[4 * r : 4 * r + 4], empty], 0)
                state[8 * (rho + 15) : 8 * (rho + 16), :] = start * row * (field.natural * field.fine_ok(rho))
    out_lo, n_out = rows["out"]
    state_ref[...] = state[8 * (out_lo + 15) : 8 * (out_lo + 15 + n_out), :]
    encoder(
        field, rows, state, coef_ref[0, 1], bias_ref[0:1, :], w_in, w_enc,
        spread, firstc, firste, secondc, seconde, 9,
    )


def second_kernel(
    width_ref, coef_ref, state_in, secondc0, seconde0,
    far_up, near_up, near_down, far_down, own_cond,
    bias_ref, w_in, w_enc, w_down, w_mid, w_dec2, w_even, w_odd, w_out,
    out_ref,
    state, spread, firstc, firste, secondc1, seconde1, third, thirdl, thirdr, fourth, fourthl, fourthr,
    fifthc, fifthe, prod, picked,
):
    field = Field(width_ref[0])
    weave_j = lax.broadcasted_iota(jnp.int32, (HALF, 256), 0)
    weave_c = lax.broadcasted_iota(jnp.int32, (HALF, 256), 1)
    weave = [(weave_c == 2 * weave_j + p).astype(F32) for p in range(2)]
    repeat = (
        lax.broadcasted_iota(jnp.int32, (HALF, 64), 0) // 2 == lax.broadcasted_iota(jnp.int32, (HALF, 64), 1)
    ).astype(F32).astype(BF)
    conds = (
        (far_up, 0), (far_up, 1), (far_up, 2), (far_up, 3),
        (near_up, 0), (near_up, 1), (own_cond, 0), (own_cond, 1), (near_down, 0), (near_down, 1),
        (far_down, 0), (far_down, 1), (far_down, 2), (far_down, 3),
    )

    for step in range(2):
        rows = STEP_ROWS[step]
        scale, keep, mix, move = (coef_ref[step, 1 + i] for i in range(4))
        if step == 0:
            secondc, seconde = secondc0, seconde0
        else:
            secondc, seconde = secondc1, seconde1
            encoder(
                field, rows, state, scale, bias_ref[1:2, :], w_in, w_enc,
                spread, firstc, firste, secondc, seconde, 13,
            )

        second_lo = rows["second"][0]
        third_lo, total = rows["third"]

        def third_rows(at, n):
            begin = 2 * third_lo - 1 - second_lo + 2 * at
            x = jnp.concatenate(
                [stacked(secondc, begin + a, n, 2) for a in range(3)]
                + [
                    jnp.concatenate([seconde[begin + a + 2 * k][:, :128] for k in range(n)], 0)
                    for a in range(3)
                ],
                1,
            )
            y = dot_nt(x, w_down[...])
            add = []
            for k in range(n):
                ref, r = conds[third_lo + at + k + 6]
                add.append(jnp.dot(repeat, ref[64 * r : 64 * r + 64, :], preferred_element_type=F32))
            y = y + jnp.concatenate(add, 0)
            field.keep_half(silu(y), third, thirdl, thirdr, at, n, third_lo)

        for at in range(0, total, 7):
            third_rows(at, min(7, total - at))

        fourth_lo, total = rows["fourth"]

        def fourth_rows(at, n):
            begin = fourth_lo - 1 - third_lo + at
            x = jnp.concatenate(
                [stacked(ref, begin + a, n) for a in range(3) for ref in (thirdl, third, thirdr)], 1
            )
            field.keep_half(silu(dot_nt(x, w_mid[...])), fourth, fourthl, fourthr, at, n, fourth_lo)

        for at in range(0, total, 6):
            fourth_rows(at, min(6, total - at))

        fifth_lo, total = rows["fifth"]

        def fifth_rows(at, n):
            rho = fifth_lo + at
            odd = rho % 2
            begin = rho - 1 - second_lo
            h = (rho - odd) // 2 - fourth_lo - (0 if odd else 1)
            x = jnp.concatenate(
                [stacked(ref, begin + a, n, 2) for a in range(3) for ref in (secondc, seconde)], 1
            )
            z = jnp.concatenate(
                [stacked(ref, h + a, n) for a in range(2) for ref in (fourthl, fourth, fourthr)], 1
            )
            y = silu(dot_nt(x, w_dec2[...]) + dot_nt(z, (w_odd if odd else w_even)[...]))
            for k in range(n):
                field.keep_pairs(y[k * HALF : (k + 1) * HALF], fifthc, fifthe, at + 2 * k, 1, fifth_lo)

        for parity in range(2):
            n_rows = (total - parity + 1) // 2
            for at in range(0, n_rows, 5):
                fifth_rows(parity + 2 * at, min(5, n_rows - at))

        def out_rows(at, n):
            x = jnp.concatenate([stacked(fifthc, at, n), stacked(fifthe, at, n)], 1)
            prod[:, at * HALF : (at + n) * HALF] = dot_nt(w_out[...], x)

        for at in range(0, total, 10):
            out_rows(at, min(10, total - at))
        out_lo, total = rows["out"]
        for k in range(total):
            for p in range(2):
                picked[p, 8 * k : 8 * k + 8, :] = sum(
                    prod[16 * a + 8 * p : 16 * a + 8 * p + 8, (k + a) * HALF : (k + a + 1) * HALF]
                    for a in range(3)
                )
        net = sum(
            jnp.dot(
                picked[p, 0 : 8 * total, :], weave[p], preferred_element_type=F32, precision=lax.Precision.HIGHEST
            )
            for p in range(2)
        )
        if step == 0:
            now = state_in[...]
        else:
            skip = 8 * (out_lo - rows["scaled"][0])
            now = state[skip : skip + 8 * total, :]
        denoised = keep * now + mix * net
        now = now + move * (now - denoised)
        for k in range(total):
            value = now[8 * k : 8 * k + 8] * (field.natural * field.fine_ok(out_lo + k))
            if step == 0:
                state[8 * k : 8 * k + 8, :] = value
            else:
                out_ref[:, k, :] = value[0:4]


def turn(x, by):
    n = lax.axis_size("tile")
    return lax.ppermute(x, "tile", [(i, (i + by) % n) for i in range(n)])


VMEM = pl.BlockSpec(memory_space=pltpu.VMEM)
SMEM = pl.BlockSpec(memory_space=pltpu.SMEM)
PARAMS = pltpu.CompilerParams(vmem_limit_bytes=56 << 20)


def pair_map(count):
    return [[q - p if 0 <= q - p <= 2 else None for q in range(count)] for p in range(2)]


def small_weights(w_in, w_out):
    pad_in = jnp.pad(w_in.reshape(3, 3, 128, 4), ((0, 0), (0, 0), (0, 0), (0, 4)))
    zero = jnp.zeros((128, 8), BF)
    rows = []
    for p in range(2):
        cols = [
            pad_in[a, q - p] if 0 <= q - p <= 2 else zero for a in range(3) for q in range(4)
        ]
        rows.append(jnp.concatenate(cols, 1))
    packed_in = jnp.concatenate(rows, 0)
    pad_out = jnp.pad(w_out.reshape(3, 3, 4, 128), ((0, 0), (0, 0), (0, 4), (0, 0)))
    zero = jnp.zeros((8, 128), BF)
    rows = []
    for a in range(3):
        for p in range(2):
            cols = [q - p for q in (1, 2, 0, 3)]
            rows.append(jnp.concatenate([pad_out[a, b] if 0 <= b <= 2 else zero for b in cols], 1))
    return packed_in, jnp.concatenate(rows, 0)


def prep_call(w_enc, w_down, w_mid, w_dec):
    shapes = ((256, 1536), (256, 1152), (256, 2304), (256, 1536), (256, 1536), (256, 1536))
    return pl.pallas_call(
        prep_kernel,
        out_shape=[jax.ShapeDtypeStruct(s, BF) for s in shapes],
        in_specs=[VMEM] * 4,
        out_specs=[VMEM] * 6,
        compiler_params=PARAMS,
        name="prep",
    )(w_enc, w_down, w_mid, w_dec)


def rowbuf(n):
    return pltpu.VMEM((n, HALF, 256), BF)


def cost(passes):
    return pl.CostEstimate(flops=passes * 128 * 65536 * 2, bytes_accessed=1 << 20, transcendentals=0)


def first_call(width, coef, noise_parts, bias, w_in, w_enc):
    return pl.pallas_call(
        first_kernel,
        out_shape=[
            jax.ShapeDtypeStruct((17 * 8, 256), F32),
            jax.ShapeDtypeStruct((27, HALF, 256), BF),
            jax.ShapeDtypeStruct((27, HALF, 256), BF),
        ],
        in_specs=[SMEM, SMEM] + [VMEM] * 8,
        out_specs=[VMEM] * 3,
        scratch_shapes=[
            pltpu.VMEM((31 * 8, 256), F32), pltpu.VMEM((31 * 8, 512), F32), rowbuf(29), rowbuf(29),
        ],
        compiler_params=PARAMS,
        cost_estimate=cost(200),
        name="first",
    )(width, coef, *noise_parts, bias, w_in, w_enc)


def second_call(width, coef, fields, cond_parts, bias, weights):
    return pl.pallas_call(
        second_kernel,
        out_shape=jax.ShapeDtypeStruct((4, 4, 256), F32),
        in_specs=[SMEM, SMEM] + [VMEM] * 17,
        out_specs=VMEM,
        scratch_shapes=[
            pltpu.VMEM((17 * 8, 256), F32),
            pltpu.VMEM((17 * 8, 512), F32),
            rowbuf(15), rowbuf(15), rowbuf(13), rowbuf(13),
            rowbuf(13), rowbuf(13), rowbuf(13), rowbuf(11), rowbuf(11), rowbuf(11),
            rowbuf(19), rowbuf(19),
            pltpu.VMEM((48, 19 * HALF), F32),
            pltpu.VMEM((2, 17 * 8, HALF), F32),
        ],
        compiler_params=PARAMS,
        cost_estimate=cost(600),
        name="second",
    )(width, coef, *fields, *cond_parts, bias, *weights)


def encode_call(block_anchor, coarse_blocks, w_context):
    chans = w_context.shape[1]
    cells = coarse_blocks.shape[1] // chans
    count = coarse_blocks.shape[0]
    tiles = coarse_blocks.shape[1] // 128
    return pl.pallas_call(
        encode_kernel,
        out_shape=jax.ShapeDtypeStruct((8, 2 * cells, 256), BF),
        in_specs=[SMEM, VMEM, VMEM],
        out_specs=VMEM,
        scratch_shapes=[
            pltpu.VMEM((count, cells, 256), F32),
            pltpu.VMEM((count * tiles + 64, 128), F32),
            pltpu.VMEM((2, 80, 128), F32),
        ],
        compiler_params=PARAMS,
        cost_estimate=cost(100),
        name="encode",
    )(block_anchor, coarse_blocks, w_context.T)


def coefficients(sigmas, w_sigma):
    now = sigmas[:2]
    var = now * now + SIGMA_DATA * SIGMA_DATA
    coef = jnp.stack(
        [
            jnp.broadcast_to(sigmas[0], (2,)),
            1.0 / jnp.sqrt(var),
            SIGMA_DATA * SIGMA_DATA / var,
            now * SIGMA_DATA / jnp.sqrt(var),
            (sigmas[1:] - now) / now,
        ],
        1,
    )
    bias = jnp.log(now)[:, None] * jnp.concatenate([w_sigma, w_sigma])[None, :]
    return coef, bias


def per_device(
    coarse_blocks, block_anchor, nest_width, sigmas, noise,
    w_context, w_in, w_sigma, w_enc, w_down, w_mid, w_dec, w_out,
):
    partial = encode_call(block_anchor, coarse_blocks, w_context)
    arrived = lax.all_to_all(partial, "band", 0, 0, tiled=True)

    held = lax.optimization_barrier((partial, noise, sigmas, w_sigma, w_in, w_out, w_enc, w_down, w_mid, w_dec))
    noise, sigmas, w_sigma, w_in, w_out, w_enc, w_down, w_mid, w_dec = held[1:]
    own = noise[0].transpose(1, 0, 2).reshape(16, 256)
    up3 = turn(own, 3)
    down3 = turn(own, -3)
    coef, bias = coefficients(sigmas, w_sigma)
    packed_in, packed_out = small_weights(w_in, w_out)
    enc, down, mid, dec2, even, odd = prep_call(w_enc, w_down, w_mid, w_dec)
    arrived, own, up3, down3, coef, bias, packed_in, packed_out, enc, down, mid, dec2, even, odd = (
        lax.optimization_barrier(
            (arrived, own, up3, down3, coef, bias, packed_in, packed_out, enc, down, mid, dec2, even, odd)
        )
    )

    cond = (jnp.sum(arrived.astype(F32), axis=0) * (1.0 / math.sqrt(K // 2))).astype(BF)
    noises = jnp.concatenate([up3, own, down3], 0)
    high = lax.reduce_precision(noises, 8, 7)
    parcel = jnp.concatenate([cond, high.astype(BF), (noises - high).astype(BF)], 0)
    near_up = turn(parcel, 1)
    near_down = turn(parcel, -1)
    far_up = turn(jnp.concatenate([near_up[:128], cond], 0), 2)
    far_down = turn(jnp.concatenate([cond, near_down[:128]], 0), -2)

    fields = first_call(nest_width, coef, (own, up3, down3, near_up, near_down), bias, packed_in, enc)
    out = second_call(
        nest_width, coef, fields, (far_up, near_up, near_down, far_down, cond), bias,
        (packed_in, enc, down, mid, dec2, even, odd, packed_out),
    )
    return out[None]


def solution(mesh):
    return jax.shard_map(
        per_device,
        mesh=mesh,
        in_specs=(
            P("band", None), P(), P("band"), P(), P("band", None, "tile", None),
            P(), P(), P(), P(), P(), P(), P(), P(),
        ),
        out_specs=P("band", None, "tile", None),
        check_vma=False,
    )
```

time: 104 us -> 93.6 us (0.90)
  the two profiles are of different devices: /device:TPU:8 before, /device:TPU:2 now
where the time goes in v2:
time: 93.6 us; the launch traced here: 93.2 us
  Pallas kernels  42.2 us (45%)
  starting transfers between devices  37.1 us (40%)
  waiting for transfers between devices  8.8 us (9%)
  local copies, waits for them, and re-layouts  2.53 us (3%)
  other arithmetic  1.54 us (2%)
  between operations  1.02 us (1%)
    ppermute x6, starting transfers between devices, turn(): return lax.ppermute(x, 'tile', [(i, (i + by) % n) for i in range(n)])  27.6 us
    pallas_call x1, Pallas kernels, second_call(): pl.pallas_call(second_kernel, out_shape=jax.ShapeDtypeStruct((4, 4, 256),...  22.3 us
    pallas_call x1, Pallas kernels, first_call(): pl.pallas_call(first_kernel, out_shape=[jax.ShapeDtypeStruct((17 * 8, 256...  9.86 us
    all_to_all x1, starting transfers between devices, per_device(): arrived = lax.all_to_all(partial, 'band', 0, 0, tiled=True)  9.44 us
    ppermute x6, waiting for transfers between devices, turn(): return lax.ppermute(x, 'tile', [(i, (i + by) % n) for i in range(n)])  8.79 us
    pallas_call x1, Pallas kernels, encode_call(): pl.pallas_call(encode_kernel, out_shape=jax.ShapeDtypeStruct((8, 2 * cell...  5.93 us
    pallas_call x1, Pallas kernels, prep_call(): pl.pallas_call(prep_kernel, out_shape=[jax.ShapeDtypeStruct(s, BF) for s...  4.14 us
  transfers between devices with their start and end apart: 7, of which 2 were waited for; matrix products, arithmetic and copies ran while one was open for 3% of the time, Pallas kernels for 15%

profile of v2, /device:TPU:2, one launch (start us, length us, event | category | flops | bytes accessed | tf_op | source)
XLA Modules:
  0.0 93.2 jit_solution(2307404569105425818)
XLA Ops:
  0.0 5.9 %encode.1 = bf16[8,128,256]{2,1,0:T(8,128)(2,1)} custom-call(s32[8,64]{1,0:T(8,128)} %anchor_ref.1, bf16[64,4480]{1,0:T(8,128)(2,1)} %blocks_ref.1, bf16[70,256]{1,0:T(8,128)(2,1)} %bitcast.57), custom_call_target="tpu_custom_call" | custom-call | flops 1677721600 | bytes 1048576 | tf_op jit(solution)/shard_map/encode/pallas_call | solution.py:486
  6.0 9.4 %all-to-all-start = ((bf16[8,128,256]{2,1,0:T(8,128)(2,1)}), bf16[8,128,256]{2,1,0:T(8,128)(2,1)S(1)}, u32[]{:S(2)}, u32[]{:S(2)}) async-start(bf16[8,128,256]{2,1,0:T(8,128)(2,1)} %encode.1), calls=%async_computation | async-start | bytes 1048576 | tf_op jit(solution)/shard_map/all_to_all | solution.py:524
  15.4 0.0 copy-start.1
  15.4 10.9 %collective-permute-start.1 = (f32[16,256]{1,0:T(8,128)S(1)}, f32[16,256]{1,0:T(8,128)S(1)}, u32[]{:S(2)}, u32[]{:S(2)}) collective-permute-start(f32[16,256]{1,0:T(8,128)S(1)} %reshape.11.own), channel_id=1, source_target_pairs={{0,61},{1,62},{2,63},{3,0},{4,1},{5,2},{6,3},{7,4},{8,5},{9,6},{10... | collective-permute-start | bytes 49160 | tf_op jit(solution)/shard_map/ppermute | solution.py:389
  26.4 1.9 %collective-permute-start = (f32[16,256]{1,0:T(8,128)S(1)}, f32[16,256]{1,0:T(8,128)S(1)}, u32[]{:S(2)}, u32[]{:S(2)}) collective-permute-start(f32[16,256]{1,0:T(8,128)S(1)} %reshape.11.own), channel_id=1, source_target_pairs={{0,3},{1,4},{2,5},{3,6},{4,7},{5,8},{6,9},{7,10},{8,11},{9,12},{10... | collective-permute-start | bytes 49160 | tf_op jit(solution)/shard_map/ppermute | solution.py:389
  28.3 0.1 slice_log_fusion
  28.5 0.3 copy.19
  28.7 0.1 slice_bitcast_fusion
  28.9 0.2 concatenate.47
  29.1 0.2 concatenate.46
  29.3 0.6 pad_maximum_fusion.3.w_in
  29.9 0.7 broadcast_multiply_fusion.bias_ref
  30.6 0.1 copy.17
  30.7 0.1 copy.16
  30.7 0.1 copy.18
  30.8 0.1 copy.15
  30.9 4.1 %prep.1 = (bf16[256,1536]{1,0:T(8,128)(2,1)}, bf16[256,1152]{1,0:T(8,128)(2,1)}, bf16[256,2304]{1,0:T(8,128)(2,1)}, bf16[256,1536]{1,0:T(8,128)(2,1)}, bf16[256,...) custom-call(bf16[9,128,128]{2,1,0:T(8,128)(2,1)} %w_enc, bf16[9,256,128]{2,1,0:T(8,128)(2,1)} %w_down, ...), custom_call_target="tpu_custom_call" | custom-call | tf_op jit(solution)/shard_map/prep/pallas_call | solution.py:423
  35.1 0.6 stack.19.coef_ref
  35.7 0.0 collective-permute-done.1.down3
  35.7 1.4 %collective-permute-done.up3 = f32[16,256]{1,0:T(8,128)S(1)} collective-permute-done((f32[16,256]{1,0:T(8,128)S(1)}, f32[16,256]{1,0:T(8,128)S(1)}, u32[]{:S(2)}, u32[]{:S(2)}) %collective-permute-start) | collective-permute-done | bytes 16416 | tf_op jit(solution)/shard_map/ppermute | solution.py:389
  37.1 0.0 all-to-all-done
  37.1 0.1 convert_reduce_fusion
  37.3 6.1 %collective-permute-start.3 = (bf16[224,256]{1,0:T(8,128)(2,1)S(1)}, bf16[224,256]{1,0:T(8,128)(2,1)S(1)}, u32[]{:S(2)}, u32[]{:S(2)}) collective-permute-start(bf16[224,256]{1,0:T(8,128)(2,1)S(1)} %pad_maximum_fusion.2), channel_id=1, source_target_pairs={{0,63},{1,0},{2,1},{3,2},{4,3},{5,4},{6,5},{7,6},{8,7},{9,8},{10,9... | collective-permute-start | bytes 344072 | tf_op jit(solution)/shard_map/ppermute | solution.py:389
  43.5 1.9 %collective-permute-start.2 = (bf16[224,256]{1,0:T(8,128)(2,1)S(1)}, bf16[224,256]{1,0:T(8,128)(2,1)S(1)}, u32[]{:S(2)}, u32[]{:S(2)}) collective-permute-start(bf16[224,256]{1,0:T(8,128)(2,1)S(1)} %pad_maximum_fusion.2), channel_id=1, source_target_pairs={{0,1},{1,2},{2,3},{3,4},{4,5},{5,6},{6,7},{7,8},{8,9},{9,10},{10,1... | collective-permute-start | bytes 344072 | tf_op jit(solution)/shard_map/ppermute | solution.py:389
  46.1 7.4 %collective-permute-done.2.near_up = bf16[224,256]{1,0:T(8,128)(2,1)S(1)} collective-permute-done((bf16[224,256]{1,0:T(8,128)(2,1)S(1)}, bf16[224,256]{1,0:T(8,128)(2,1)S(1)}, u32[]{:S(2)}, u32[]{:S(2)}) %collective-permute-start.2) | collective-permute-done | bytes 114720 | tf_op jit(solution)/shard_map/ppermute | solution.py:389
  53.5 1.9 %collective-permute-start.5 = (bf16[256,256]{1,0:T(8,128)(2,1)S(1)}, bf16[256,256]{1,0:T(8,128)(2,1)S(1)}, u32[]{:S(2)}, u32[]{:S(2)}) collective-permute-start(bf16[256,256]{1,0:T(8,128)(2,1)S(1)} %get-tuple-element.78), channel_id=1, source_target_pairs={{0,62},{1,63},{2,0},{3,1},{4,2},{5,3},{6,4},{7,5},{8,6},{9,7},{10,... | collective-permute-start | bytes 393224 | tf_op jit(solution)/shard_map/ppermute | solution.py:389
  55.4 4.8 %collective-permute-start.4 = (bf16[256,256]{1,0:T(8,128)(2,1)S(1)}, bf16[256,256]{1,0:T(8,128)(2,1)S(1)}, u32[]{:S(2)}, u32[]{:S(2)}) collective-permute-start(bf16[256,256]{1,0:T(8,128)(2,1)S(1)} %get-tuple-element.79), channel_id=1, source_target_pairs={{0,2},{1,3},{2,4},{3,5},{4,6},{5,7},{6,8},{7,9},{8,10},{9,11},{10,... | collective-permute-start | bytes 393224 | tf_op jit(solution)/shard_map/ppermute | solution.py:389
  60.3 9.9 %first.1 = (f32[136,256]{1,0:T(8,128)}, bf16[27,128,256]{2,1,0:T(8,128)(2,1)}, bf16[27,128,256]{2,1,0:T(8,128)(2,1)}) custom-call(s32[1]{0:T(128)S(6)} %copy.27.width_ref, f32[2,5]{1,0:T(2,128)} %stack.19.coef_ref, f32[16,256]{1,0:T(8,128)} %copy-done.1, f32[16,256]{1,0:T(8,128)} %copy-done.6, f32[16,256]{1,0:T(8,128)} %copy-done.5, ...), custom_call_target="tpu_custom_call" | custom-call | flops 3355443200 | bytes 1048576 | tf_op jit(solution)/shard_map/first/pallas_call | solution.py:442
  70.2 0.0 collective-permute-done.5.far_down
  70.2 0.6 copy-done.11
  70.8 0.1 copy-done.12
  70.9 22.3 %second.1 = f32[4,4,256]{2,1,0:T(4,128)} custom-call(s32[1]{0:T(128)S(6)} %copy.27.width_ref, f32[2,5]{1,0:T(2,128)} %stack.19.coef_ref, f32[136,256]{1,0:T(8,128)} %get-tuple-element.60.state_in, bf16[27,128,256]{2,1,0:T(8,128)(2,1)} %get-tuple-element.61.secondc0, bf16[27,128,256]{2,1,0:T(8,128)(2,1)} %get-tuple-element.62.seconde0, ...), custom_call_target="tpu_custom_call" | custom-call | flops 10066329600 | bytes 1048576 | tf_op jit(solution)/shard_map/second/pallas_call | solution.py:461
  (49 shorter events, 0.2 us)
Async XLA Ops:
  0.0 15.4 %copy-start.4 = (f32[1,4,4,256]{3,2,1,0:T(4,128)S(1)}, f32[1,4,4,256]{3,2,1,0:T(4,128)}, u32[]{:S(2)}) copy-start(f32[1,4,4,256]{3,2,1,0:T(4,128)} %param.17) | copy-start | bytes 49156
  0.0 28.3 %copy-start.9 = (f32[3]{0:T(128)S(1)}, f32[3]{0:T(128)}, u32[]{:S(2)}) copy-start(f32[3]{0:T(128)} %param.16) | copy-start | bytes 40
  0.0 28.4 %copy-start.8 = (bf16[9,4,128]{2,1,0:T(4,128)(2,1)S(1)}, bf16[9,4,128]{2,1,0:T(4,128)(2,1)}, u32[]{:S(2)}) copy-start(bf16[9,4,128]{2,1,0:T(4,128)(2,1)} %param.25) | copy-start | bytes 27652
  0.0 28.5 %copy-start.7 = (bf16[9,128,4]{1,2,0:T(4,128)(2,1)S(1)}, bf16[9,128,4]{1,2,0:T(4,128)(2,1)}, u32[]{:S(2)}) copy-start(bf16[9,128,4]{1,2,0:T(4,128)(2,1)} %param.19) | copy-start | bytes 27652
  5.9 22.9 %copy-start.13 = (f32[128]{0:T(128)S(1)}, f32[128]{0:T(128)}, u32[]{:S(2)}) copy-start(f32[128]{0:T(128)} %param.20) | copy-start | bytes 1540
  6.0 31.2 %all-to-all-start = ((bf16[8,128,256]{2,1,0:T(8,128)(2,1)}), bf16[8,128,256]{2,1,0:T(8,128)(2,1)S(1)}, u32[]{:S(2)}, u32[]{:S(2)}) async-start(bf16[8,128,256]{2,1,0:T(8,128)(2,1)} %encode.1), calls=%async_computation | async-start | bytes 1048576 | tf_op jit(solution)/shard_map/all_to_all | solution.py:524
  15.4 21.8 %copy-start.1 = (f32[16,256]{1,0:T(8,128)}, f32[16,256]{1,0:T(8,128)S(1)}, u32[]{:S(2)}) copy-start(f32[16,256]{1,0:T(8,128)S(1)} %reshape.11.own) | copy-start | bytes 49156
  15.4 20.3 %collective-permute-start.1 = (f32[16,256]{1,0:T(8,128)S(1)}, f32[16,256]{1,0:T(8,128)S(1)}, u32[]{:S(2)}, u32[]{:S(2)}) collective-permute-start(f32[16,256]{1,0:T(8,128)S(1)} %reshape.11.own), channel_id=1, source_target_pairs={{0,61},{1,62},{2,63},{3,0},{4,1},{5,2},{6,3},{7,4},{8,5},{9,6},{10... | collective-permute-start | bytes 49160 | tf_op jit(solution)/shard_map/ppermute | solution.py:389
  26.4 10.8 %collective-permute-start = (f32[16,256]{1,0:T(8,128)S(1)}, f32[16,256]{1,0:T(8,128)S(1)}, u32[]{:S(2)}, u32[]{:S(2)}) collective-permute-start(f32[16,256]{1,0:T(8,128)S(1)} %reshape.11.own), channel_id=1, source_target_pairs={{0,3},{1,4},{2,5},{3,6},{4,7},{5,8},{6,9},{7,10},{8,11},{9,12},{10... | collective-permute-start | bytes 49160 | tf_op jit(solution)/shard_map/ppermute | solution.py:389
  30.6 6.7 %copy-start.10 = (bf16[48,512]{1,0:T(8,128)(2,1)}, bf16[48,512]{1,0:T(8,128)(2,1)S(1)}, u32[]{:S(2)}) copy-start(bf16[48,512]{1,0:T(8,128)(2,1)S(1)} %constant_dynamic-update-slice_fusion.w_out) | copy-start | bytes 147460
  35.7 24.5 %copy-start.5 = (f32[16,256]{1,0:T(8,128)}, f32[16,256]{1,0:T(8,128)S(1)}, u32[]{:S(2)}) copy-start(f32[16,256]{1,0:T(8,128)S(1)} %collective-permute-done.1.down3) | copy-start | bytes 49156
  37.1 23.1 %copy-start.6 = (f32[16,256]{1,0:T(8,128)}, f32[16,256]{1,0:T(8,128)S(1)}, u32[]{:S(2)}) copy-start(f32[16,256]{1,0:T(8,128)S(1)} %collective-permute-done.up3) | copy-start | bytes 49156
  37.2 32.9 %copy-start = (bf16[128,256]{1,0:T(8,128)(2,1)}, bf16[128,256]{1,0:T(8,128)(2,1)S(1)}, u32[]{:S(2)}) copy-start(bf16[128,256]{1,0:T(8,128)(2,1)S(1)} %multiply_convert_fusion.own_cond) | copy-start | bytes 196612
  37.3 8.7 %collective-permute-start.3 = (bf16[224,256]{1,0:T(8,128)(2,1)S(1)}, bf16[224,256]{1,0:T(8,128)(2,1)S(1)}, u32[]{:S(2)}, u32[]{:S(2)}) collective-permute-start(bf16[224,256]{1,0:T(8,128)(2,1)S(1)} %pad_maximum_fusion.2), channel_id=1, source_target_pairs={{0,63},{1,0},{2,1},{3,2},{4,3},{5,4},{6,5},{7,6},{8,7},{9,8},{10,9... | collective-permute-start | bytes 344072 | tf_op jit(solution)/shard_map/ppermute | solution.py:389
  43.5 10.0 %collective-permute-start.2 = (bf16[224,256]{1,0:T(8,128)(2,1)S(1)}, bf16[224,256]{1,0:T(8,128)(2,1)S(1)}, u32[]{:S(2)}, u32[]{:S(2)}) collective-permute-start(bf16[224,256]{1,0:T(8,128)(2,1)S(1)} %pad_maximum_fusion.2), channel_id=1, source_target_pairs={{0,1},{1,2},{2,3},{3,4},{4,5},{5,6},{6,7},{7,8},{8,9},{9,10},{10,1... | collective-permute-start | bytes 344072 | tf_op jit(solution)/shard_map/ppermute | solution.py:389
  46.0 14.2 %copy-start.2 = (bf16[224,256]{1,0:T(8,128)(2,1)}, bf16[224,256]{1,0:T(8,128)(2,1)S(1)}, u32[]{:S(2)}) copy-start(bf16[224,256]{1,0:T(8,128)(2,1)S(1)} %collective-permute-done.3.near_down) | copy-start | bytes 344068
  53.5 6.8 %copy-start.3 = (bf16[224,256]{1,0:T(8,128)(2,1)}, bf16[224,256]{1,0:T(8,128)(2,1)S(1)}, u32[]{:S(2)}) copy-start(bf16[224,256]{1,0:T(8,128)(2,1)S(1)} %collective-permute-done.2.near_up) | copy-start | bytes 344068
  53.5 16.7 %collective-permute-start.5 = (bf16[256,256]{1,0:T(8,128)(2,1)S(1)}, bf16[256,256]{1,0:T(8,128)(2,1)S(1)}, u32[]{:S(2)}, u32[]{:S(2)}) collective-permute-start(bf16[256,256]{1,0:T(8,128)(2,1)S(1)} %get-tuple-element.78), channel_id=1, source_target_pairs={{0,62},{1,63},{2,0},{3,1},{4,2},{5,3},{6,4},{7,5},{8,6},{9,7},{10,... | collective-permute-start | bytes 393224 | tf_op jit(solution)/shard_map/ppermute | solution.py:389
  55.4 14.8 %collective-permute-start.4 = (bf16[256,256]{1,0:T(8,128)(2,1)S(1)}, bf16[256,256]{1,0:T(8,128)(2,1)S(1)}, u32[]{:S(2)}, u32[]{:S(2)}) collective-permute-start(bf16[256,256]{1,0:T(8,128)(2,1)S(1)} %get-tuple-element.79), channel_id=1, source_target_pairs={{0,2},{1,3},{2,4},{3,5},{4,6},{5,7},{6,8},{7,9},{8,10},{9,11},{10,... | collective-permute-start | bytes 393224 | tf_op jit(solution)/shard_map/ppermute | solution.py:389
  70.2 0.7 copy-start.11
  70.2 0.7 copy-start.12

commit v3 on v2

--- a/solution.py
+++ b/solution.py
@@ -15,7 +15,7 @@
 HALF = 128
 ROWS = 256
 NT = (((1,), (1,)), ((), ()))
-TN = (((0,), (1,)), ((), ()))
+TN = (((0,), (0,)), ((), ()))
 
 STEP_ROWS = (
     dict(scaled=(-15, 31), first=(-14, 29), second=(-13, 27), third=(-6, 13), fourth=(-5, 11), fifth=(-8, 19), out=(-7, 17)),
@@ -35,7 +35,8 @@
 def encode_kernel(anchor_ref, blocks_ref, w_ref, out_ref, enc_ref, flat, wide):
     band = lax.axis_index("band")
     tile = lax.axis_index("tile")
-    count, cells = enc_ref.shape[:2]
+    count = blocks_ref.shape[0]
+    cells = enc_ref.shape[1]
     chans = w_ref.shape[0]
     tiles = blocks_ref.shape[1] // 128
     group = 8 * tiles
@@ -70,26 +71,29 @@
             odd = jnp.where(first, pltpu.roll(one, 64, 1), two)
             cols.append(jnp.concatenate([even, odd], 0))
         x = jnp.concatenate(cols, 1).astype(BF)
-        v = lax.dot_general(x, weight, (((0,), (0,)), ((), ())), preferred_element_type=F32)
+        v = lax.dot_general(x, weight, TN, preferred_element_type=F32)
         v = silu(v).astype(BF).astype(F32)
         enc_ref[pl.ds(g * 8, 8)] = v.reshape(8, cells, 256)
         return carry
 
     lax.fori_loop(0, count // 8, encode, 0)
 
+    enc_ref[pl.ds(count, 8)] = enc_ref[pl.ds(0, 8)]
+
     def window(k, carry):
-        nest = k // 2
-        part = k % 2
-        anchor = anchor_ref[nest, tile]
-        begin = anchor + (band - anchor + 512) % 8 + part * 48
+        nest = k // 6
+        part = k % 6
+        at = jnp.clip(tile + part // 2 - 1, 0, anchor_ref.shape[1] - 1)
+        anchor = anchor_ref[nest, at]
+        begin = anchor + (band - anchor + 512) % 8 + (part % 2) * 48
         row = (begin % 512) // 8
         total = enc_ref[row]
         for m in range(1, 6):
-            total = total + enc_ref[(row + m) % count]
+            total = total + enc_ref[row + m]
         out_ref[nest, pl.ds(pl.multiple_of(part * cells, cells), cells), :] = total.astype(BF)
         return carry
 
-    lax.fori_loop(0, 16, window, 0)
+    lax.fori_loop(0, 48, window, 0, unroll=4)
 
 
 def pair_weight(w, a):
@@ -103,7 +107,30 @@
     return own, rim
 
 
-def prep_kernel(w_enc, w_down, w_mid, w_dec, enc_o, down_o, mid_o, dec2_o, even_o, odd_o):
+def prep_kernel(
+    w_in, w_enc, w_down, w_mid, w_dec, w_out, in_o, enc_o, down_o, mid_o, dec2_o, even_o, odd_o, out_o
+):
+    def tall(ref, a, b):
+        if not 0 <= b <= 2:
+            return jnp.zeros((8, 128), F32)
+        return jnp.concatenate([ref[3 * a + b].astype(F32), jnp.zeros((4, 128), F32)], 0)
+
+    in_o[...] = jnp.concatenate(
+        [
+            jnp.concatenate([tall(w_in, a, q - p) for p in range(2)], 1)
+            for a in range(3)
+            for q in range(4)
+        ],
+        0,
+    ).astype(BF)
+    out_o[...] = jnp.concatenate(
+        [
+            jnp.concatenate([tall(w_out, a, q - p) for q in (1, 2, 0, 3)], 1)
+            for a in range(3)
+            for p in range(2)
+        ],
+        0,
+    ).astype(BF)
     for a in range(3):
         own, rim = pair_weight(lambda i, b: w_enc[3 * i + b], a)
         enc_o[:, 512 * a : 512 * a + 256] = own
@@ -171,6 +198,18 @@
             right[at + k] = sides[1][cut]
 
 
+def levels(sigma_ref, step):
+    now = jnp.full((1, 256), sigma_ref[step], F32)
+    after = jnp.full((1, 256), sigma_ref[step + 1], F32)
+    var = now * now + SIGMA_DATA * SIGMA_DATA
+    root = jnp.sqrt(var)
+    return now, 1.0 / root, SIGMA_DATA * SIGMA_DATA / var, now * SIGMA_DATA / root, (after - now) / now
+
+
+def embedding(w_sigma, now):
+    return jnp.concatenate([w_sigma[...], w_sigma[...]], 1) * jnp.log(now)
+
+
 def slide(x, by):
     rows = x.shape[0]
     edge = 0 if by == 1 else HALF - 1
@@ -229,40 +268,35 @@
 
 
 def first_kernel(
-    width_ref, coef_ref, own, up3, down3, near_up, near_down, bias_ref, w_in, w_enc,
+    width_ref, sigma_ref, own, up3, down3, near_up, near_down, w_sigma, w_in, w_enc,
     state_ref, secondc, seconde,
     state, spread, firstc, firste,
 ):
     field = Field(width_ref[0])
     rows = STEP_ROWS[0]
-    start = coef_ref[0, 0]
+    now, scale = levels(sigma_ref, 0)[:2]
     empty = jnp.zeros((4, 256), F32)
-    pieces = {-3: up3, 0: own, 3: down3}
+    pieces = {-3: (up3, 0), 0: (own, 0), 3: (down3, 0)}
+    for slot in range(3):
+        pieces[3 * slot - 4] = (near_up, 16 * slot)
+        pieces[3 * slot - 2] = (near_down, 16 * slot)
     for tile_off in range(-4, 4):
-        if tile_off in pieces:
-            value = pieces[tile_off][...]
-        else:
-            ref = near_up if (tile_off + 1) % 3 == 0 else near_down
-            slot = (tile_off + (1 if ref is near_up else -1)) // 3 + 1
-            begin = 128 + 16 * slot
-            value = ref[begin : begin + 16, :].astype(F32) + ref[begin + 48 : begin + 64, :].astype(F32)
+        ref, begin = pieces[tile_off]
         for r in range(4):
             rho = 4 * tile_off + r
             if rho >= -15:
-                row = jnp.concatenate([value[4 * r : 4 * r + 4], empty], 0)
-                state[8 * (rho + 15) : 8 * (rho + 16), :] = start * row * (field.natural * field.fine_ok(rho))
+                row = jnp.concatenate([ref[begin + 4 * r : begin + 4 * r + 4, :], empty], 0)
+                state[8 * (rho + 15) : 8 * (rho + 16), :] = now * row * (field.natural * field.fine_ok(rho))
     out_lo, n_out = rows["out"]
     state_ref[...] = state[8 * (out_lo + 15) : 8 * (out_lo + 15 + n_out), :]
     encoder(
-        field, rows, state, coef_ref[0, 1], bias_ref[0:1, :], w_in, w_enc,
+        field, rows, state, scale, embedding(w_sigma, now), w_in, w_enc,
         spread, firstc, firste, secondc, seconde, 9,
     )
 
 
 def second_kernel(
-    width_ref, coef_ref, state_in, secondc0, seconde0,
-    far_up, near_up, near_down, far_down, own_cond,
-    bias_ref, w_in, w_enc, w_down, w_mid, w_dec2, w_even, w_odd, w_out,
+    width_ref, sigma_ref, state_in, secondc0, seconde0, far_up, near, far_down, w_sigma, w_in, w_enc, w_down, w_mid, w_dec2, w_even, w_odd, w_out,
     out_ref,
     state, spread, firstc, firste, secondc1, seconde1, third, thirdl, thirdr, fourth, fourthl, fourthr,
     fifthc, fifthe, prod, picked,
@@ -274,21 +308,17 @@
     repeat = (
         lax.broadcasted_iota(jnp.int32, (HALF, 64), 0) // 2 == lax.broadcasted_iota(jnp.int32, (HALF, 64), 1)
     ).astype(F32).astype(BF)
-    conds = (
-        (far_up, 0), (far_up, 1), (far_up, 2), (far_up, 3),
-        (near_up, 0), (near_up, 1), (own_cond, 0), (own_cond, 1), (near_down, 0), (near_down, 1),
-        (far_down, 0), (far_down, 1), (far_down, 2), (far_down, 3),
-    )
+    conds = [(ref, r) for ref, n in ((far_up, 4), (near, 6), (far_down, 4)) for r in range(n)]
 
     for step in range(2):
         rows = STEP_ROWS[step]
-        scale, keep, mix, move = (coef_ref[step, 1 + i] for i in range(4))
+        sigma, scale, keep, mix, move = levels(sigma_ref, step)
         if step == 0:
             secondc, seconde = secondc0, seconde0
         else:
             secondc, seconde = secondc1, seconde1
             encoder(
-                field, rows, state, scale, bias_ref[1:2, :], w_in, w_enc,
+                field, rows, state, scale, embedding(w_sigma, sigma), w_in, w_enc,
                 spread, firstc, firste, secondc, seconde, 13,
             )
 
@@ -391,43 +421,23 @@
 
 VMEM = pl.BlockSpec(memory_space=pltpu.VMEM)
 SMEM = pl.BlockSpec(memory_space=pltpu.SMEM)
-PARAMS = pltpu.CompilerParams(vmem_limit_bytes=56 << 20)
-
-
-def pair_map(count):
-    return [[q - p if 0 <= q - p <= 2 else None for q in range(count)] for p in range(2)]
-
-
-def small_weights(w_in, w_out):
-    pad_in = jnp.pad(w_in.reshape(3, 3, 128, 4), ((0, 0), (0, 0), (0, 0), (0, 4)))
-    zero = jnp.zeros((128, 8), BF)
-    rows = []
-    for p in range(2):
-        cols = [
-            pad_in[a, q - p] if 0 <= q - p <= 2 else zero for a in range(3) for q in range(4)
-        ]
-        rows.append(jnp.concatenate(cols, 1))
-    packed_in = jnp.concatenate(rows, 0)
-    pad_out = jnp.pad(w_out.reshape(3, 3, 4, 128), ((0, 0), (0, 0), (0, 4), (0, 0)))
-    zero = jnp.zeros((8, 128), BF)
-    rows = []
-    for a in range(3):
-        for p in range(2):
-            cols = [q - p for q in (1, 2, 0, 3)]
-            rows.append(jnp.concatenate([pad_out[a, b] if 0 <= b <= 2 else zero for b in cols], 1))
-    return packed_in, jnp.concatenate(rows, 0)
-
-
-def prep_call(w_enc, w_down, w_mid, w_dec):
-    shapes = ((256, 1536), (256, 1152), (256, 2304), (256, 1536), (256, 1536), (256, 1536))
+
+
+def limit(mib):
+    return pltpu.CompilerParams(vmem_limit_bytes=mib << 20)
+
+
+def prep_call(w_in, w_enc, w_down, w_mid, w_dec, w_out):
+    shapes = ((96, 256), (256, 1536), (256, 1152), (256, 2304), (256, 1536), (256, 1536), (256, 1536), (48, 512))
     return pl.pallas_call(
         prep_kernel,
         out_shape=[jax.ShapeDtypeStruct(s, BF) for s in shapes],
-        in_specs=[VMEM] * 4,
-        out_specs=[VMEM] * 6,
-        compiler_params=PARAMS,
+        in_specs=[VMEM] * 6,
+        out_specs=[VMEM] * 8,
+        compiler_params=limit(12),
+        cost_estimate=cost(20),
         name="prep",
-    )(w_enc, w_down, w_mid, w_dec)
+    )(w_in.transpose(0, 2, 1), w_enc, w_down, w_mid, w_dec, w_out)
 
 
 def rowbuf(n):
@@ -438,7 +448,7 @@
     return pl.CostEstimate(flops=passes * 128 * 65536 * 2, bytes_accessed=1 << 20, transcendentals=0)
 
 
-def first_call(width, coef, noise_parts, bias, w_in, w_enc):
+def first_call(width, sigmas, noise_parts, w_sigma, w_in, w_enc):
     return pl.pallas_call(
         first_kernel,
         out_shape=[
@@ -451,17 +461,17 @@
         scratch_shapes=[
             pltpu.VMEM((31 * 8, 256), F32), pltpu.VMEM((31 * 8, 512), F32), rowbuf(29), rowbuf(29),
         ],
-        compiler_params=PARAMS,
+        compiler_params=limit(16),
         cost_estimate=cost(200),
         name="first",
-    )(width, coef, *noise_parts, bias, w_in, w_enc)
-
-
-def second_call(width, coef, fields, cond_parts, bias, weights):
+    )(width, sigmas, *noise_parts, w_sigma, w_in, w_enc)
+
+
+def second_call(width, sigmas, fields, conds, w_sigma, weights):
     return pl.pallas_call(
         second_kernel,
         out_shape=jax.ShapeDtypeStruct((4, 4, 256), F32),
-        in_specs=[SMEM, SMEM] + [VMEM] * 17,
+        in_specs=[SMEM, SMEM] + [VMEM] * 15,
         out_specs=VMEM,
         scratch_shapes=[
             pltpu.VMEM((17 * 8, 256), F32),
@@ -472,10 +482,10 @@
             pltpu.VMEM((48, 19 * HALF), F32),
             pltpu.VMEM((2, 17 * 8, HALF), F32),
         ],
-        compiler_params=PARAMS,
+        compiler_params=limit(28),
         cost_estimate=cost(600),
         name="second",
-    )(width, coef, *fields, *cond_parts, bias, *weights)
+    )(width, sigmas, *fields, *conds, w_sigma, *weights)
 
 
 def encode_call(block_anchor, coarse_blocks, w_context):
@@ -485,35 +495,18 @@
     tiles = coarse_blocks.shape[1] // 128
     return pl.pallas_call(
         encode_kernel,
-        out_shape=jax.ShapeDtypeStruct((8, 2 * cells, 256), BF),
+        out_shape=jax.ShapeDtypeStruct((8, 6 * cells, 256), BF),
         in_specs=[SMEM, VMEM, VMEM],
         out_specs=VMEM,
         scratch_shapes=[
-            pltpu.VMEM((count, cells, 256), F32),
+            pltpu.VMEM((count + 8, cells, 256), F32),
             pltpu.VMEM((count * tiles + 64, 128), F32),
             pltpu.VMEM((2, 80, 128), F32),
         ],
-        compiler_params=PARAMS,
+        compiler_params=limit(16),
         cost_estimate=cost(100),
         name="encode",
     )(block_anchor, coarse_blocks, w_context.T)
-
-
-def coefficients(sigmas, w_sigma):
-    now = sigmas[:2]
-    var = now * now + SIGMA_DATA * SIGMA_DATA
-    coef = jnp.stack(
-        [
-            jnp.broadcast_to(sigmas[0], (2,)),
-            1.0 / jnp.sqrt(var),
-            SIGMA_DATA * SIGMA_DATA / var,
-            now * SIGMA_DATA / jnp.sqrt(var),
-            (sigmas[1:] - now) / now,
-        ],
-        1,
-    )
-    bias = jnp.log(now)[:, None] * jnp.concatenate([w_sigma, w_sigma])[None, :]
-    return coef, bias
 
 
 def per_device(
@@ -523,33 +516,24 @@
     partial = encode_call(block_anchor, coarse_blocks, w_context)
     arrived = lax.all_to_all(partial, "band", 0, 0, tiled=True)
 
-    held = lax.optimization_barrier((partial, noise, sigmas, w_sigma, w_in, w_out, w_enc, w_down, w_mid, w_dec))
-    noise, sigmas, w_sigma, w_in, w_out, w_enc, w_down, w_mid, w_dec = held[1:]
+    held = lax.optimization_barrier((partial, noise, w_in, w_enc, w_down, w_mid, w_dec, w_out))
+    noise = held[1]
     own = noise[0].transpose(1, 0, 2).reshape(16, 256)
     up3 = turn(own, 3)
     down3 = turn(own, -3)
-    coef, bias = coefficients(sigmas, w_sigma)
-    packed_in, packed_out = small_weights(w_in, w_out)
-    enc, down, mid, dec2, even, odd = prep_call(w_enc, w_down, w_mid, w_dec)
-    arrived, own, up3, down3, coef, bias, packed_in, packed_out, enc, down, mid, dec2, even, odd = (
-        lax.optimization_barrier(
-            (arrived, own, up3, down3, coef, bias, packed_in, packed_out, enc, down, mid, dec2, even, odd)
-        )
-    )
-
-    cond = (jnp.sum(arrived.astype(F32), axis=0) * (1.0 / math.sqrt(K // 2))).astype(BF)
-    noises = jnp.concatenate([up3, own, down3], 0)
-    high = lax.reduce_precision(noises, 8, 7)
-    parcel = jnp.concatenate([cond, high.astype(BF), (noises - high).astype(BF)], 0)
-    near_up = turn(parcel, 1)
-    near_down = turn(parcel, -1)
-    far_up = turn(jnp.concatenate([near_up[:128], cond], 0), 2)
-    far_down = turn(jnp.concatenate([cond, near_down[:128]], 0), -2)
-
-    fields = first_call(nest_width, coef, (own, up3, down3, near_up, near_down), bias, packed_in, enc)
+    three = jnp.concatenate([up3, own, down3], 0)
+    near_up = turn(three, 1)
+    near_down = turn(three, -1)
+    packed_in, enc, *rest = prep_call(*held[2:])
+    w_sigma = w_sigma.reshape(1, -1)
+    fields = first_call(nest_width, sigmas, (own, up3, down3, near_up, near_down), w_sigma, packed_in, enc)
+    arrived, fields, rest = lax.optimization_barrier((arrived, fields, rest))
+
+    near = (jnp.sum(arrived.astype(F32), axis=0) * (1.0 / math.sqrt(K // 2))).astype(BF)
+    far_up = turn(near[:256], 2)
+    far_down = turn(near[128:], -2)
     out = second_call(
-        nest_width, coef, fields, (far_up, near_up, near_down, far_down, cond), bias,
-        (packed_in, enc, down, mid, dec2, even, odd, packed_out),
+        nest_width, sigmas, fields, (far_up, near, far_down), w_sigma, (packed_in, enc, *rest)
     )
     return out[None]
 

time: 93.6 us -> 106 us (1.13)
  the two profiles are of different devices: /device:TPU:2 before, /device:TPU:10 now
where the time goes in v3:
time: 106 us; the launch traced here: 105 us
  starting transfers between devices  40.6 us (38%)
  Pallas kernels  33.5 us (32%)
  local copies, waits for them, and re-layouts  17.2 us (16%)
  waiting for transfers between devices  11.3 us (11%)
  other arithmetic  1.84 us (2%)
    ppermute x6, starting transfers between devices, turn(): return lax.ppermute(x, 'tile', [(i, (i + by) % n) for i in range(n)])  35.5 us
    pallas_call x1, Pallas kernels, second_call(): pl.pallas_call(second_kernel, out_shape=jax.ShapeDtypeStruct((4, 4, 256),...  19 us
    unnamed x70, local copies, waits for them, and re-layouts  17.1 us
    ppermute x6, waiting for transfers between devices, turn(): return lax.ppermute(x, 'tile', [(i, (i + by) % n) for i in range(n)])  11.3 us
    pallas_call x1, Pallas kernels, first_call(): pl.pallas_call(first_kernel, out_shape=[jax.ShapeDtypeStruct((17 * 8, 256...  7.27 us
    pallas_call x1, Pallas kernels, encode_call(): pl.pallas_call(encode_kernel, out_shape=jax.ShapeDtypeStruct((8, 6 * cell...  6.73 us
    all_to_all x1, starting transfers between devices, per_device(): arrived = lax.all_to_all(partial, 'band', 0, 0, tiled=True)  5.1 us
  transfers between devices with their start and end apart: 7, of which 4 were waited for; matrix products, arithmetic and copies ran while one was open for 0% of the time, Pallas kernels for 7%

profile of v3, /device:TPU:10, one launch (start us, length us, event | category | flops | bytes accessed | tf_op | source)
XLA Modules:
  0.0 105.3 jit_solution(18107034726451397789)
XLA Ops:
  0.0 1.1 %copy-done.18 = bf16[64,4480]{1,0:T(8,128)(2,1)S(1)} copy-done((bf16[64,4480]{1,0:T(8,128)(2,1)S(1)}, bf16[64,4480]{1,0:T(8,128)(2,1)}, u32[]{:S(2)}) %copy-start.18) | copy-done | bytes 573464
  1.1 0.8 copy-done.23
  1.8 0.7 copy-done.24
  2.5 6.7 %encode.1 = bf16[8,384,256]{2,1,0:T(8,128)(2,1)} custom-call(s32[8,64]{1,0:T(8,128)S(1)} %copy-done.24, bf16[64,4480]{1,0:T(8,128)(2,1)S(1)} %copy-done.18, bf16[70,256]{1,0:T(8,128)(2,1)S(1)} %bitcast.8), custom_call_target="tpu_custom_call" | custom-call | flops 1677721600 | bytes 1048576 | tf_op jit(solution)/shard_map/encode/pallas_call | solution.py:496
  9.3 5.1 %all-to-all-start = ((bf16[8,384,256]{2,1,0:T(8,128)(2,1)}), bf16[8,384,256]{2,1,0:T(8,128)(2,1)}, u32[]{:S(2)}, u32[]{:S(2)}) async-start(bf16[8,384,256]{2,1,0:T(8,128)(2,1)} %encode.1), calls=%async_computation | async-start | bytes 3145728 | tf_op jit(solution)/shard_map/all_to_all | solution.py:517
  14.4 6.7 %collective-permute-start = (f32[16,256]{1,0:T(8,128)S(1)}, f32[16,256]{1,0:T(8,128)S(1)}, u32[]{:S(2)}, u32[]{:S(2)}) collective-permute-start(f32[16,256]{1,0:T(8,128)S(1)} %reshape.6.own), channel_id=1, source_target_pairs={{0,3},{1,4},{2,5},{3,6},{4,7},{5,8},{6,9},{7,10},{8,11},{9,12},{10... | collective-permute-start | bytes 49160 | tf_op jit(solution)/shard_map/ppermute | solution.py:419
  21.2 9.7 %collective-permute-start.1 = (f32[16,256]{1,0:T(8,128)S(1)}, f32[16,256]{1,0:T(8,128)S(1)}, u32[]{:S(2)}, u32[]{:S(2)}) collective-permute-start(f32[16,256]{1,0:T(8,128)S(1)} %reshape.6.own), channel_id=1, source_target_pairs={{0,61},{1,62},{2,63},{3,0},{4,1},{5,2},{6,3},{7,4},{8,5},{9,6},{10... | collective-permute-start | bytes 49160 | tf_op jit(solution)/shard_map/ppermute | solution.py:419
  30.9 1.4 %collective-permute-done.1.down3 = f32[16,256]{1,0:T(8,128)S(1)} collective-permute-done((f32[16,256]{1,0:T(8,128)S(1)}, f32[16,256]{1,0:T(8,128)S(1)}, u32[]{:S(2)}, u32[]{:S(2)}) %collective-permute-start.1) | collective-permute-done | bytes 16416 | tf_op jit(solution)/shard_map/ppermute | solution.py:419
  32.3 3.2 %collective-permute-start.3 = (f32[48,256]{1,0:T(8,128)S(1)}, f32[48,256]{1,0:T(8,128)S(1)}, u32[]{:S(2)}, u32[]{:S(2)}) collective-permute-start(f32[48,256]{1,0:T(8,128)S(1)} %constant_dynamic-update-slice_fusion), channel_id=1, source_target_pairs={{0,63},{1,0},{2,1},{3,2},{4,3},{5,4},{6,5},{7,6},{8,7},{9,8},{10,9... | collective-permute-start | bytes 147464 | tf_op jit(solution)/shard_map/ppermute | solution.py:419
  35.6 2.6 %collective-permute-start.2 = (f32[48,256]{1,0:T(8,128)S(1)}, f32[48,256]{1,0:T(8,128)S(1)}, u32[]{:S(2)}, u32[]{:S(2)}) collective-permute-start(f32[48,256]{1,0:T(8,128)S(1)} %constant_dynamic-update-slice_fusion), channel_id=1, source_target_pairs={{0,1},{1,2},{2,3},{3,4},{4,5},{5,6},{6,7},{7,8},{8,9},{9,10},{10,1... | collective-permute-start | bytes 147464 | tf_op jit(solution)/shard_map/ppermute | solution.py:419
  39.4 1.1 copy-done.6
  40.4 0.9 copy-done.10
  41.3 0.9 copy-done.12
  42.2 0.9 copy-done.14
  43.2 0.8 copy-done.16
  44.0 0.6 copy-done.21
  44.6 0.8 collective-permute-done.2.near_up
  45.4 0.7 copy-done.25
  46.1 0.7 copy-done.27
  46.8 7.3 %first.1 = (f32[136,256]{1,0:T(8,128)S(1)}, bf16[27,128,256]{2,1,0:T(8,128)(2,1)S(1)}, bf16[27,128,256]{2,1,0:T(8,128)(2,1)S(1)}) custom-call(s32[1]{0:T(128)S(6)} %copy.17.width_ref, f32[3]{0:T(128)S(1)} %copy-done.25, f32[16,256]{1,0:T(8,128)S(1)} %reshape.6.own, f32[16,256]{1,0:T(8,128)S(1)} %collective-permute-done.up3, ...), custom_call_target="tpu_custom_call" | custom-call | flops 3355443200 | bytes 1048576 | tf_op jit(solution)/shard_map/first/pallas_call | solution.py:452
  54.0 0.9 copy-done.8
  54.9 0.6 copy-done.19
  55.6 1.2 %copy-done.29 = bf16[27,128,256]{2,1,0:T(8,128)(2,1)} copy-done((bf16[27,128,256]{2,1,0:T(8,128)(2,1)}, bf16[27,128,256]{2,1,0:T(8,128)(2,1)S(1)}, u32[]{:S(2)}) %copy-start.29) | copy-done | bytes 1769496
  56.8 1.2 %copy-done.31 = bf16[27,128,256]{2,1,0:T(8,128)(2,1)} copy-done((bf16[27,128,256]{2,1,0:T(8,128)(2,1)}, bf16[27,128,256]{2,1,0:T(8,128)(2,1)S(1)}, u32[]{:S(2)}) %copy-start.31) | copy-done | bytes 1769496
  58.0 1.8 %convert_reduce_fusion = f32[384,256]{1,0:T(8,128)S(1)} fusion(bf16[8,384,256]{2,1,0:T(8,128)(2,1)} %all-to-all-done), kind=kLoop, calls=%fused_computation | loop fusion | flops 1474560 | bytes 1966080 | tf_op jit(solution)/shard_map/reduce_sum | solution.py:532
  59.9 11.1 %collective-permute-start.5 = (bf16[256,256]{1,0:T(8,128)(2,1)S(1)}, bf16[256,256]{1,0:T(8,128)(2,1)S(1)}, u32[]{:S(2)}, u32[]{:S(2)}) collective-permute-start(bf16[256,256]{1,0:T(8,128)(2,1)S(1)} %get-tuple-element.61), channel_id=1, source_target_pairs={{0,62},{1,63},{2,0},{3,1},{4,2},{5,3},{6,4},{7,5},{8,6},{9,7},{10,... | collective-permute-start | bytes 393224 | tf_op jit(solution)/shard_map/ppermute | solution.py:419
  71.0 2.1 %collective-permute-start.4 = (bf16[256,256]{1,0:T(8,128)(2,1)S(1)}, bf16[256,256]{1,0:T(8,128)(2,1)S(1)}, u32[]{:S(2)}, u32[]{:S(2)}) collective-permute-start(bf16[256,256]{1,0:T(8,128)(2,1)S(1)} %get-tuple-element.62), channel_id=1, source_target_pairs={{0,2},{1,3},{2,4},{3,5},{4,6},{5,7},{6,8},{7,9},{8,10},{9,11},{10,... | collective-permute-start | bytes 393224 | tf_op jit(solution)/shard_map/ppermute | solution.py:419
  73.5 8.6 %collective-permute-done.4.far_up = bf16[256,256]{1,0:T(8,128)(2,1)S(1)} collective-permute-done((bf16[256,256]{1,0:T(8,128)(2,1)S(1)}, bf16[256,256]{1,0:T(8,128)(2,1)S(1)}, u32[]{:S(2)}, u32[]{:S(2)}) %collective-permute-start.4) | collective-permute-done | bytes 131104 | tf_op jit(solution)/shard_map/ppermute | solution.py:419
  82.2 1.1 %copy-done.15 = bf16[256,1536]{1,0:T(8,128)(2,1)S(1)} copy-done((bf16[256,1536]{1,0:T(8,128)(2,1)S(1)}, bf16[256,1536]{1,0:T(8,128)(2,1)}, u32[]{:S(2)}) %copy-start.15) | copy-done | bytes 786456
  83.4 1.5 %copy-done.30 = bf16[27,128,256]{2,1,0:T(8,128)(2,1)S(1)} copy-done((bf16[27,128,256]{2,1,0:T(8,128)(2,1)S(1)}, bf16[27,128,256]{2,1,0:T(8,128)(2,1)}, u32[]{:S(2)}) %copy-start.30) | copy-done | bytes 1769496
  84.8 1.5 %copy-done.32 = bf16[27,128,256]{2,1,0:T(8,128)(2,1)S(1)} copy-done((bf16[27,128,256]{2,1,0:T(8,128)(2,1)S(1)}, bf16[27,128,256]{2,1,0:T(8,128)(2,1)}, u32[]{:S(2)}) %copy-start.32) | copy-done | bytes 1769496
  86.3 19.0 %second.1 = f32[4,4,256]{2,1,0:T(4,128)} custom-call(s32[1]{0:T(128)S(6)} %copy.17.width_ref, f32[3]{0:T(128)S(1)} %copy-done.26, f32[136,256]{1,0:T(8,128)S(1)} %get-tuple-element.51.state_in, bf16[27,128,256]{2,1,0:T(8,128)(2,1)S(1)} %copy-done.30, bf16[27,128,256]{2,1,0:T(8,128)(2,1)S(1)} %copy-done.32, ...), custom_call_target="tpu_custom_call" | custom-call | flops 10066329600 | bytes 1048576 | tf_op jit(solution)/shard_map/second/pallas_call | solution.py:471
  (62 shorter events, 1.1 us)
Async XLA Ops:
  0.0 1.1 %copy-start.18 = (bf16[64,4480]{1,0:T(8,128)(2,1)S(1)}, bf16[64,4480]{1,0:T(8,128)(2,1)}, u32[]{:S(2)}) copy-start(bf16[64,4480]{1,0:T(8,128)(2,1)} %blocks_ref.1) | copy-start | bytes 1720324
  9.2 5.2 %copy-start.33 = (f32[1,4,4,256]{3,2,1,0:T(4,128)S(1)}, f32[1,4,4,256]{3,2,1,0:T(4,128)}, u32[]{:S(2)}) copy-start(f32[1,4,4,256]{3,2,1,0:T(4,128)} %param.17) | copy-start | bytes 49156
  9.2 29.6 %copy-start = (bf16[9,256,256]{2,1,0:T(8,128)(2,1)S(1)}, bf16[9,256,256]{2,1,0:T(8,128)(2,1)}, u32[]{:S(2)}) copy-start(bf16[9,256,256]{2,1,0:T(8,128)(2,1)} %w_mid) | copy-start | bytes 3538948
  9.2 29.6 %copy-start.1 = (bf16[9,128,384]{2,1,0:T(8,128)(2,1)S(1)}, bf16[9,128,384]{2,1,0:T(8,128)(2,1)}, u32[]{:S(2)}) copy-start(bf16[9,128,384]{2,1,0:T(8,128)(2,1)} %w_dec) | copy-start | bytes 2654212
  9.2 29.6 %copy-start.2 = (bf16[9,256,128]{2,1,0:T(8,128)(2,1)S(1)}, bf16[9,256,128]{2,1,0:T(8,128)(2,1)}, u32[]{:S(2)}) copy-start(bf16[9,256,128]{2,1,0:T(8,128)(2,1)} %w_down) | copy-start | bytes 1769476
  9.3 29.6 %copy-start.3 = (bf16[9,128,128]{2,1,0:T(8,128)(2,1)S(1)}, bf16[9,128,128]{2,1,0:T(8,128)(2,1)}, u32[]{:S(2)}) copy-start(bf16[9,128,128]{2,1,0:T(8,128)(2,1)} %w_enc) | copy-start | bytes 884740
  9.3 29.6 %copy-start.4 = (bf16[9,128,4]{1,2,0:T(4,128)(2,1)S(1)}, bf16[9,128,4]{1,2,0:T(4,128)(2,1)}, u32[]{:S(2)}) copy-start(bf16[9,128,4]{1,2,0:T(4,128)(2,1)} %param.19) | copy-start | bytes 27652
  9.3 29.6 %copy-start.5 = (bf16[9,4,128]{2,1,0:T(4,128)(2,1)S(1)}, bf16[9,4,128]{2,1,0:T(4,128)(2,1)}, u32[]{:S(2)}) copy-start(bf16[9,4,128]{2,1,0:T(4,128)(2,1)} %w_out) | copy-start | bytes 27652
  9.3 48.7 %all-to-all-start = ((bf16[8,384,256]{2,1,0:T(8,128)(2,1)}), bf16[8,384,256]{2,1,0:T(8,128)(2,1)}, u32[]{:S(2)}, u32[]{:S(2)}) async-start(bf16[8,384,256]{2,1,0:T(8,128)(2,1)} %encode.1), calls=%async_computation | async-start | bytes 3145728 | tf_op jit(solution)/shard_map/all_to_all | solution.py:517
  14.4 16.5 %collective-permute-start = (f32[16,256]{1,0:T(8,128)S(1)}, f32[16,256]{1,0:T(8,128)S(1)}, u32[]{:S(2)}, u32[]{:S(2)}) collective-permute-start(f32[16,256]{1,0:T(8,128)S(1)} %reshape.6.own), channel_id=1, source_target_pairs={{0,3},{1,4},{2,5},{3,6},{4,7},{5,8},{6,9},{7,10},{8,11},{9,12},{10... | collective-permute-start | bytes 49160 | tf_op jit(solution)/shard_map/ppermute | solution.py:419
  21.2 11.2 %collective-permute-start.1 = (f32[16,256]{1,0:T(8,128)S(1)}, f32[16,256]{1,0:T(8,128)S(1)}, u32[]{:S(2)}, u32[]{:S(2)}) collective-permute-start(f32[16,256]{1,0:T(8,128)S(1)} %reshape.6.own), channel_id=1, source_target_pairs={{0,61},{1,62},{2,63},{3,0},{4,1},{5,2},{6,3},{7,4},{8,5},{9,6},{10... | collective-permute-start | bytes 49160 | tf_op jit(solution)/shard_map/ppermute | solution.py:419
  32.3 12.3 %collective-permute-start.3 = (f32[48,256]{1,0:T(8,128)S(1)}, f32[48,256]{1,0:T(8,128)S(1)}, u32[]{:S(2)}, u32[]{:S(2)}) collective-permute-start(f32[48,256]{1,0:T(8,128)S(1)} %constant_dynamic-update-slice_fusion), channel_id=1, source_target_pairs={{0,63},{1,0},{2,1},{3,2},{4,3},{5,4},{6,5},{7,6},{8,7},{9,8},{10,9... | collective-permute-start | bytes 147464 | tf_op jit(solution)/shard_map/ppermute | solution.py:419
  35.6 9.9 %collective-permute-start.2 = (f32[48,256]{1,0:T(8,128)S(1)}, f32[48,256]{1,0:T(8,128)S(1)}, u32[]{:S(2)}, u32[]{:S(2)}) collective-permute-start(f32[48,256]{1,0:T(8,128)S(1)} %constant_dynamic-update-slice_fusion), channel_id=1, source_target_pairs={{0,1},{1,2},{2,3},{3,4},{4,5},{5,6},{6,7},{7,8},{8,9},{9,10},{10,1... | collective-permute-start | bytes 147464 | tf_op jit(solution)/shard_map/ppermute | solution.py:419
  39.4 1.1 %copy-start.6 = (bf16[256,2304]{1,0:T(8,128)(2,1)}, bf16[256,2304]{1,0:T(8,128)(2,1)S(1)}, u32[]{:S(2)}) copy-start(bf16[256,2304]{1,0:T(8,128)(2,1)S(1)} %get-tuple-element.56.w_mid) | copy-start | bytes 3538948
  42.2 0.9 copy-start.14
  46.7 35.4 %copy-start.13 = (bf16[256,1536]{1,0:T(8,128)(2,1)S(1)}, bf16[256,1536]{1,0:T(8,128)(2,1)}, u32[]{:S(2)}) copy-start(bf16[256,1536]{1,0:T(8,128)(2,1)} %copy-done.12) | copy-start | bytes 2359300
  46.8 35.4 %copy-start.17 = (bf16[256,1152]{1,0:T(8,128)(2,1)S(1)}, bf16[256,1152]{1,0:T(8,128)(2,1)}, u32[]{:S(2)}) copy-start(bf16[256,1152]{1,0:T(8,128)(2,1)} %copy-done.16) | copy-start | bytes 1769476
  54.0 0.9 copy-start.8
  55.6 1.2 %copy-start.29 = (bf16[27,128,256]{2,1,0:T(8,128)(2,1)}, bf16[27,128,256]{2,1,0:T(8,128)(2,1)S(1)}, u32[]{:S(2)}) copy-start(bf16[27,128,256]{2,1,0:T(8,128)(2,1)S(1)} %get-tuple-element.52.secondc0) | copy-start | bytes 5308420
  56.8 1.2 %copy-start.31 = (bf16[27,128,256]{2,1,0:T(8,128)(2,1)}, bf16[27,128,256]{2,1,0:T(8,128)(2,1)S(1)}, u32[]{:S(2)}) copy-start(bf16[27,128,256]{2,1,0:T(8,128)(2,1)S(1)} %get-tuple-element.53.seconde0) | copy-start | bytes 5308420
  58.0 24.2 %copy-start.7 = (bf16[256,2304]{1,0:T(8,128)(2,1)S(1)}, bf16[256,2304]{1,0:T(8,128)(2,1)}, u32[]{:S(2)}) copy-start(bf16[256,2304]{1,0:T(8,128)(2,1)} %copy-done.6) | copy-start | bytes 3538948
  58.0 24.2 %copy-start.11 = (bf16[256,1536]{1,0:T(8,128)(2,1)S(1)}, bf16[256,1536]{1,0:T(8,128)(2,1)}, u32[]{:S(2)}) copy-start(bf16[256,1536]{1,0:T(8,128)(2,1)} %copy-done.10) | copy-start | bytes 2359300
  58.0 24.2 %copy-start.22 = (bf16[48,512]{1,0:T(8,128)(2,1)S(1)}, bf16[48,512]{1,0:T(8,128)(2,1)}, u32[]{:S(2)}) copy-start(bf16[48,512]{1,0:T(8,128)(2,1)} %copy-done.21) | copy-start | bytes 147460
  58.0 24.2 %copy-start.26 = (f32[3]{0:T(128)S(1)}, f32[3]{0:T(128)}, u32[]{:S(2)}) copy-start(f32[3]{0:T(128)} %sigma_ref.3) | copy-start | bytes 40
  58.0 24.2 %copy-start.28 = (f32[128]{0:T(128)S(1)}, f32[128]{0:T(128)}, u32[]{:S(2)}) copy-start(f32[128]{0:T(128)} %param.20) | copy-start | bytes 1540
  58.0 24.2 %copy-start.9 = (bf16[256,1536]{1,0:T(8,128)(2,1)S(1)}, bf16[256,1536]{1,0:T(8,128)(2,1)}, u32[]{:S(2)}) copy-start(bf16[256,1536]{1,0:T(8,128)(2,1)} %copy-done.8) | copy-start | bytes 2359300
  58.0 24.2 %copy-start.20 = (bf16[96,256]{1,0:T(8,128)(2,1)S(1)}, bf16[96,256]{1,0:T(8,128)(2,1)}, u32[]{:S(2)}) copy-start(bf16[96,256]{1,0:T(8,128)(2,1)} %copy-done.19) | copy-start | bytes 147460
  59.9 13.6 %collective-permute-start.5 = (bf16[256,256]{1,0:T(8,128)(2,1)S(1)}, bf16[256,256]{1,0:T(8,128)(2,1)S(1)}, u32[]{:S(2)}, u32[]{:S(2)}) collective-permute-start(bf16[256,256]{1,0:T(8,128)(2,1)S(1)} %get-tuple-element.61), channel_id=1, source_target_pairs={{0,62},{1,63},{2,0},{3,1},{4,2},{5,3},{6,4},{7,5},{8,6},{9,7},{10,... | collective-permute-start | bytes 393224 | tf_op jit(solution)/shard_map/ppermute | solution.py:419
  71.0 11.1 %collective-permute-start.4 = (bf16[256,256]{1,0:T(8,128)(2,1)S(1)}, bf16[256,256]{1,0:T(8,128)(2,1)S(1)}, u32[]{:S(2)}, u32[]{:S(2)}) collective-permute-start(bf16[256,256]{1,0:T(8,128)(2,1)S(1)} %get-tuple-element.62), channel_id=1, source_target_pairs={{0,2},{1,3},{2,4},{3,5},{4,6},{5,7},{6,8},{7,9},{8,10},{9,11},{10,... | collective-permute-start | bytes 393224 | tf_op jit(solution)/shard_map/ppermute | solution.py:419
  82.2 1.1 %copy-start.15 = (bf16[256,1536]{1,0:T(8,128)(2,1)S(1)}, bf16[256,1536]{1,0:T(8,128)(2,1)}, u32[]{:S(2)}) copy-start(bf16[256,1536]{1,0:T(8,128)(2,1)} %copy-done.14) | copy-start | bytes 2359300
  83.3 1.5 %copy-start.30 = (bf16[27,128,256]{2,1,0:T(8,128)(2,1)S(1)}, bf16[27,128,256]{2,1,0:T(8,128)(2,1)}, u32[]{:S(2)}) copy-start(bf16[27,128,256]{2,1,0:T(8,128)(2,1)} %copy-done.29) | copy-start | bytes 5308420
  84.8 1.5 %copy-start.32 = (bf16[27,128,256]{2,1,0:T(8,128)(2,1)S(1)}, bf16[27,128,256]{2,1,0:T(8,128)(2,1)}, u32[]{:S(2)}) copy-start(bf16[27,128,256]{2,1,0:T(8,128)(2,1)} %copy-done.31) | copy-start | bytes 5308420
  (9 other events, 6.6 us)

commit v4 on v3

v4 whole, which is shorter than its diff:
```python
import functools
import math

import jax
import jax.numpy as jnp
from jax import lax
from jax.experimental import pallas as pl
from jax.experimental.pallas import tpu as pltpu
from jax.sharding import PartitionSpec as P

K = 96
SIGMA_DATA = 0.5
BF = jnp.bfloat16
F32 = jnp.float32
HALF = 128
ROWS = 256
NT = (((1,), (1,)), ((), ()))
TN = (((0,), (0,)), ((), ()))

SCALED = (-7, 17)
FIRST = (-6, 15)
SECOND = (-5, 13)
THIRD = (-2, 6)
FOURTH = (-1, 4)
FIFTH = (-1, 6)


def silu(v):
    h = 0.5 * v
    return h + h * jnp.tanh(h)


def dot_nt(a, b):
    return lax.dot_general(a, b, NT, preferred_element_type=F32)


def encode_kernel(anchor_ref, blocks_ref, w_ref, out_ref, enc_ref, flat, wide):
    band = lax.axis_index("band")
    tile = lax.axis_index("tile")
    count = blocks_ref.shape[0]
    cells = enc_ref.shape[1]
    chans = w_ref.shape[0]
    tiles = blocks_ref.shape[1] // 128
    group = 8 * tiles

    flat[count * tiles :, :] = jnp.zeros((flat.shape[0] - count * tiles, 128), F32)
    for g in range(count // 16):
        for t in range(tiles):
            v = blocks_ref[16 * g : 16 * g + 16, 128 * t : 128 * t + 128].astype(F32)
            flat[2 * g * group + 8 * t : 2 * g * group + 8 * t + 8, :] = v[:8]
            flat[(2 * g + 1) * group + 8 * t : (2 * g + 1) * group + 8 * t + 8, :] = v[8:]

    w = w_ref[...].astype(F32)
    for half in range(2):
        wide[half, 0:chans, :] = w[:, 128 * half : 128 * half + 128]
        wide[half, chans:80, :] = jnp.zeros((80 - chans, 128), F32)
    weight = jnp.concatenate(
        [
            jnp.concatenate([wide[half, pl.ds(odd, 40, stride=2), :] for half in range(2)], 1)
            for odd in range(2)
        ],
        0,
    ).astype(BF)
    first = lax.broadcasted_iota(jnp.int32, (40, 128), 1) < 64

    def encode(g, carry):
        begin = pl.multiple_of(g * group, 8)
        cols = []
        for k in range(4):
            one = flat[pl.ds(begin + 2 * k, 40, stride=8), :]
            two = flat[pl.ds(begin + 2 * k + 1, 40, stride=8), :]
            even = jnp.where(first, one, pltpu.roll(two, 64, 1))
            odd = jnp.where(first, pltpu.roll(one, 64, 1), two)
            cols.append(jnp.concatenate([even, odd], 0))
        x = jnp.concatenate(cols, 1).astype(BF)
        v = lax.dot_general(x, weight, TN, preferred_element_type=F32)
        v = silu(v).astype(BF).astype(F32)
        enc_ref[pl.ds(g * 8, 8)] = v.reshape(8, cells, 256)
        return carry

    lax.fori_loop(0, count // 8, encode, 0)

    enc_ref[pl.ds(count, 8)] = enc_ref[pl.ds(0, 8)]

    def window(k, carry):
        nest = k // 2
        part = k % 2
        anchor = anchor_ref[nest, tile]
        begin = anchor + (band - anchor + 512) % 8 + part * 48
        row = (begin % 512) // 8
        total = enc_ref[row]
        for m in range(1, 6):
            total = total + enc_ref[row + m]
        out_ref[nest, pl.ds(pl.multiple_of(part * cells, cells), cells), :] = total.astype(BF)
        return carry

    lax.fori_loop(0, 16, window, 0, unroll=4)


def pair_weight(w, a):
    zero = jnp.zeros_like(w(a, 0))
    own = jnp.concatenate(
        [jnp.concatenate([w(a, 1), w(a, 2)], 1), jnp.concatenate([w(a, 0), w(a, 1)], 1)], 0
    )
    rim = jnp.concatenate(
        [jnp.concatenate([w(a, 0), zero], 1), jnp.concatenate([zero, w(a, 2)], 1)], 0
    )
    return own, rim


def form_small(w_in, w_out, in_o, out_o):
    def tall(ref, a, b):
        if not 0 <= b <= 2:
            return jnp.zeros((8, 128), F32)
        return jnp.concatenate([ref[3 * a + b].astype(F32), jnp.zeros((4, 128), F32)], 0)

    in_o[...] = jnp.concatenate(
        [
            jnp.concatenate([tall(w_in, a, q - p) for p in range(2)], 1)
            for a in range(3)
            for q in range(4)
        ],
        0,
    ).astype(BF)
    out_o[...] = jnp.concatenate(
        [
            jnp.concatenate([tall(w_out, a, q - p) for q in (1, 2, 0, 3)], 1)
            for a in range(3)
            for p in range(2)
        ],
        0,
    ).astype(BF)


def form_pairs(w, chans, out):
    for a in range(3):
        own, rim = pair_weight(lambda i, b: w[3 * i + b][:, 0:chans], a)
        out[:, 512 * a : 512 * a + 256] = own
        out[:, 512 * a + 256 : 512 * a + 512] = rim


def form_down(w, out):
    for a in range(3):
        out[:, 256 * a : 256 * a + 128] = w[3 * a + 1]
        out[:, 256 * a + 128 : 256 * a + 256] = w[3 * a + 2]
        out[:, 768 + 128 * a : 896 + 128 * a] = w[3 * a]


def form_mid(w, out):
    for a in range(3):
        for b in range(3):
            out[:, 768 * a + 256 * b : 768 * a + 256 * b + 256] = w[3 * a + b]


def form_up(w, even, odd):
    def up(a, b):
        return w[3 * a + b][:, 128:384].astype(F32)

    for out, sets in ((even, ((0,), (1, 2))), (odd, ((0, 1), (2,)))):
        for k, taps in enumerate(sets):
            col = [sum(up(a, b) for a in taps) for b in range(3)]
            zero = jnp.zeros_like(col[0])
            out[:, 768 * k : 768 * k + 256] = jnp.concatenate([col[0], zero], 0).astype(BF)
            out[:, 768 * k + 256 : 768 * k + 512] = jnp.concatenate(
                [col[1] + col[2], col[0] + col[1]], 0
            ).astype(BF)
            out[:, 768 * k + 512 : 768 * k + 768] = jnp.concatenate([zero, col[2]], 0).astype(BF)


class Field:
    def __init__(self, width):
        self.tile = lax.axis_index("tile")
        lane = lax.broadcasted_iota(jnp.int32, (HALF, 256), 1)
        pair = lax.broadcasted_iota(jnp.int32, (HALF, 256), 0)
        self.colmask = (2 * pair + lane // 128 < width).astype(F32)
        self.halfmask = (2 * pair < width).astype(F32)
        self.natural = (lax.broadcasted_iota(jnp.int32, (8, 256), 1) < width).astype(F32)

    def fine_ok(self, rho):
        row = self.tile * 4 + rho
        return jnp.logical_and(row >= 0, row < ROWS).astype(F32)

    def half_ok(self, h):
        row = self.tile * 2 + h
        return jnp.logical_and(row >= 0, row < ROWS // 2).astype(F32)

    def keep_pairs(self, y, center, rim, at, n, lo):
        y = jnp.concatenate(
            [y[k * HALF : (k + 1) * HALF] * (self.colmask * self.fine_ok(lo + at + k)) for k in range(n)], 0
        )
        side = jnp.concatenate([slide(y[:, 128:], 1), slide(y[:, :128], -1)], 1).astype(BF)
        y = y.astype(BF)
        for k in range(n):
            center[at + k] = y[k * HALF : (k + 1) * HALF]
            rim[at + k] = side[k * HALF : (k + 1) * HALF]

    def keep_half(self, y, center, left, right, at, n, lo):
        y = jnp.concatenate(
            [y[k * HALF : (k + 1) * HALF] * (self.halfmask * self.half_ok(lo + at + k)) for k in range(n)], 0
        )
        sides = (slide(y, 1).astype(BF), slide(y, -1).astype(BF))
        y = y.astype(BF)
        for k in range(n):
            cut = slice(k * HALF, (k + 1) * HALF)
            center[at + k] = y[cut]
            left[at + k] = sides[0][cut]
            right[at + k] = sides[1][cut]


def levels(sigma_ref, step):
    now = jnp.full((1, 256), sigma_ref[step], F32)
    after = jnp.full((1, 256), sigma_ref[step + 1], F32)
    var = now * now + SIGMA_DATA * SIGMA_DATA
    root = jnp.sqrt(var)
    return now, 1.0 / root, SIGMA_DATA * SIGMA_DATA / var, now * SIGMA_DATA / root, (after - now) / now


def embedding(w_sigma, now):
    return jnp.concatenate([w_sigma[...], w_sigma[...]], 1) * jnp.log(now)


def slide(x, by):
    rows = x.shape[0]
    edge = 0 if by == 1 else HALF - 1
    where = lax.broadcasted_iota(jnp.int32, x.shape, 0) % HALF
    return jnp.where(where == edge, 0.0, pltpu.roll(x, by % rows, 0))


def stacked(ref, at, n, step=1):
    return jnp.concatenate([ref[at + step * k] for k in range(n)], 0)


def chunks(total, size, body):
    full = total // size
    if full == 1:
        body(0, size)
    elif full:
        lax.fori_loop(0, full, lambda i, c: (body(i * size, size), c)[1], 0)
    if total % size:
        body(full * size, total % size)


def step_kernel(
    step, offsets,
    width_ref, sigma_ref, own, up2, up1, down1, down2, cond_up, cond_own, cond_down,
    w_sigma, w_in, w_out, w_enc_h, w_down_h, w_mid_h, w_dec_h,
    state_ref, scaled_ref,
    scaled, spread, firstc, firste, secondc, seconde, third, thirdl, thirdr, fourth, fourthl, fourthr,
    fifthc, fifthe, prod, picked,
    raw_enc, raw_down, raw_mid, raw_dec, f_in, f_out, f_enc, f_down, f_mid, f_dec, f_even, f_odd, sems,
):
    loads = [
        pltpu.make_async_copy(src, dst, sems.at[i])
        for i, (src, dst) in enumerate(
            ((w_enc_h, raw_enc), (w_down_h, raw_down), (w_mid_h, raw_mid), (w_dec_h, raw_dec))
        )
    ]
    for load in loads:
        load.start()
    field = Field(width_ref[0])
    sigma, scale, keep, mix, move = levels(sigma_ref, step)

    empty = jnp.zeros((4, 256), F32)
    scaled_lo = SCALED[0]
    for tile_off, ref, begin in ((-2, up2, offsets[0]), (-1, up1, offsets[1]), (1, down1, offsets[2]), (2, down2, offsets[3])):
        value = ref[begin : begin + 16, :].astype(F32)
        for r in range(4):
            rho = 4 * tile_off + r
            if scaled_lo <= rho < scaled_lo + SCALED[1]:
                row = jnp.concatenate([value[4 * r : 4 * r + 4], empty], 0)
                scaled[8 * (rho - scaled_lo) : 8 * (rho - scaled_lo) + 8, :] = row * field.fine_ok(rho)
    if step == 0:
        states = [sigma * own[4 * r : 4 * r + 4, :] * field.natural[0:4] for r in range(4)]
    else:
        states = [own[4 * r : 4 * r + 4, :] for r in range(4)]
    for r in range(4):
        row = jnp.concatenate([(states[r] * scale).astype(BF).astype(F32), empty], 0)
        scaled[8 * (r - scaled_lo) : 8 * (r - scaled_lo) + 8, :] = row

    form_small(w_in, w_out, f_in, f_out)

    col = lax.broadcasted_iota(jnp.int32, (256, 512), 0)
    place = lax.broadcasted_iota(jnp.int32, (256, 512), 1)
    pick = (col == 2 * (place % 128) + place // 128 - 1).astype(F32).astype(BF)
    spread[...] = jnp.dot(scaled[...].astype(BF), pick, preferred_element_type=F32)
    bias = embedding(w_sigma, sigma)

    def first_rows(at, n):
        cols = [
            jnp.concatenate(
                [
                    spread[pl.ds(pl.multiple_of((at + k + a) * 8, 8), 8), 128 * q : 128 * q + 128]
                    for a in range(3)
                    for q in range(4)
                ],
                0,
            )
            for k in range(n)
        ]
        x = jnp.concatenate(cols, 1).astype(BF)
        y = lax.dot_general(x, f_in[...], TN, preferred_element_type=F32)
        field.keep_pairs(silu(y + bias), firstc, firste, at, n, FIRST[0])

    chunks(FIRST[1], 5, first_rows)

    loads[0].wait()
    form_pairs(raw_enc, 128, f_enc)
    x = jnp.concatenate([stacked(ref, a, SECOND[1]) for a in range(3) for ref in (firstc, firste)], 1)
    field.keep_pairs(silu(dot_nt(x, f_enc[...])), secondc, seconde, 0, SECOND[1], SECOND[0])

    loads[1].wait()
    form_down(raw_down, f_down)
    repeat = (
        lax.broadcasted_iota(jnp.int32, (HALF, 64), 0) // 2 == lax.broadcasted_iota(jnp.int32, (HALF, 64), 1)
    ).astype(F32).astype(BF)
    n = THIRD[1]
    begin = 2 * THIRD[0] - 1 - SECOND[0]
    x = jnp.concatenate(
        [stacked(secondc, begin + a, n, 2) for a in range(3)]
        + [jnp.concatenate([seconde[begin + a + 2 * k][:, :128] for k in range(n)], 0) for a in range(3)],
        1,
    )
    add = [
        jnp.dot(repeat, ref[64 * r : 64 * r + 64, :], preferred_element_type=F32)
        for ref in (cond_up, cond_own, cond_down)
        for r in range(2)
    ]
    y = dot_nt(x, f_down[...]) + jnp.concatenate(add, 0)
    field.keep_half(silu(y), third, thirdl, thirdr, 0, n, THIRD[0])

    loads[2].wait()
    form_mid(raw_mid, f_mid)
    n = FOURTH[1]
    x = jnp.concatenate([stacked(ref, a, n) for a in range(3) for ref in (thirdl, third, thirdr)], 1)
    field.keep_half(silu(dot_nt(x, f_mid[...])), fourth, fourthl, fourthr, 0, n, FOURTH[0])

    loads[3].wait()
    form_pairs(raw_dec, 128, f_dec)
    form_up(raw_dec, f_even, f_odd)
    for at in range(2):
        rho = FIFTH[0] + at
        odd = rho % 2
        n = FIFTH[1] // 2
        begin = rho - 1 - SECOND[0]
        h = (rho - odd) // 2 - FOURTH[0] - (0 if odd else 1)
        x = jnp.concatenate(
            [stacked(ref, begin + a, n, 2) for a in range(3) for ref in (secondc, seconde)], 1
        )
        z = jnp.concatenate(
            [stacked(ref, h + a, n) for a in range(2) for ref in (fourthl, fourth, fourthr)], 1
        )
        y = silu(dot_nt(x, f_dec[...]) + dot_nt(z, (f_odd if odd else f_even)[...]))
        for k in range(n):
            field.keep_pairs(y[k * HALF : (k + 1) * HALF], fifthc, fifthe, at + 2 * k, 1, FIFTH[0])

    n = FIFTH[1]
    x = jnp.concatenate([stacked(fifthc, 0, n), stacked(fifthe, 0, n)], 1)
    prod[...] = dot_nt(f_out[...], x)
    for k in range(4):
        for p in range(2):
            picked[p, 8 * k : 8 * k + 8, :] = sum(
                prod[16 * a + 8 * p : 16 * a + 8 * p + 8, (k + a) * HALF : (k + a + 1) * HALF]
                for a in range(3)
            )
    weave_j = lax.broadcasted_iota(jnp.int32, (HALF, 256), 0)
    weave_c = lax.broadcasted_iota(jnp.int32, (HALF, 256), 1)
    net = sum(
        jnp.dot(
            picked[p],
            (weave_c == 2 * weave_j + p).astype(F32),
            preferred_element_type=F32,
            precision=lax.Precision.HIGHEST,
        )
        for p in range(2)
    )
    for r in range(4):
        denoised = keep * states[r] + mix * net[8 * r : 8 * r + 4]
        now = (states[r] + move * (states[r] - denoised)) * field.natural[0:4]
        if step == 0:
            state_ref[4 * r : 4 * r + 4, :] = now
            scaled_ref[4 * r : 4 * r + 4, :] = (now * levels(sigma_ref, 1)[1]).astype(BF)
        else:
            state_ref[:, r, :] = now


def turn(x, by):
    n = lax.axis_size("tile")
    return lax.ppermute(x, "tile", [(i, (i + by) % n) for i in range(n)])


VMEM = pl.BlockSpec(memory_space=pltpu.VMEM)
SMEM = pl.BlockSpec(memory_space=pltpu.SMEM)


def limit(mib):
    return pltpu.CompilerParams(vmem_limit_bytes=mib << 20)


def rowbuf(n):
    return pltpu.VMEM((n, HALF, 256), BF)


def cost(passes):
    return pl.CostEstimate(flops=passes * 128 * 65536 * 2, bytes_accessed=1 << 20, transcendentals=0)


def step_call(step, offsets, width, sigmas, own, pieces, conds, w_sigma, weights):
    raw = [pltpu.VMEM(w.shape, BF) for w in weights[2:]]
    if step == 0:
        outs = [jax.ShapeDtypeStruct((16, 256), F32), jax.ShapeDtypeStruct((16, 256), BF)]
        kernel = functools.partial(step_kernel, step, offsets)
    else:
        outs = [jax.ShapeDtypeStruct((4, 4, 256), F32)]

        def kernel(*refs):
            step_kernel(step, offsets, *refs[:18], None, *refs[18:])

    return pl.pallas_call(
        kernel,
        out_shape=outs,
        in_specs=[SMEM, SMEM] + [VMEM] * 11 + [pl.BlockSpec(memory_space=pl.ANY)] * 4,
        out_specs=[VMEM] * len(outs),
        scratch_shapes=[
            pltpu.VMEM((SCALED[1] * 8, 256), F32), pltpu.VMEM((SCALED[1] * 8, 512), F32),
            rowbuf(FIRST[1]), rowbuf(FIRST[1]), rowbuf(SECOND[1]), rowbuf(SECOND[1]),
            *[rowbuf(THIRD[1])] * 3, *[rowbuf(FOURTH[1])] * 3, *[rowbuf(FIFTH[1])] * 2,
            pltpu.VMEM((48, FIFTH[1] * HALF), F32), pltpu.VMEM((2, 32, HALF), F32),
            *raw,
            *[
                pltpu.VMEM(shape, BF)
                for shape in (
                    (96, 256), (48, 512), (256, 1536), (256, 1152), (256, 2304),
                    (256, 1536), (256, 1536), (256, 1536),
                )
            ],
            pltpu.SemaphoreType.DMA((4,)),
        ],
        compiler_params=limit(56),
        cost_estimate=cost(240),
        name="step" + str(step),
    )(width, sigmas, own, *pieces, *conds, w_sigma, *weights)


def encode_call(block_anchor, coarse_blocks, w_context):
    chans = w_context.shape[1]
    cells = coarse_blocks.shape[1] // chans
    count = coarse_blocks.shape[0]
    tiles = coarse_blocks.shape[1] // 128
    return pl.pallas_call(
        encode_kernel,
        out_shape=jax.ShapeDtypeStruct((8, 2 * cells, 256), BF),
        in_specs=[SMEM, VMEM, VMEM],
        out_specs=VMEM,
        scratch_shapes=[
            pltpu.VMEM((count + 8, cells, 256), F32),
            pltpu.VMEM((count * tiles + 64, 128), F32),
            pltpu.VMEM((2, 80, 128), F32),
        ],
        compiler_params=limit(56),
        cost_estimate=cost(100),
        name="encode",
    )(block_anchor, coarse_blocks, w_context.T)


def per_device(
    coarse_blocks, block_anchor, nest_width, sigmas, noise,
    w_context, w_in, w_sigma, w_enc, w_down, w_mid, w_dec, w_out,
):
    partial = encode_call(block_anchor, coarse_blocks, w_context)
    arrived = lax.all_to_all(partial, "band", 0, 0, tiled=True)

    held = lax.optimization_barrier((partial, noise))
    own = held[1][0].transpose(1, 0, 2).reshape(16, 256)
    mask = (jnp.arange(256, dtype=jnp.int32) < nest_width[0]).astype(F32)
    scale = 1.0 / jnp.sqrt(sigmas[0] * sigmas[0] + SIGMA_DATA * SIGMA_DATA)
    scaled = (sigmas[0] * own * mask[None, :] * scale).astype(BF)
    up = turn(scaled, 1)
    down = turn(scaled, -1)
    arrived, own, scaled, up, down = lax.optimization_barrier((arrived, own, scaled, up, down))

    cond = (jnp.sum(arrived.astype(F32), axis=0) * (1.0 / math.sqrt(K // 2))).astype(BF)
    near_up = turn(jnp.concatenate([cond, up, scaled], 0), 1)
    near_down = turn(jnp.concatenate([cond, scaled, down], 0), -1)
    conds = (near_up, cond, near_down)
    w_sigma = w_sigma.reshape(1, -1)
    weights = (w_in.transpose(0, 2, 1), w_out, w_enc, w_down, w_mid, w_dec)
    state, scaled = step_call(
        0, (128, 144, 128, 144), nest_width, sigmas, own, (near_up, near_up, near_down, near_down),
        conds, w_sigma, weights,
    )
    pieces = tuple(turn(scaled, by) for by in (2, 1, -1, -2))
    (out,) = step_call(1, (0, 0, 0, 0), nest_width, sigmas, state, pieces, conds, w_sigma, weights)
    return out[None]


def solution(mesh):
    return jax.shard_map(
        per_device,
        mesh=mesh,
        in_specs=(
            P("band", None), P(), P("band"), P(), P("band", None, "tile", None),
            P(), P(), P(), P(), P(), P(), P(), P(),
        ),
        out_specs=P("band", None, "tile", None),
        check_vma=False,
    )
```

time: 106 us -> 82.7 us (0.78)
  the two profiles are of different devices: /device:TPU:10 before, /device:TPU:2 now
where the time goes in v4:
time: 82.7 us; the launch traced here: 82.2 us
  starting transfers between devices  46.5 us (56%)
  Pallas kernels  28.3 us (34%)
  waiting for transfers between devices  4.97 us (6%)
  local copies, waits for them, and re-layouts  1.24 us (1%)
  between operations  1.11 us (1%)
    ppermute x8, starting transfers between devices, turn(): return lax.ppermute(x, 'tile', [(i, (i + by) % n) for i in range(n)])  37.2 us
    pallas_call x2, Pallas kernels, step_call(): pl.pallas_call(kernel, out_shape=outs, in_specs=[SMEM, SMEM] + [VMEM] * 1...  22.7 us
    all_to_all x1, starting transfers between devices, per_device(): arrived = lax.all_to_all(partial, 'band', 0, 0, tiled=True)  9.31 us
    pallas_call x1, Pallas kernels, encode_call(): pl.pallas_call(encode_kernel, out_shape=jax.ShapeDtypeStruct((8, 2 * cell...  5.52 us
    ppermute x8, waiting for transfers between devices, turn(): return lax.ppermute(x, 'tile', [(i, (i + by) % n) for i in range(n)])  4.96 us
  transfers between devices with their start and end apart: 9, of which 4 were waited for; matrix products, arithmetic and copies ran while one was open for 0% of the time, Pallas kernels for 0%

profile of v4, /device:TPU:2, one launch (start us, length us, event | category | flops | bytes accessed | tf_op | source)
XLA Modules:
  0.0 82.2 jit_solution(4045916218114370995)
XLA Ops:
  0.0 5.5 %encode.1 = bf16[8,128,256]{2,1,0:T(8,128)(2,1)} custom-call(s32[8,64]{1,0:T(8,128)} %anchor_ref.1, bf16[64,4480]{1,0:T(8,128)(2,1)} %blocks_ref.1, bf16[70,256]{1,0:T(8,128)(2,1)} %bitcast.15), custom_call_target="tpu_custom_call" | custom-call | flops 1677721600 | bytes 1048576 | tf_op jit(solution)/shard_map/encode/pallas_call | solution.py:449
  5.5 9.3 %all-to-all-start = ((bf16[8,128,256]{2,1,0:T(8,128)(2,1)}), bf16[8,128,256]{2,1,0:T(8,128)(2,1)S(1)}, u32[]{:S(2)}, u32[]{:S(2)}) async-start(bf16[8,128,256]{2,1,0:T(8,128)(2,1)} %encode.1), calls=%async_computation | async-start | bytes 1048576 | tf_op jit(solution)/shard_map/all_to_all | solution.py:470
  15.5 0.0 copy-done.2
  15.5 0.0 copy-start.1
  15.5 0.0 copy-done.3
  15.7 1.9 %collective-permute-start = (bf16[16,256]{1,0:T(8,128)(2,1)S(1)}, bf16[16,256]{1,0:T(8,128)(2,1)S(1)}, u32[]{:S(2)}, u32[]{:S(2)}) collective-permute-start(bf16[16,256]{1,0:T(8,128)(2,1)S(1)} %multiply_convert_fusion.1), channel_id=1, source_target_pairs={{0,1},{1,2},{2,3},{3,4},{4,5},{5,6},{6,7},{7,8},{8,9},{9,10},{10,1... | collective-permute-start | bytes 24584 | tf_op jit(solution)/shard_map/ppermute | solution.py:388
  17.6 9.4 %collective-permute-start.1 = (bf16[16,256]{1,0:T(8,128)(2,1)S(1)}, bf16[16,256]{1,0:T(8,128)(2,1)S(1)}, u32[]{:S(2)}, u32[]{:S(2)}) collective-permute-start(bf16[16,256]{1,0:T(8,128)(2,1)S(1)} %multiply_convert_fusion.1), channel_id=1, source_target_pairs={{0,63},{1,0},{2,1},{3,2},{4,3},{5,4},{6,5},{7,6},{8,7},{9,8},{10,9... | collective-permute-start | bytes 24584 | tf_op jit(solution)/shard_map/ppermute | solution.py:388
  27.0 0.0 collective-permute-done
  27.0 1.3 %collective-permute-done.1 = bf16[16,256]{1,0:T(8,128)(2,1)S(1)} collective-permute-done((bf16[16,256]{1,0:T(8,128)(2,1)S(1)}, bf16[16,256]{1,0:T(8,128)(2,1)S(1)}, u32[]{:S(2)}, u32[]{:S(2)}) %collective-permute-start.1) | collective-permute-done | bytes 8224 | tf_op jit(solution)/shard_map/ppermute | solution.py:388
  28.3 0.0 all-to-all-done
  28.3 0.1 convert_reduce_fusion
  28.4 0.0 copy-start
  28.5 1.9 %collective-permute-start.2 = (bf16[160,256]{1,0:T(8,128)(2,1)S(1)}, bf16[160,256]{1,0:T(8,128)(2,1)S(1)}, u32[]{:S(2)}, u32[]{:S(2)}) collective-permute-start(bf16[160,256]{1,0:T(8,128)(2,1)S(1)} %get-tuple-element.22), channel_id=1, source_target_pairs={{0,1},{1,2},{2,3},{3,4},{4,5},{5,6},{6,7},{7,8},{8,9},{9,10},{10,1... | collective-permute-start | bytes 245768 | tf_op jit(solution)/shard_map/ppermute | solution.py:388
  30.4 7.5 %collective-permute-start.3 = (bf16[160,256]{1,0:T(8,128)(2,1)S(1)}, bf16[160,256]{1,0:T(8,128)(2,1)S(1)}, u32[]{:S(2)}, u32[]{:S(2)}) collective-permute-start(bf16[160,256]{1,0:T(8,128)(2,1)S(1)} %get-tuple-element.21), channel_id=1, source_target_pairs={{0,63},{1,0},{2,1},{3,2},{4,3},{5,4},{6,5},{7,6},{8,7},{9,8},{10,9... | collective-permute-start | bytes 245768 | tf_op jit(solution)/shard_map/ppermute | solution.py:388
  37.9 0.5 collective-permute-done.2.up2.up1.cond_up.refs_7_
  38.4 1.6 %collective-permute-done.3.down1.down2.cond_down.refs_9_ = bf16[160,256]{1,0:T(8,128)(2,1)S(1)} collective-permute-done((bf16[160,256]{1,0:T(8,128)(2,1)S(1)}, bf16[160,256]{1,0:T(8,128)(2,1)S(1)}, u32[]{:S(2)}, u32[]{:S(2)}) %collective-permute-start.3) | collective-permute-done | bytes 81952 | tf_op jit(solution)/shard_map/ppermute | solution.py:388
  40.0 0.0 copy-done.1
  40.0 0.0 copy-done
  40.0 0.6 copy-done.5
  40.6 11.4 %step0.1 = (f32[16,256]{1,0:T(8,128)}, bf16[16,256]{1,0:T(8,128)(2,1)}) custom-call(s32[1]{0:T(128)} %copy.15.width_ref.refs_0_, f32[3]{0:T(128)} %refs_1_.1, f32[16,256]{1,0:T(8,128)} %copy-done.1, bf16[160,256]{1,0:T(8,128)(2,1)} %copy-done.4, bf16[160,256]{1,0:T(8,128)(2,1)} %copy-done.4, bf16[160,256]{1,0:T(8,128)(2,1)} %copy-done.5, ...), custom_call_target="tpu_custom_call" | custom-call | flops 4026531840 | bytes 1048576 | tf_op jit(solution)/shard_map/step0/pallas_call | solution.py:418
  52.0 1.9 %collective-permute-start.4 = (bf16[16,256]{1,0:T(8,128)(2,1)}, bf16[16,256]{1,0:T(8,128)(2,1)S(1)}, u32[]{:S(2)}, u32[]{:S(2)}) collective-permute-start(bf16[16,256]{1,0:T(8,128)(2,1)} %get-tuple-element.20), channel_id=1, source_target_pairs={{0,2},{1,3},{2,4},{3,5},{4,6},{5,7},{6,8},{7,9},{8,10},{9,11},{10,... | collective-permute-start | bytes 24584 | tf_op jit(solution)/shard_map/ppermute | solution.py:388
  53.9 1.9 %collective-permute-start.5 = (bf16[16,256]{1,0:T(8,128)(2,1)}, bf16[16,256]{1,0:T(8,128)(2,1)S(1)}, u32[]{:S(2)}, u32[]{:S(2)}) collective-permute-start(bf16[16,256]{1,0:T(8,128)(2,1)} %get-tuple-element.20), channel_id=1, source_target_pairs={{0,1},{1,2},{2,3},{3,4},{4,5},{5,6},{6,7},{7,8},{8,9},{9,10},{10,1... | collective-permute-start | bytes 24584 | tf_op jit(solution)/shard_map/ppermute | solution.py:388
  55.9 7.6 %collective-permute-start.6 = (bf16[16,256]{1,0:T(8,128)(2,1)}, bf16[16,256]{1,0:T(8,128)(2,1)S(1)}, u32[]{:S(2)}, u32[]{:S(2)}) collective-permute-start(bf16[16,256]{1,0:T(8,128)(2,1)} %get-tuple-element.20), channel_id=1, source_target_pairs={{0,63},{1,0},{2,1},{3,2},{4,3},{5,4},{6,5},{7,6},{8,7},{9,8},{10,9... | collective-permute-start | bytes 24584 | tf_op jit(solution)/shard_map/ppermute | solution.py:388
  63.5 5.0 %collective-permute-start.7 = (bf16[16,256]{1,0:T(8,128)(2,1)}, bf16[16,256]{1,0:T(8,128)(2,1)S(1)}, u32[]{:S(2)}, u32[]{:S(2)}) collective-permute-start(bf16[16,256]{1,0:T(8,128)(2,1)} %get-tuple-element.20), channel_id=1, source_target_pairs={{0,62},{1,63},{2,0},{3,1},{4,2},{5,3},{6,4},{7,5},{8,6},{9,7},{10,... | collective-permute-start | bytes 24584 | tf_op jit(solution)/shard_map/ppermute | solution.py:388
  68.5 0.0 collective-permute-done.4.refs_3_
  68.5 0.0 collective-permute-done.5.refs_4_
  68.5 0.0 copy-start.7
  68.5 0.0 collective-permute-done.6.refs_5_
  68.6 1.6 %collective-permute-done.7.refs_6_ = bf16[16,256]{1,0:T(8,128)(2,1)S(1)} collective-permute-done((bf16[16,256]{1,0:T(8,128)(2,1)}, bf16[16,256]{1,0:T(8,128)(2,1)S(1)}, u32[]{:S(2)}, u32[]{:S(2)}) %collective-permute-start.7) | collective-permute-done | bytes 8224 | tf_op jit(solution)/shard_map/ppermute | solution.py:388
  70.1 0.0 copy-done.8
  70.2 0.6 copy-done.9
  70.7 11.3 %step1.1 = f32[4,4,256]{2,1,0:T(4,128)} custom-call(s32[1]{0:T(128)} %copy.15.width_ref.refs_0_, f32[3]{0:T(128)} %refs_1_.1, f32[16,256]{1,0:T(8,128)} %get-tuple-element.19.refs_2_, bf16[16,256]{1,0:T(8,128)(2,1)} %copy-done.6, bf16[16,256]{1,0:T(8,128)(2,1)} %copy-done.7, bf16[16,256]{1,0:T(8,128)(2,1)} %copy-done.8, bf16[16,256]{1,0:T(8,128)(2,1)} %copy-done.9, ...), custom_call_target="tpu_custom_call" | custom-call | flops 4026531840 | bytes 1048576 | tf_op jit(solution)/shard_map/step1/pallas_call | solution.py:418
  (16 shorter events, 0.1 us)
Async XLA Ops:
  0.0 15.5 %copy-start.2 = (f32[1,4,4,256]{3,2,1,0:T(4,128)S(1)}, f32[1,4,4,256]{3,2,1,0:T(4,128)}, u32[]{:S(2)}) copy-start(f32[1,4,4,256]{3,2,1,0:T(4,128)} %param.17) | copy-start | bytes 49156
  0.0 15.5 %copy-start.3 = (f32[3]{0:T(128)S(1)}, f32[3]{0:T(128)}, u32[]{:S(2)}) copy-start(f32[3]{0:T(128)} %refs_1_.1) | copy-start | bytes 40
  5.5 22.8 %all-to-all-start = ((bf16[8,128,256]{2,1,0:T(8,128)(2,1)}), bf16[8,128,256]{2,1,0:T(8,128)(2,1)S(1)}, u32[]{:S(2)}, u32[]{:S(2)}) async-start(bf16[8,128,256]{2,1,0:T(8,128)(2,1)} %encode.1), calls=%async_computation | async-start | bytes 1048576 | tf_op jit(solution)/shard_map/all_to_all | solution.py:470
  15.5 24.4 %copy-start.1 = (f32[16,256]{1,0:T(8,128)}, f32[16,256]{1,0:T(8,128)S(1)}, u32[]{:S(2)}) copy-start(f32[16,256]{1,0:T(8,128)S(1)} %reshape.11.own) | copy-start | bytes 49156
  15.7 11.3 %collective-permute-start = (bf16[16,256]{1,0:T(8,128)(2,1)S(1)}, bf16[16,256]{1,0:T(8,128)(2,1)S(1)}, u32[]{:S(2)}, u32[]{:S(2)}) collective-permute-start(bf16[16,256]{1,0:T(8,128)(2,1)S(1)} %multiply_convert_fusion.1), channel_id=1, source_target_pairs={{0,1},{1,2},{2,3},{3,4},{4,5},{5,6},{6,7},{7,8},{8,9},{9,10},{10,1... | collective-permute-start | bytes 24584 | tf_op jit(solution)/shard_map/ppermute | solution.py:388
  17.6 10.7 %collective-permute-start.1 = (bf16[16,256]{1,0:T(8,128)(2,1)S(1)}, bf16[16,256]{1,0:T(8,128)(2,1)S(1)}, u32[]{:S(2)}, u32[]{:S(2)}) collective-permute-start(bf16[16,256]{1,0:T(8,128)(2,1)S(1)} %multiply_convert_fusion.1), channel_id=1, source_target_pairs={{0,63},{1,0},{2,1},{3,2},{4,3},{5,4},{6,5},{7,6},{8,7},{9,8},{10,9... | collective-permute-start | bytes 24584 | tf_op jit(solution)/shard_map/ppermute | solution.py:388
  28.4 11.5 %copy-start = (bf16[128,256]{1,0:T(8,128)(2,1)}, bf16[128,256]{1,0:T(8,128)(2,1)S(1)}, u32[]{:S(2)}) copy-start(bf16[128,256]{1,0:T(8,128)(2,1)S(1)} %multiply_convert_fusion.cond_own.refs_8_) | copy-start | bytes 196612
  28.5 9.9 %collective-permute-start.2 = (bf16[160,256]{1,0:T(8,128)(2,1)S(1)}, bf16[160,256]{1,0:T(8,128)(2,1)S(1)}, u32[]{:S(2)}, u32[]{:S(2)}) collective-permute-start(bf16[160,256]{1,0:T(8,128)(2,1)S(1)} %get-tuple-element.22), channel_id=1, source_target_pairs={{0,1},{1,2},{2,3},{3,4},{4,5},{5,6},{6,7},{7,8},{8,9},{9,10},{10,1... | collective-permute-start | bytes 245768 | tf_op jit(solution)/shard_map/ppermute | solution.py:388
  30.4 9.6 %collective-permute-start.3 = (bf16[160,256]{1,0:T(8,128)(2,1)S(1)}, bf16[160,256]{1,0:T(8,128)(2,1)S(1)}, u32[]{:S(2)}, u32[]{:S(2)}) collective-permute-start(bf16[160,256]{1,0:T(8,128)(2,1)S(1)} %get-tuple-element.21), channel_id=1, source_target_pairs={{0,63},{1,0},{2,1},{3,2},{4,3},{5,4},{6,5},{7,6},{8,7},{9,8},{10,9... | collective-permute-start | bytes 245768 | tf_op jit(solution)/shard_map/ppermute | solution.py:388
  38.4 1.6 %copy-start.4 = (bf16[160,256]{1,0:T(8,128)(2,1)}, bf16[160,256]{1,0:T(8,128)(2,1)S(1)}, u32[]{:S(2)}) copy-start(bf16[160,256]{1,0:T(8,128)(2,1)S(1)} %collective-permute-done.2.up2.up1.cond_up.refs_7_) | copy-start | bytes 245764
  40.0 0.6 copy-start.5
  52.0 16.5 %collective-permute-start.4 = (bf16[16,256]{1,0:T(8,128)(2,1)}, bf16[16,256]{1,0:T(8,128)(2,1)S(1)}, u32[]{:S(2)}, u32[]{:S(2)}) collective-permute-start(bf16[16,256]{1,0:T(8,128)(2,1)} %get-tuple-element.20), channel_id=1, source_target_pairs={{0,2},{1,3},{2,4},{3,5},{4,6},{5,7},{6,8},{7,9},{8,10},{9,11},{10,... | collective-permute-start | bytes 24584 | tf_op jit(solution)/shard_map/ppermute | solution.py:388
  53.9 14.6 %collective-permute-start.5 = (bf16[16,256]{1,0:T(8,128)(2,1)}, bf16[16,256]{1,0:T(8,128)(2,1)S(1)}, u32[]{:S(2)}, u32[]{:S(2)}) collective-permute-start(bf16[16,256]{1,0:T(8,128)(2,1)} %get-tuple-element.20), channel_id=1, source_target_pairs={{0,1},{1,2},{2,3},{3,4},{4,5},{5,6},{6,7},{7,8},{8,9},{9,10},{10,1... | collective-permute-start | bytes 24584 | tf_op jit(solution)/shard_map/ppermute | solution.py:388
  55.9 12.7 %collective-permute-start.6 = (bf16[16,256]{1,0:T(8,128)(2,1)}, bf16[16,256]{1,0:T(8,128)(2,1)S(1)}, u32[]{:S(2)}, u32[]{:S(2)}) collective-permute-start(bf16[16,256]{1,0:T(8,128)(2,1)} %get-tuple-element.20), channel_id=1, source_target_pairs={{0,63},{1,0},{2,1},{3,2},{4,3},{5,4},{6,5},{7,6},{8,7},{9,8},{10,9... | collective-permute-start | bytes 24584 | tf_op jit(solution)/shard_map/ppermute | solution.py:388
  63.5 6.7 %collective-permute-start.7 = (bf16[16,256]{1,0:T(8,128)(2,1)}, bf16[16,256]{1,0:T(8,128)(2,1)S(1)}, u32[]{:S(2)}, u32[]{:S(2)}) collective-permute-start(bf16[16,256]{1,0:T(8,128)(2,1)} %get-tuple-element.20), channel_id=1, source_target_pairs={{0,62},{1,63},{2,0},{3,1},{4,2},{5,3},{6,4},{7,5},{8,6},{9,7},{10,... | collective-permute-start | bytes 24584 | tf_op jit(solution)/shard_map/ppermute | solution.py:388
  68.5 1.6 %copy-start.6 = (bf16[16,256]{1,0:T(8,128)(2,1)}, bf16[16,256]{1,0:T(8,128)(2,1)S(1)}, u32[]{:S(2)}) copy-start(bf16[16,256]{1,0:T(8,128)(2,1)S(1)} %collective-permute-done.4.refs_3_) | copy-start | bytes 24580
  68.5 1.6 %copy-start.7 = (bf16[16,256]{1,0:T(8,128)(2,1)}, bf16[16,256]{1,0:T(8,128)(2,1)S(1)}, u32[]{:S(2)}) copy-start(bf16[16,256]{1,0:T(8,128)(2,1)S(1)} %collective-permute-done.5.refs_4_) | copy-start | bytes 24580
  68.5 1.6 %copy-start.8 = (bf16[16,256]{1,0:T(8,128)(2,1)}, bf16[16,256]{1,0:T(8,128)(2,1)S(1)}, u32[]{:S(2)}) copy-start(bf16[16,256]{1,0:T(8,128)(2,1)S(1)} %collective-permute-done.6.refs_5_) | copy-start | bytes 24580
  70.1 0.6 copy-start.9

commit v5 on v4

v5 whole, which is shorter than its diff:
```python
import functools
import math

import jax
import jax.numpy as jnp
from jax import lax
from jax.experimental import pallas as pl
from jax.experimental.pallas import tpu as pltpu
from jax.sharding import PartitionSpec as P

K = 96
SIGMA_DATA = 0.5
BF = jnp.bfloat16
F32 = jnp.float32
HALF = 128
ROWS = 256
NT = (((1,), (1,)), ((), ()))
TN = (((0,), (0,)), ((), ()))

BLOCKS = (5, 5, 3, 2)
SCALED = (-7, 17)
FIRST = (-6, 15)
SECOND = (-5, 13)
THIRD = (-2, 6)
FOURTH = (-1, 4)
FIFTH = (-1, 6)


def silu_twice(h):
    return h + h * jnp.tanh(h)


def dot_nt(a, b):
    return lax.dot_general(a, b, NT, preferred_element_type=F32)


def levels(sigma_ref, step):
    now = jnp.full((1, 256), sigma_ref[step], F32)
    after = jnp.full((1, 256), sigma_ref[step + 1], F32)
    var = now * now + SIGMA_DATA * SIGMA_DATA
    root = jnp.sqrt(var)
    return now, 1.0 / root, SIGMA_DATA * SIGMA_DATA / var, now * SIGMA_DATA / root, (after - now) / now


def encode_kernel(
    anchor_ref, width_ref, sigma_ref, blocks_ref, w_ref, noise_ref, out_ref, state_ref, scaled_ref, enc_ref, flat, wide
):
    band = lax.axis_index("band")
    tile = lax.axis_index("tile")
    count = blocks_ref.shape[0]
    cells = enc_ref.shape[1]
    chans = w_ref.shape[0]
    tiles = blocks_ref.shape[1] // 128
    group = 8 * tiles

    flat[count * tiles :, :] = jnp.zeros((flat.shape[0] - count * tiles, 128), F32)
    for g in range(count // 16):
        for t in range(tiles):
            v = blocks_ref[16 * g : 16 * g + 16, 128 * t : 128 * t + 128].astype(F32)
            flat[2 * g * group + 8 * t : 2 * g * group + 8 * t + 8, :] = v[:8]
            flat[(2 * g + 1) * group + 8 * t : (2 * g + 1) * group + 8 * t + 8, :] = v[8:]

    sigma, scale = levels(sigma_ref, 0)[:2]
    natural = (lax.broadcasted_iota(jnp.int32, (4, 256), 1) < width_ref[0]).astype(F32)
    for r in range(4):
        row = sigma * noise_ref[:, r, :] * natural
        state_ref[4 * r : 4 * r + 4, :] = row
        scaled_ref[4 * r : 4 * r + 4, :] = (row * scale).astype(BF)

    w = 0.5 * w_ref[...].astype(F32)
    for half in range(2):
        wide[half, 0:chans, :] = w[:, 128 * half : 128 * half + 128]
        wide[half, chans:80, :] = jnp.zeros((80 - chans, 128), F32)
    weight = jnp.concatenate(
        [
            jnp.concatenate([wide[half, pl.ds(odd, 40, stride=2), :] for half in range(2)], 1)
            for odd in range(2)
        ],
        0,
    ).astype(BF)
    first = lax.broadcasted_iota(jnp.int32, (40, 128), 1) < 64

    def encode(g, carry):
        begin = pl.multiple_of(g * group, 8)
        cols = []
        for k in range(4):
            one = flat[pl.ds(begin + 2 * k, 40, stride=8), :]
            two = flat[pl.ds(begin + 2 * k + 1, 40, stride=8), :]
            even = jnp.where(first, one, pltpu.roll(two, 64, 1))
            odd = jnp.where(first, pltpu.roll(one, 64, 1), two)
            cols.append(jnp.concatenate([even, odd], 0))
        x = jnp.concatenate(cols, 1).astype(BF)
        v = lax.dot_general(x, weight, TN, preferred_element_type=F32)
        v = silu_twice(v).astype(BF).astype(F32)
        enc_ref[pl.ds(g * 8, 8)] = v.reshape(8, cells, 256)
        return carry

    lax.fori_loop(0, count // 8, encode, 0, unroll=True)

    enc_ref[pl.ds(count, 8)] = enc_ref[pl.ds(0, 8)]

    def window(k, carry):
        nest = k // 2
        part = k % 2
        anchor = anchor_ref[nest, tile]
        begin = anchor + (band - anchor + 512) % 8 + part * 48
        row = (begin % 512) // 8
        total = enc_ref[row]
        for m in range(1, 6):
            total = total + enc_ref[row + m]
        out_ref[nest, pl.ds(pl.multiple_of(part * cells, cells), cells), :] = total.astype(BF)
        return carry

    lax.fori_loop(0, 16, window, 0, unroll=4)


def pair_weight(w, a):
    zero = jnp.zeros_like(w(a, 0))
    own = jnp.concatenate(
        [jnp.concatenate([w(a, 1), w(a, 2)], 1), jnp.concatenate([w(a, 0), w(a, 1)], 1)], 0
    )
    rim = jnp.concatenate(
        [jnp.concatenate([w(a, 0), zero], 1), jnp.concatenate([zero, w(a, 2)], 1)], 0
    )
    return own, rim


def form_small(w_in, w_out, in_o, out_o):
    half = jnp.asarray(0.5, BF)

    def tall(ref, a, b):
        if not 0 <= b <= 2:
            return jnp.zeros((8, 128), F32)
        return jnp.concatenate([ref[3 * a + b].astype(F32), jnp.zeros((4, 128), F32)], 0)

    in_o[...] = jnp.concatenate(
        [
            jnp.concatenate([tall(w_in, a, q - p) for p in range(2)], 1)
            for a in range(3)
            for q in range(4)
        ],
        0,
    ).astype(BF)
    in_o[...] = in_o[...] * half
    out_o[...] = jnp.concatenate(
        [
            jnp.concatenate([tall(w_out, a, q - p) for q in (1, 2, 0, 3)], 1)
            for a in range(3)
            for p in range(2)
        ],
        0,
    ).astype(BF)


def form_pairs(w, chans, out):
    half = jnp.asarray(0.5, BF)
    for a in range(3):
        own, rim = pair_weight(lambda i, b: w[3 * i + b][:, 0:chans] * half, a)
        out[:, 512 * a : 512 * a + 256] = own
        out[:, 512 * a + 256 : 512 * a + 512] = rim


def form_down(w, out):
    half = jnp.asarray(0.5, BF)
    for a in range(3):
        out[:, 256 * a : 256 * a + 128] = w[3 * a + 1] * half
        out[:, 256 * a + 128 : 256 * a + 256] = w[3 * a + 2] * half
        out[:, 768 + 128 * a : 896 + 128 * a] = w[3 * a] * half


def form_mid(w, out):
    half = jnp.asarray(0.5, BF)
    for a in range(3):
        for b in range(3):
            out[:, 768 * a + 256 * b : 768 * a + 256 * b + 256] = w[3 * a + b] * half


def form_up(w, even, odd):
    def up(a, b):
        return 0.5 * w[3 * a + b][:, 128:384].astype(F32)

    for out, sets in ((even, ((0,), (1, 2))), (odd, ((0, 1), (2,)))):
        for k, taps in enumerate(sets):
            col = [sum(up(a, b) for a in taps) for b in range(3)]
            zero = jnp.zeros_like(col[0])
            out[:, 768 * k : 768 * k + 256] = jnp.concatenate([col[0], zero], 0).astype(BF)
            out[:, 768 * k + 256 : 768 * k + 512] = jnp.concatenate(
                [col[1] + col[2], col[0] + col[1]], 0
            ).astype(BF)
            out[:, 768 * k + 512 : 768 * k + 768] = jnp.concatenate([zero, col[2]], 0).astype(BF)


def parts(total, most):
    count = -(-total // most)
    cuts = [total * i // count for i in range(count + 1)]
    return [(a, b - a) for a, b in zip(cuts, cuts[1:])]


class Field:
    def __init__(self, width, masks):
        self.tile = lax.axis_index("tile")
        self.masks = masks
        lane = lax.broadcasted_iota(jnp.int32, (HALF, 256), 1)
        pair = lax.broadcasted_iota(jnp.int32, (HALF, 256), 0)
        masks[0] = jnp.zeros((HALF, 256), F32)
        masks[1] = (2 * pair + lane // 128 < width).astype(F32)
        masks[2] = (2 * pair < width).astype(F32)
        self.natural = (lax.broadcasted_iota(jnp.int32, (4, 256), 1) < width).astype(F32)

    def fine_ok(self, rho):
        row = self.tile * 4 + rho
        return jnp.logical_and(row >= 0, row < ROWS).astype(jnp.int32)

    def half_ok(self, h):
        row = self.tile * 2 + h
        return jnp.logical_and(row >= 0, row < ROWS // 2).astype(jnp.int32)

    def keep_pairs(self, y, center, rim, at, rho):
        y = y * self.masks[self.fine_ok(rho)]
        center[at] = y.astype(BF)
        rim[at] = jnp.concatenate([slide(y[:, 128:], 1), slide(y[:, :128], -1)], 1).astype(BF)

    def keep_half(self, y, center, left, right, at, h):
        y = y * self.masks[2 * self.half_ok(h)]
        center[at] = y.astype(BF)
        left[at] = slide(y, 1).astype(BF)
        right[at] = slide(y, -1).astype(BF)


def embedding(w_sigma, now):
    return jnp.concatenate([w_sigma[...], w_sigma[...]], 1) * jnp.log(now)


def slide(x, by):
    x = pltpu.roll(x, by % HALF, 0)
    where = lax.broadcasted_iota(jnp.int32, (8, x.shape[1]), 0)
    if by == 1:
        return jnp.concatenate([jnp.where(where == 0, 0.0, x[:8]), x[8:]], 0)
    return jnp.concatenate([x[: HALF - 8], jnp.where(where == 7, 0.0, x[HALF - 8 :])], 0)


def stacked(ref, at, n, step=1):
    return jnp.concatenate([ref[at + step * k] for k in range(n)], 0)


def step_kernel(
    step, width_ref, sigma_ref, own, halo, cond_up, cond_own, cond_down, weights, state_ref, scaled_ref,
    scaled, spread, firstc, firste, secondc, seconde, third, thirdl, thirdr, fourth, fourthl, fourthr,
    fifthc, fifthe, prod, picked, masks,
    f_in, f_out, f_enc, f_down, f_mid, f_dec, f_even, f_odd,
):
    w_sigma, w_in, w_out, w_enc, w_down, w_mid, w_dec = weights
    field = Field(width_ref[0], masks)
    sigma, scale, keep, mix, move = levels(sigma_ref, step)

    empty = jnp.zeros((4, 256), F32)
    scaled_lo = SCALED[0]
    for tile_off, ref, begin in halo:
        value = ref[begin : begin + 16, :].astype(F32)
        for r in range(4):
            rho = 4 * tile_off + r
            if scaled_lo <= rho < scaled_lo + SCALED[1]:
                row = jnp.concatenate([value[4 * r : 4 * r + 4], empty], 0)
                scaled[8 * (rho - scaled_lo) : 8 * (rho - scaled_lo) + 8, :] = row * field.fine_ok(rho).astype(F32)
    states = [own[4 * r : 4 * r + 4, :] for r in range(4)]
    for r in range(4):
        row = jnp.concatenate([(states[r] * scale).astype(BF).astype(F32), empty], 0)
        scaled[8 * (r - scaled_lo) : 8 * (r - scaled_lo) + 8, :] = row

    form_small(w_in, w_out, f_in, f_out)

    col = lax.broadcasted_iota(jnp.int32, (256, 512), 0)
    place = lax.broadcasted_iota(jnp.int32, (256, 512), 1)
    pick = (col == 2 * (place % 128) + place // 128 - 1).astype(F32).astype(BF)
    spread[...] = jnp.dot(scaled[...].astype(BF), pick, preferred_element_type=F32)
    bias = 0.5 * embedding(w_sigma, sigma)
    for at, n in parts(FIRST[1], BLOCKS[0]):
        cols = [
            jnp.concatenate(
                [spread[8 * (k + a) : 8 * (k + a) + 8, 128 * q : 128 * q + 128] for a in range(3) for q in range(4)],
                0,
            )
            for k in range(at, at + n)
        ]
        x = jnp.concatenate(cols, 1).astype(BF)
        y = lax.dot_general(x, f_in[...], TN, preferred_element_type=F32)
        for k in range(n):
            part = silu_twice(y[k * HALF : (k + 1) * HALF] + bias)
            field.keep_pairs(part, firstc, firste, at + k, FIRST[0] + at + k)

    form_pairs(w_enc, 128, f_enc)
    for at, n in parts(SECOND[1], BLOCKS[1]):
        x = jnp.concatenate([stacked(ref, at + a, n) for a in range(3) for ref in (firstc, firste)], 1)
        y = dot_nt(x, f_enc[...])
        for k in range(n):
            part = silu_twice(y[k * HALF : (k + 1) * HALF])
            field.keep_pairs(part, secondc, seconde, at + k, SECOND[0] + at + k)

    form_down(w_down, f_down)
    repeat = (
        lax.broadcasted_iota(jnp.int32, (HALF, 64), 0) // 2 == lax.broadcasted_iota(jnp.int32, (HALF, 64), 1)
    ).astype(F32)
    repeat = (0.5 * repeat).astype(BF)
    add = [
        jnp.dot(repeat, ref[64 * r : 64 * r + 64, :], preferred_element_type=F32)
        for ref in (cond_up, cond_own, cond_down)
        for r in range(2)
    ]
    for at, n in parts(THIRD[1], BLOCKS[2]):
        begin = 2 * (THIRD[0] + at) - 1 - SECOND[0]
        x = jnp.concatenate(
            [stacked(secondc, begin + a, n, 2) for a in range(3)]
            + [jnp.concatenate([seconde[begin + a + 2 * k][:, :128] for k in range(n)], 0) for a in range(3)],
            1,
        )
        y = dot_nt(x, f_down[...])
        for k in range(n):
            part = silu_twice(y[k * HALF : (k + 1) * HALF] + add[at + k])
            field.keep_half(part, third, thirdl, thirdr, at + k, THIRD[0] + at + k)

    form_mid(w_mid, f_mid)
    for at, n in parts(FOURTH[1], BLOCKS[3]):
        x = jnp.concatenate(
            [stacked(ref, at + a, n) for a in range(3) for ref in (thirdl, third, thirdr)], 1
        )
        y = dot_nt(x, f_mid[...])
        for k in range(n):
            part = silu_twice(y[k * HALF : (k + 1) * HALF])
            field.keep_half(part, fourth, fourthl, fourthr, at + k, FOURTH[0] + at + k)

    form_pairs(w_dec, 128, f_dec)
    form_up(w_dec, f_even, f_odd)
    for at in range(2):
        rho = FIFTH[0] + at
        odd = rho % 2
        n = FIFTH[1] // 2
        begin = rho - 1 - SECOND[0]
        h = (rho - odd) // 2 - FOURTH[0] - (0 if odd else 1)
        x = jnp.concatenate(
            [stacked(ref, begin + a, n, 2) for a in range(3) for ref in (secondc, seconde)], 1
        )
        z = jnp.concatenate(
            [stacked(ref, h + a, n) for a in range(2) for ref in (fourthl, fourth, fourthr)], 1
        )
        y = dot_nt(x, f_dec[...]) + dot_nt(z, (f_odd if odd else f_even)[...])
        for k in range(n):
            part = silu_twice(y[k * HALF : (k + 1) * HALF])
            field.keep_pairs(part, fifthc, fifthe, at + 2 * k, FIFTH[0] + at + 2 * k)

    n = FIFTH[1]
    x = jnp.concatenate([stacked(fifthc, 0, n), stacked(fifthe, 0, n)], 1)
    prod[...] = dot_nt(f_out[...], x)
    for k in range(4):
        for p in range(2):
            picked[8 * k : 8 * k + 8, HALF * p : HALF * p + HALF] = sum(
                prod[16 * a + 8 * p : 16 * a + 8 * p + 8, (k + a) * HALF : (k + a + 1) * HALF]
                for a in range(3)
            )
    high = picked[...].astype(BF)
    low = (picked[...] - high.astype(F32)).astype(BF)
    weave_j = lax.broadcasted_iota(jnp.int32, (256, 256), 0)
    weave_c = lax.broadcasted_iota(jnp.int32, (256, 256), 1)
    weave = (weave_c == 2 * (weave_j % HALF) + weave_j // HALF).astype(F32).astype(BF)
    net = jnp.dot(high, weave, preferred_element_type=F32) + jnp.dot(low, weave, preferred_element_type=F32)
    for r in range(4):
        denoised = keep * states[r] + mix * net[8 * r : 8 * r + 4]
        now = (states[r] + move * (states[r] - denoised)) * field.natural
        if step == 0:
            state_ref[4 * r : 4 * r + 4, :] = now
            scaled_ref[4 * r : 4 * r + 4, :] = (now * levels(sigma_ref, 1)[1]).astype(BF)
        else:
            state_ref[:, r, :] = now


def turn(x, by):
    n = lax.axis_size("tile")
    return lax.ppermute(x, "tile", [(i, (i + by) % n) for i in range(n)])


VMEM = pl.BlockSpec(memory_space=pltpu.VMEM)
SMEM = pl.BlockSpec(memory_space=pltpu.SMEM)


LIMIT = 20


def limit(mib):
    return pltpu.CompilerParams(vmem_limit_bytes=mib << 20)


def rowbuf(n):
    return pltpu.VMEM((n, HALF, 256), BF)


def cost(passes):
    return pl.CostEstimate(flops=passes * 128 * 65536 * 2, bytes_accessed=1 << 20, transcendentals=0)


def step_call(step, width, sigmas, own, pieces, conds, weights):
    distinct = list(conds)
    for array, _ in pieces:
        if not any(array is d for d in distinct):
            distinct.append(array)
    place = [next(i for i, d in enumerate(distinct) if d is array) for array, _ in pieces]
    outs = [jax.ShapeDtypeStruct((16, 256), F32), jax.ShapeDtypeStruct((16, 256), BF)]
    if step == 1:
        outs = [jax.ShapeDtypeStruct((4, 4, 256), F32)]
    n_arrays, n_weights = len(distinct), len(weights)

    def kernel(width_ref, sigma_ref, own_ref, *refs):
        arrays, refs = refs[:n_arrays], refs[n_arrays:]
        weight_refs, refs = refs[:n_weights], refs[n_weights:]
        out_refs, refs = list(refs[: len(outs)]), refs[len(outs) :]
        halo = [(off, arrays[place[i]], pieces[i][1]) for i, off in enumerate((-2, -1, 1, 2))]
        step_kernel(
            step, width_ref, sigma_ref, own_ref, halo, *arrays[:3], weight_refs,
            *(out_refs + [None])[:2], *refs,
        )

    return pl.pallas_call(
        kernel,
        out_shape=outs,
        in_specs=[SMEM, SMEM] + [VMEM] * (1 + n_arrays + n_weights),
        out_specs=[VMEM] * len(outs),
        scratch_shapes=[
            pltpu.VMEM((SCALED[1] * 8, 256), F32), pltpu.VMEM((SCALED[1] * 8, 512), F32),
            rowbuf(FIRST[1]), rowbuf(FIRST[1]), rowbuf(SECOND[1]), rowbuf(SECOND[1]),
            *[rowbuf(THIRD[1])] * 3, *[rowbuf(FOURTH[1])] * 3, *[rowbuf(FIFTH[1])] * 2,
            pltpu.VMEM((48, FIFTH[1] * HALF), F32), pltpu.VMEM((32, 256), F32), pltpu.VMEM((3, HALF, 256), F32),
            *[
                pltpu.VMEM(shape, BF)
                for shape in (
                    (96, 256), (48, 512), (256, 1536), (256, 1152), (256, 2304),
                    (256, 1536), (256, 1536), (256, 1536),
                )
            ],
        ],
        compiler_params=limit(LIMIT),
        cost_estimate=cost(240),
        name="step" + str(step),
    )(width, sigmas, own, *distinct, *weights)


def encode_call(block_anchor, nest_width, sigmas, coarse_blocks, w_context, noise):
    chans = w_context.shape[1]
    cells = coarse_blocks.shape[1] // chans
    count = coarse_blocks.shape[0]
    tiles = coarse_blocks.shape[1] // 128
    return pl.pallas_call(
        encode_kernel,
        out_shape=[
            jax.ShapeDtypeStruct((8, 2 * cells, 256), BF),
            jax.ShapeDtypeStruct((16, 256), F32),
            jax.ShapeDtypeStruct((16, 256), BF),
        ],
        in_specs=[SMEM, SMEM, SMEM, VMEM, VMEM, VMEM],
        out_specs=[VMEM] * 3,
        scratch_shapes=[
            pltpu.VMEM((count + 8, cells, 256), F32),
            pltpu.VMEM((count * tiles + 64, 128), F32),
            pltpu.VMEM((2, 80, 128), F32),
        ],
        compiler_params=limit(56),
        cost_estimate=cost(100),
        name="encode",
    )(block_anchor, nest_width, sigmas, coarse_blocks, w_context.T, noise)


def per_device(
    coarse_blocks, block_anchor, nest_width, sigmas, noise,
    w_context, w_in, w_sigma, w_enc, w_down, w_mid, w_dec, w_out,
):
    partial, state, scaled = encode_call(block_anchor, nest_width, sigmas, coarse_blocks, w_context, noise[0])
    arrived = lax.all_to_all(partial, "band", 0, 0, tiled=True)

    up = turn(scaled, 1)
    down = turn(scaled, -1)
    arrived, up, down = lax.optimization_barrier((arrived, up, down))

    cond = (jnp.sum(arrived.astype(F32), axis=0) * (1.0 / math.sqrt(K // 2))).astype(BF)
    near_up = turn(jnp.concatenate([cond, up, scaled], 0), 1)
    near_down = turn(jnp.concatenate([cond, scaled, down], 0), -1)
    conds = (near_up, cond, near_down)
    weights = (w_sigma.reshape(1, -1), w_in.transpose(0, 2, 1), w_out, w_enc, w_down, w_mid, w_dec)
    pieces = ((near_up, 128), (near_up, 144), (near_down, 128), (near_down, 144))
    state, scaled = step_call(0, nest_width, sigmas, state, pieces, conds, weights)
    pieces = tuple((turn(scaled, by), 0) for by in (2, 1, -1, -2))
    (out,) = step_call(1, nest_width, sigmas, state, pieces, conds, weights)
    return out[None]


def solution(mesh):
    return jax.shard_map(
        per_device,
        mesh=mesh,
        in_specs=(
            P("band", None), P(), P("band"), P(), P("band", None, "tile", None),
            P(), P(), P(), P(), P(), P(), P(), P(),
        ),
        out_specs=P("band", None, "tile", None),
        check_vma=False,
    )
```

time: 82.7 us -> 75.7 us (0.915)
  waiting for transfers between devices: 4.97 us -> 17.8 us
  Pallas kernels: 28.3 us -> 16.5 us
  starting transfers between devices: 46.5 us -> 39.2 us
  local copies, waits for them, and re-layouts: 1.24 us -> 0.04 us
    ppermute x8, waiting for transfers between devices: 4.96 us -> 17.8 us  [turn(): return lax.ppermute(x, 'tile', [(i, (i + by) % n) for i in range(n)])]
    pallas_call x3, Pallas kernels: 28.3 us -> 16.5 us  [the longest x2 12.8 us: step_call(): pl.pallas_call(kernel, out_shape=outs, in_specs=[SMEM, SMEM] + [VMEM] * (...]
    ppermute x8, starting transfers between devices: 37.2 us -> 29.7 us  [turn(): return lax.ppermute(x, 'tile', [(i, (i + by) % n) for i in range(n)])]
    unnamed x20 -> x18, local copies, waits for them, and re-layouts: 1.22 us -> 0.04 us
  transfers between devices with their start and end apart: 9 -> 9, of which waited for: 4 -> 5; matrix products, arithmetic and copies ran while one was open for 0% -> 0% of each run, Pallas kernels for 0% -> 0%
where the time goes in v5:
time: 75.7 us; the launch traced here: 75.2 us
  starting transfers between devices  39.2 us (52%)
  waiting for transfers between devices  17.8 us (24%)
  Pallas kernels  16.5 us (22%)
  other arithmetic  0.87 us (1%)
  between operations  0.87 us (1%)
    ppermute x8, starting transfers between devices, turn(): return lax.ppermute(x, 'tile', [(i, (i + by) % n) for i in range(n)])  29.7 us
    ppermute x8, waiting for transfers between devices, turn(): return lax.ppermute(x, 'tile', [(i, (i + by) % n) for i in range(n)])  17.8 us
    pallas_call x2, Pallas kernels, step_call(): pl.pallas_call(kernel, out_shape=outs, in_specs=[SMEM, SMEM] + [VMEM] * (...  12.8 us
    all_to_all x1, starting transfers between devices, per_device(): arrived = lax.all_to_all(partial, 'band', 0, 0, tiled=True)  9.46 us
    pallas_call x1, Pallas kernels, encode_call(): pl.pallas_call(encode_kernel, out_shape=[jax.ShapeDtypeStruct((8, 2 * cel...  3.72 us
  transfers between devices with their start and end apart: 9, of which 5 were waited for; matrix products, arithmetic and copies ran while one was open for 0% of the time, Pallas kernels for 0%

profile of v5, /device:TPU:2, one launch (start us, length us, event | category | flops | bytes accessed | tf_op | source)
XLA Modules:
  0.0 75.2 jit_solution(3868734511957527916)
XLA Ops:
  0.7 0.0 copy-start.2
  0.7 0.0 copy-start.3
  0.7 3.7 %encode.1 = (bf16[8,128,256]{2,1,0:T(8,128)(2,1)}, f32[16,256]{1,0:T(8,128)}, bf16[16,256]{1,0:T(8,128)(2,1)}) custom-call(s32[8,64]{1,0:T(8,128)} %anchor_ref.1, s32[1]{0:T(128)S(6)} %copy.14.width_ref, f32[3]{0:T(128)} %sigma_ref.5, bf16[64,4480]{1,0:T(8,128)(2,1)} %blocks_ref.1, bf16[70,256]{1,0:T(8,128)(2,1)} %bitcast.9, f32[4,4,256]{2,1,0:T(4,128)} %bitcast.10), custom_call_target="tpu_custom_call" | custom-call | flops 1677721600 | bytes 1048576 | tf_op jit(solution)/shard_map/encode/pallas_call | solution.py:449
  4.4 0.0 copy-start.5
  4.4 0.0 copy-start.6
  4.4 0.0 copy-start.7
  4.4 0.0 copy-start.8
  4.4 9.5 %all-to-all-start = ((bf16[8,128,256]{2,1,0:T(8,128)(2,1)}), bf16[8,128,256]{2,1,0:T(8,128)(2,1)S(1)}, u32[]{:S(2)}, u32[]{:S(2)}) async-start(bf16[8,128,256]{2,1,0:T(8,128)(2,1)} %get-tuple-element.14), calls=%async_computation | async-start | bytes 1048576 | tf_op jit(solution)/shard_map/all_to_all | solution.py:474
  13.9 9.4 %collective-permute-start.1 = (bf16[16,256]{1,0:T(8,128)(2,1)}, bf16[16,256]{1,0:T(8,128)(2,1)S(1)}, u32[]{:S(2)}, u32[]{:S(2)}) collective-permute-start(bf16[16,256]{1,0:T(8,128)(2,1)} %get-tuple-element.15), channel_id=1, source_target_pairs={{0,63},{1,0},{2,1},{3,2},{4,3},{5,4},{6,5},{7,6},{8,7},{9,8},{10,9... | collective-permute-start | bytes 24584 | tf_op jit(solution)/shard_map/ppermute | solution.py:377
  23.3 1.9 %collective-permute-start = (bf16[16,256]{1,0:T(8,128)(2,1)}, bf16[16,256]{1,0:T(8,128)(2,1)S(1)}, u32[]{:S(2)}, u32[]{:S(2)}) collective-permute-start(bf16[16,256]{1,0:T(8,128)(2,1)} %get-tuple-element.15), channel_id=1, source_target_pairs={{0,1},{1,2},{2,3},{3,4},{4,5},{5,6},{6,7},{7,8},{8,9},{9,10},{10,1... | collective-permute-start | bytes 24584 | tf_op jit(solution)/shard_map/ppermute | solution.py:377
  25.2 0.0 collective-permute-done.1
  25.2 7.1 %collective-permute-done = bf16[16,256]{1,0:T(8,128)(2,1)S(1)} collective-permute-done((bf16[16,256]{1,0:T(8,128)(2,1)}, bf16[16,256]{1,0:T(8,128)(2,1)S(1)}, u32[]{:S(2)}, u32[]{:S(2)}) %collective-permute-start) | collective-permute-done | bytes 8224 | tf_op jit(solution)/shard_map/ppermute | solution.py:377
  32.4 0.0 all-to-all-done
  32.4 0.1 convert_reduce_fusion
  32.5 0.8 %pad_maximum_fusion.1 = (bf16[160,256]{1,0:T(8,128)(2,1)S(1)}, bf16[160,256]{1,0:T(8,128)(2,1)S(1)}) fusion(bf16[16,256]{1,0:T(8,128)(2,1)S(1)} %collective-permute-done.1, bf16[16,256]{1,0:T(8,128)(2,1)} %get-tuple-element.15, bf16[128,256]{1,0:T(8,128)(2,1)S(1)} %multiply_convert_fusion.refs_1_, bf16[16,256]{1,0:T(8,128)(2,1)S(1)} %collective-permute-done), kind=kLoop, calls=%fused_computation.3 | loop fusion | flops 450560 | bytes 253952 | tf_op jit(solution)/shard_map/concatenate | solution.py:482
  33.2 1.9 %collective-permute-start.3 = (bf16[160,256]{1,0:T(8,128)(2,1)S(1)}, bf16[160,256]{1,0:T(8,128)(2,1)S(1)}, u32[]{:S(2)}, u32[]{:S(2)}) collective-permute-start(bf16[160,256]{1,0:T(8,128)(2,1)S(1)} %get-tuple-element.21), channel_id=1, source_target_pairs={{0,63},{1,0},{2,1},{3,2},{4,3},{5,4},{6,5},{7,6},{8,7},{9,8},{10,9... | collective-permute-start | bytes 245768 | tf_op jit(solution)/shard_map/ppermute | solution.py:377
  35.2 3.9 %collective-permute-start.2 = (bf16[160,256]{1,0:T(8,128)(2,1)S(1)}, bf16[160,256]{1,0:T(8,128)(2,1)S(1)}, u32[]{:S(2)}, u32[]{:S(2)}) collective-permute-start(bf16[160,256]{1,0:T(8,128)(2,1)S(1)} %get-tuple-element.22), channel_id=1, source_target_pairs={{0,1},{1,2},{2,3},{3,4},{4,5},{5,6},{6,7},{7,8},{8,9},{9,10},{10,1... | collective-permute-start | bytes 245768 | tf_op jit(solution)/shard_map/ppermute | solution.py:377
  39.1 0.5 collective-permute-done.3.refs_2_
  39.6 5.2 %collective-permute-done.2.refs_0_ = bf16[160,256]{1,0:T(8,128)(2,1)S(1)} collective-permute-done((bf16[160,256]{1,0:T(8,128)(2,1)S(1)}, bf16[160,256]{1,0:T(8,128)(2,1)S(1)}, u32[]{:S(2)}, u32[]{:S(2)}) %collective-permute-start.2) | collective-permute-done | bytes 81952 | tf_op jit(solution)/shard_map/ppermute | solution.py:377
  44.8 0.0 copy-done.2
  44.8 0.0 copy-done.3
  44.8 0.0 copy-done
  44.9 6.1 %step0.1 = (f32[16,256]{1,0:T(8,128)S(1)}, bf16[16,256]{1,0:T(8,128)(2,1)S(1)}) custom-call(s32[1]{0:T(128)S(6)} %copy.14.width_ref, f32[3]{0:T(128)S(1)} %copy-done.6, f32[16,256]{1,0:T(8,128)S(1)} %copy-done.8, bf16[160,256]{1,0:T(8,128)(2,1)S(1)} %collective-permute-done.2.refs_0_, bf16[128,256]{1,0:T(8,128)(2,1)S(1)} %multiply_convert_fusion.refs_1_, ...), custom_call_target="tpu_custom_call" | custom-call | flops 4026531840 | bytes 1048576 | tf_op jit(solution)/shard_map/step0/pallas_call | solution.py:420
  51.0 1.9 %collective-permute-start.7 = (bf16[16,256]{1,0:T(8,128)(2,1)S(1)}, bf16[16,256]{1,0:T(8,128)(2,1)S(1)}, u32[]{:S(2)}, u32[]{:S(2)}) collective-permute-start(bf16[16,256]{1,0:T(8,128)(2,1)S(1)} %get-tuple-element.20), channel_id=1, source_target_pairs={{0,62},{1,63},{2,0},{3,1},{4,2},{5,3},{6,4},{7,5},{8,6},{9,7},{10,... | collective-permute-start | bytes 24584 | tf_op jit(solution)/shard_map/ppermute | solution.py:377
  52.9 1.9 %collective-permute-start.6 = (bf16[16,256]{1,0:T(8,128)(2,1)S(1)}, bf16[16,256]{1,0:T(8,128)(2,1)S(1)}, u32[]{:S(2)}, u32[]{:S(2)}) collective-permute-start(bf16[16,256]{1,0:T(8,128)(2,1)S(1)} %get-tuple-element.20), channel_id=1, source_target_pairs={{0,63},{1,0},{2,1},{3,2},{4,3},{5,4},{6,5},{7,6},{8,7},{9,8},{10,9... | collective-permute-start | bytes 24584 | tf_op jit(solution)/shard_map/ppermute | solution.py:377
  54.8 3.9 %collective-permute-start.5 = (bf16[16,256]{1,0:T(8,128)(2,1)S(1)}, bf16[16,256]{1,0:T(8,128)(2,1)S(1)}, u32[]{:S(2)}, u32[]{:S(2)}) collective-permute-start(bf16[16,256]{1,0:T(8,128)(2,1)S(1)} %get-tuple-element.20), channel_id=1, source_target_pairs={{0,1},{1,2},{2,3},{3,4},{4,5},{5,6},{6,7},{7,8},{8,9},{9,10},{10,1... | collective-permute-start | bytes 24584 | tf_op jit(solution)/shard_map/ppermute | solution.py:377
  58.8 4.8 %collective-permute-start.4 = (bf16[16,256]{1,0:T(8,128)(2,1)S(1)}, bf16[16,256]{1,0:T(8,128)(2,1)S(1)}, u32[]{:S(2)}, u32[]{:S(2)}) collective-permute-start(bf16[16,256]{1,0:T(8,128)(2,1)S(1)} %get-tuple-element.20), channel_id=1, source_target_pairs={{0,2},{1,3},{2,4},{3,5},{4,6},{5,7},{6,8},{7,9},{8,10},{9,11},{10,... | collective-permute-start | bytes 24584 | tf_op jit(solution)/shard_map/ppermute | solution.py:377
  63.6 0.0 collective-permute-done.7.refs_6_
  63.6 0.0 collective-permute-done.6.refs_5_
  63.6 0.1 collective-permute-done.5.refs_4_
  63.7 4.8 %collective-permute-done.4.refs_3_ = bf16[16,256]{1,0:T(8,128)(2,1)S(1)} collective-permute-done((bf16[16,256]{1,0:T(8,128)(2,1)S(1)}, bf16[16,256]{1,0:T(8,128)(2,1)S(1)}, u32[]{:S(2)}, u32[]{:S(2)}) %collective-permute-start.4) | collective-permute-done | bytes 8224 | tf_op jit(solution)/shard_map/ppermute | solution.py:377
  68.5 6.7 %step1.1 = f32[4,4,256]{2,1,0:T(4,128)} custom-call(s32[1]{0:T(128)S(6)} %copy.14.width_ref, f32[3]{0:T(128)S(1)} %copy-done.6, f32[16,256]{1,0:T(8,128)S(1)} %get-tuple-element.19.own_ref, bf16[160,256]{1,0:T(8,128)(2,1)S(1)} %collective-permute-done.2.refs_0_, bf16[128,256]{1,0:T(8,128)(2,1)S(1)} %multiply_convert_fusion.refs_1_, ...), custom_call_target="tpu_custom_call" | custom-call | flops 4026531840 | bytes 1048576 | tf_op jit(solution)/shard_map/step1/pallas_call | solution.py:420
  (10 shorter events, 0.0 us)
Async XLA Ops:
  0.7 44.2 %copy-start.2 = (bf16[9,256,128]{2,1,0:T(8,128)(2,1)S(1)}, bf16[9,256,128]{2,1,0:T(8,128)(2,1)}, u32[]{:S(2)}) copy-start(bf16[9,256,128]{2,1,0:T(8,128)(2,1)} %refs_11_.1) | copy-start | bytes 1769476
  0.7 44.2 %copy-start.3 = (bf16[9,128,128]{2,1,0:T(8,128)(2,1)S(1)}, bf16[9,128,128]{2,1,0:T(8,128)(2,1)}, u32[]{:S(2)}) copy-start(bf16[9,128,128]{2,1,0:T(8,128)(2,1)} %refs_10_.1) | copy-start | bytes 884740
  4.4 40.4 %copy-start = (bf16[9,256,256]{2,1,0:T(8,128)(2,1)S(1)}, bf16[9,256,256]{2,1,0:T(8,128)(2,1)}, u32[]{:S(2)}) copy-start(bf16[9,256,256]{2,1,0:T(8,128)(2,1)} %refs_12_.1) | copy-start | bytes 3538948
  4.4 40.4 %copy-start.1 = (bf16[9,128,384]{2,1,0:T(8,128)(2,1)S(1)}, bf16[9,128,384]{2,1,0:T(8,128)(2,1)}, u32[]{:S(2)}) copy-start(bf16[9,128,384]{2,1,0:T(8,128)(2,1)} %refs_13_.1) | copy-start | bytes 2654212
  4.4 40.5 %copy-start.4 = (bf16[9,128,4]{1,2,0:T(4,128)(2,1)S(1)}, bf16[9,128,4]{1,2,0:T(4,128)(2,1)}, u32[]{:S(2)}) copy-start(bf16[9,128,4]{1,2,0:T(4,128)(2,1)} %param.19) | copy-start | bytes 27652
  4.4 40.5 %copy-start.5 = (bf16[9,4,128]{2,1,0:T(4,128)(2,1)S(1)}, bf16[9,4,128]{2,1,0:T(4,128)(2,1)}, u32[]{:S(2)}) copy-start(bf16[9,4,128]{2,1,0:T(4,128)(2,1)} %refs_9_.3) | copy-start | bytes 27652
  4.4 40.5 %copy-start.6 = (f32[3]{0:T(128)S(1)}, f32[3]{0:T(128)}, u32[]{:S(2)}) copy-start(f32[3]{0:T(128)} %sigma_ref.5) | copy-start | bytes 40
  4.4 40.5 %copy-start.7 = (f32[128]{0:T(128)S(1)}, f32[128]{0:T(128)}, u32[]{:S(2)}) copy-start(f32[128]{0:T(128)} %param.20) | copy-start | bytes 1540
  4.4 40.4 %copy-start.8 = (f32[16,256]{1,0:T(8,128)S(1)}, f32[16,256]{1,0:T(8,128)}, u32[]{:S(2)}) copy-start(f32[16,256]{1,0:T(8,128)} %get-tuple-element.13.own_ref) | copy-start | bytes 49156
  4.4 27.9 %all-to-all-start = ((bf16[8,128,256]{2,1,0:T(8,128)(2,1)}), bf16[8,128,256]{2,1,0:T(8,128)(2,1)S(1)}, u32[]{:S(2)}, u32[]{:S(2)}) async-start(bf16[8,128,256]{2,1,0:T(8,128)(2,1)} %get-tuple-element.14), calls=%async_computation | async-start | bytes 1048576 | tf_op jit(solution)/shard_map/all_to_all | solution.py:474
  13.9 11.3 %collective-permute-start.1 = (bf16[16,256]{1,0:T(8,128)(2,1)}, bf16[16,256]{1,0:T(8,128)(2,1)S(1)}, u32[]{:S(2)}, u32[]{:S(2)}) collective-permute-start(bf16[16,256]{1,0:T(8,128)(2,1)} %get-tuple-element.15), channel_id=1, source_target_pairs={{0,63},{1,0},{2,1},{3,2},{4,3},{5,4},{6,5},{7,6},{8,7},{9,8},{10,9... | collective-permute-start | bytes 24584 | tf_op jit(solution)/shard_map/ppermute | solution.py:377
  23.3 9.1 %collective-permute-start = (bf16[16,256]{1,0:T(8,128)(2,1)}, bf16[16,256]{1,0:T(8,128)(2,1)S(1)}, u32[]{:S(2)}, u32[]{:S(2)}) collective-permute-start(bf16[16,256]{1,0:T(8,128)(2,1)} %get-tuple-element.15), channel_id=1, source_target_pairs={{0,1},{1,2},{2,3},{3,4},{4,5},{5,6},{6,7},{7,8},{8,9},{9,10},{10,1... | collective-permute-start | bytes 24584 | tf_op jit(solution)/shard_map/ppermute | solution.py:377
  33.2 6.3 %collective-permute-start.3 = (bf16[160,256]{1,0:T(8,128)(2,1)S(1)}, bf16[160,256]{1,0:T(8,128)(2,1)S(1)}, u32[]{:S(2)}, u32[]{:S(2)}) collective-permute-start(bf16[160,256]{1,0:T(8,128)(2,1)S(1)} %get-tuple-element.21), channel_id=1, source_target_pairs={{0,63},{1,0},{2,1},{3,2},{4,3},{5,4},{6,5},{7,6},{8,7},{9,8},{10,9... | collective-permute-start | bytes 245768 | tf_op jit(solution)/shard_map/ppermute | solution.py:377
  35.2 9.7 %collective-permute-start.2 = (bf16[160,256]{1,0:T(8,128)(2,1)S(1)}, bf16[160,256]{1,0:T(8,128)(2,1)S(1)}, u32[]{:S(2)}, u32[]{:S(2)}) collective-permute-start(bf16[160,256]{1,0:T(8,128)(2,1)S(1)} %get-tuple-element.22), channel_id=1, source_target_pairs={{0,1},{1,2},{2,3},{3,4},{4,5},{5,6},{6,7},{7,8},{8,9},{9,10},{10,1... | collective-permute-start | bytes 245768 | tf_op jit(solution)/shard_map/ppermute | solution.py:377
  51.0 12.6 %collective-permute-start.7 = (bf16[16,256]{1,0:T(8,128)(2,1)S(1)}, bf16[16,256]{1,0:T(8,128)(2,1)S(1)}, u32[]{:S(2)}, u32[]{:S(2)}) collective-permute-start(bf16[16,256]{1,0:T(8,128)(2,1)S(1)} %get-tuple-element.20), channel_id=1, source_target_pairs={{0,62},{1,63},{2,0},{3,1},{4,2},{5,3},{6,4},{7,5},{8,6},{9,7},{10,... | collective-permute-start | bytes 24584 | tf_op jit(solution)/shard_map/ppermute | solution.py:377
  52.9 10.7 %collective-permute-start.6 = (bf16[16,256]{1,0:T(8,128)(2,1)S(1)}, bf16[16,256]{1,0:T(8,128)(2,1)S(1)}, u32[]{:S(2)}, u32[]{:S(2)}) collective-permute-start(bf16[16,256]{1,0:T(8,128)(2,1)S(1)} %get-tuple-element.20), channel_id=1, source_target_pairs={{0,63},{1,0},{2,1},{3,2},{4,3},{5,4},{6,5},{7,6},{8,7},{9,8},{10,9... | collective-permute-start | bytes 24584 | tf_op jit(solution)/shard_map/ppermute | solution.py:377
  54.8 8.9 %collective-permute-start.5 = (bf16[16,256]{1,0:T(8,128)(2,1)S(1)}, bf16[16,256]{1,0:T(8,128)(2,1)S(1)}, u32[]{:S(2)}, u32[]{:S(2)}) collective-permute-start(bf16[16,256]{1,0:T(8,128)(2,1)S(1)} %get-tuple-element.20), channel_id=1, source_target_pairs={{0,1},{1,2},{2,3},{3,4},{4,5},{5,6},{6,7},{7,8},{8,9},{9,10},{10,1... | collective-permute-start | bytes 24584 | tf_op jit(solution)/shard_map/ppermute | solution.py:377
  58.8 9.8 %collective-permute-start.4 = (bf16[16,256]{1,0:T(8,128)(2,1)S(1)}, bf16[16,256]{1,0:T(8,128)(2,1)S(1)}, u32[]{:S(2)}, u32[]{:S(2)}) collective-permute-start(bf16[16,256]{1,0:T(8,128)(2,1)S(1)} %get-tuple-element.20), channel_id=1, source_target_pairs={{0,2},{1,3},{2,4},{3,5},{4,6},{5,7},{6,8},{7,9},{8,10},{9,11},{10,... | collective-permute-start | bytes 24584 | tf_op jit(solution)/shard_map/ppermute | solution.py:377

commit v6 on v5

v6 whole, which is shorter than its diff:
```python
import functools
import math

import jax
import jax.numpy as jnp
from jax import lax
from jax.experimental import pallas as pl
from jax.experimental.pallas import tpu as pltpu
from jax.sharding import PartitionSpec as P

K = 96
SIGMA_DATA = 0.5
BF = jnp.bfloat16
F32 = jnp.float32
HALF = 128
ROWS = 256
NT = (((1,), (1,)), ((), ()))
TN = (((0,), (0,)), ((), ()))

BLOCKS = (4, 4, 4, 3, 3, 4)
FIELDS = ("scaled", "first", "second", "third", "fourth", "fifth", "out")
STEP_ROWS = (
    dict(zip(FIELDS, ((-15, 31), (-14, 29), (-13, 27), (-6, 13), (-5, 11), (-8, 19), (-7, 17)))),
    dict(zip(FIELDS, ((-7, 17), (-6, 15), (-5, 13), (-2, 6), (-1, 4), (-1, 6), (0, 4)))),
)


def silu_twice(h):
    return h + h * jnp.tanh(h)


def dot_nt(a, b):
    return lax.dot_general(a, b, NT, preferred_element_type=F32)


def levels(sigma_ref, step):
    now = jnp.full((1, 256), sigma_ref[step], F32)
    after = jnp.full((1, 256), sigma_ref[step + 1], F32)
    var = now * now + SIGMA_DATA * SIGMA_DATA
    root = jnp.sqrt(var)
    return now, 1.0 / root, SIGMA_DATA * SIGMA_DATA / var, now * SIGMA_DATA / root, (after - now) / now


def encode_kernel(
    anchor_ref, width_ref, sigma_ref, blocks_ref, w_ref, noise_ref, out_ref, state_ref, parts_ref, enc_ref, flat, wide
):
    band = lax.axis_index("band")
    tile = lax.axis_index("tile")
    count = blocks_ref.shape[0]
    cells = enc_ref.shape[1]
    chans = w_ref.shape[0]
    tiles = blocks_ref.shape[1] // 128
    group = 8 * tiles

    flat[count * tiles :, :] = jnp.zeros((flat.shape[0] - count * tiles, 128), F32)
    for g in range(count // 16):
        for t in range(tiles):
            v = blocks_ref[16 * g : 16 * g + 16, 128 * t : 128 * t + 128].astype(F32)
            flat[2 * g * group + 8 * t : 2 * g * group + 8 * t + 8, :] = v[:8]
            flat[(2 * g + 1) * group + 8 * t : (2 * g + 1) * group + 8 * t + 8, :] = v[8:]

    sigma = levels(sigma_ref, 0)[0]
    natural = (lax.broadcasted_iota(jnp.int32, (4, 256), 1) < width_ref[0]).astype(F32)
    for r in range(4):
        row = sigma * noise_ref[:, r, :] * natural
        state_ref[4 * r : 4 * r + 4, :] = row
    state = state_ref[...]
    high = state.astype(BF)
    parts_ref[0:16, :] = high
    parts_ref[16:32, :] = (state - high.astype(F32)).astype(BF)

    w = 0.5 * w_ref[...].astype(F32)
    for half in range(2):
        wide[half, 0:chans, :] = w[:, 128 * half : 128 * half + 128]
        wide[half, chans:80, :] = jnp.zeros((80 - chans, 128), F32)
    weight = jnp.concatenate(
        [
            jnp.concatenate([wide[half, pl.ds(odd, 40, stride=2), :] for half in range(2)], 1)
            for odd in range(2)
        ],
        0,
    ).astype(BF)
    first = lax.broadcasted_iota(jnp.int32, (40, 128), 1) < 64

    def encode(g, carry):
        begin = pl.multiple_of(g * group, 8)
        cols = []
        for k in range(4):
            one = flat[pl.ds(begin + 2 * k, 40, stride=8), :]
            two = flat[pl.ds(begin + 2 * k + 1, 40, stride=8), :]
            even = jnp.where(first, one, pltpu.roll(two, 64, 1))
            odd = jnp.where(first, pltpu.roll(one, 64, 1), two)
            cols.append(jnp.concatenate([even, odd], 0))
        x = jnp.concatenate(cols, 1).astype(BF)
        v = lax.dot_general(x, weight, TN, preferred_element_type=F32)
        v = silu_twice(v).astype(BF).astype(F32)
        enc_ref[pl.ds(g * 8, 8)] = v.reshape(8, cells, 256)
        return carry

    lax.fori_loop(0, count // 8, encode, 0, unroll=True)

    enc_ref[pl.ds(count, 8)] = enc_ref[pl.ds(0, 8)]

    def window(k, carry):
        nest = k // 2
        part = k % 2
        anchor = anchor_ref[nest, tile]
        begin = anchor + (band - anchor + 512) % 8 + part * 48
        row = (begin % 512) // 8
        total = enc_ref[row]
        for m in range(1, 6):
            total = total + enc_ref[row + m]
        out_ref[nest, pl.ds(pl.multiple_of(part * cells, cells), cells), :] = total.astype(BF)
        return carry

    lax.fori_loop(0, 16, window, 0, unroll=4)


def pair_weight(w, a):
    zero = jnp.zeros_like(w(a, 0))
    own = jnp.concatenate(
        [jnp.concatenate([w(a, 1), w(a, 2)], 1), jnp.concatenate([w(a, 0), w(a, 1)], 1)], 0
    )
    rim = jnp.concatenate(
        [jnp.concatenate([w(a, 0), zero], 1), jnp.concatenate([zero, w(a, 2)], 1)], 0
    )
    return own, rim


def tall(ref, a, b):
    if not 0 <= b <= 2:
        return jnp.zeros((8, 128), F32)
    return jnp.concatenate([ref[3 * a + b].astype(F32), jnp.zeros((4, 128), F32)], 0)


def form_in(w, out):
    taps = [jnp.concatenate([tall(w, a, q - p) for p in range(2)], 1) for a in range(3) for q in range(4)]
    out[...] = (0.5 * jnp.concatenate(taps, 0)).astype(BF)


def form_out(w, out):
    taps = [
        jnp.concatenate([tall(w, a, q - p) for q in (1, 2, 0, 3)], 1) for a in range(3) for p in range(2)
    ]
    out[...] = jnp.concatenate(taps, 0).astype(BF)


def form_pairs(w, chans, out):
    half = jnp.asarray(0.5, BF)
    for a in range(3):
        own, rim = pair_weight(lambda i, b: w[3 * i + b][:, 0:chans] * half, a)
        out[:, 512 * a : 512 * a + 256] = own
        out[:, 512 * a + 256 : 512 * a + 512] = rim


def form_down(w, out):
    half = jnp.asarray(0.5, BF)
    for a in range(3):
        out[:, 256 * a : 256 * a + 128] = w[3 * a + 1] * half
        out[:, 256 * a + 128 : 256 * a + 256] = w[3 * a + 2] * half
        out[:, 768 + 128 * a : 896 + 128 * a] = w[3 * a] * half


def form_mid(w, out):
    half = jnp.asarray(0.5, BF)
    for a in range(3):
        for b in range(3):
            out[:, 768 * a + 256 * b : 768 * a + 256 * b + 256] = w[3 * a + b] * half


def form_up(w, even, odd):
    def up(a, b):
        return 0.5 * w[3 * a + b][:, 128:384].astype(F32)

    for out, sets in ((even, ((0,), (1, 2))), (odd, ((0, 1), (2,)))):
        for k, taps in enumerate(sets):
            col = [sum(up(a, b) for a in taps) for b in range(3)]
            zero = jnp.zeros_like(col[0])
            out[:, 768 * k : 768 * k + 256] = jnp.concatenate([col[0], zero], 0).astype(BF)
            out[:, 768 * k + 256 : 768 * k + 512] = jnp.concatenate(
                [col[1] + col[2], col[0] + col[1]], 0
            ).astype(BF)
            out[:, 768 * k + 512 : 768 * k + 768] = jnp.concatenate([zero, col[2]], 0).astype(BF)


def parts(total, most):
    count = -(-total // most)
    cuts = [total * i // count for i in range(count + 1)]
    return [(a, b - a) for a, b in zip(cuts, cuts[1:])]


class Field:
    def __init__(self, width, masks):
        self.tile = lax.axis_index("tile")
        self.masks = masks
        lane = lax.broadcasted_iota(jnp.int32, (HALF, 256), 1)
        pair = lax.broadcasted_iota(jnp.int32, (HALF, 256), 0)
        masks[0] = jnp.zeros((HALF, 256), F32)
        masks[1] = (2 * pair + lane // 128 < width).astype(F32)
        masks[2] = (2 * pair < width).astype(F32)
        self.natural = (lax.broadcasted_iota(jnp.int32, (4, 256), 1) < width).astype(F32)

    def fine_ok(self, rho):
        row = self.tile * 4 + rho
        return jnp.logical_and(row >= 0, row < ROWS).astype(jnp.int32)

    def half_ok(self, h):
        row = self.tile * 2 + h
        return jnp.logical_and(row >= 0, row < ROWS // 2).astype(jnp.int32)

    def keep_pairs(self, y, center, rim, at, rho):
        y = y * self.masks[self.fine_ok(rho)]
        center[at] = y.astype(BF)
        rim[at] = jnp.concatenate([slide(y[:, 128:], 1), slide(y[:, :128], -1)], 1).astype(BF)

    def keep_half(self, y, center, left, right, at, h):
        y = y * self.masks[2 * self.half_ok(h)]
        center[at] = y.astype(BF)
        left[at] = slide(y, 1).astype(BF)
        right[at] = slide(y, -1).astype(BF)


def embedding(w_sigma, now):
    return jnp.concatenate([w_sigma[...], w_sigma[...]], 1) * jnp.log(now)


def slide(x, by):
    x = pltpu.roll(x, by % HALF, 0)
    where = lax.broadcasted_iota(jnp.int32, (8, x.shape[1]), 0)
    if by == 1:
        return jnp.concatenate([jnp.where(where == 0, 0.0, x[:8]), x[8:]], 0)
    return jnp.concatenate([x[: HALF - 8], jnp.where(where == 7, 0.0, x[HALF - 8 :])], 0)


def stacked(ref, at, n, step=1):
    return jnp.concatenate([ref[at + step * k] for k in range(n)], 0)


def encoder(field, rows, state, spread, scale, bias, f_in, f_enc, firstc, firste, secondc, seconde):
    n_state = rows["scaled"][1]
    first_lo, n_first = rows["first"]
    second_lo, n_second = rows["second"]
    col = lax.broadcasted_iota(jnp.int32, (256, 512), 0)
    place = lax.broadcasted_iota(jnp.int32, (256, 512), 1)
    pick = (col == 2 * (place % 128) + place // 128 - 1).astype(F32).astype(BF)
    scaled = (state[0 : 8 * n_state, :] * scale).astype(BF)
    spread[0 : 8 * n_state, :] = jnp.dot(scaled, pick, preferred_element_type=F32)
    for at, n in parts(n_first, BLOCKS[0]):
        cols = [
            jnp.concatenate(
                [
                    spread[8 * (k + a) : 8 * (k + a) + 8, 128 * q : 128 * q + 128]
                    for a in range(3)
                    for q in range(4)
                ],
                0,
            )
            for k in range(at, at + n)
        ]
        x = jnp.concatenate(cols, 1).astype(BF)
        y = lax.dot_general(x, f_in[...], TN, preferred_element_type=F32)
        for k in range(n):
            part = silu_twice(y[k * HALF : (k + 1) * HALF] + bias)
            field.keep_pairs(part, firstc, firste, at + k, first_lo + at + k)

    for at, n in parts(n_second, BLOCKS[1]):
        x = jnp.concatenate([stacked(ref, at + a, n) for a in range(3) for ref in (firstc, firste)], 1)
        y = dot_nt(x, f_enc[...])
        for k in range(n):
            part = silu_twice(y[k * HALF : (k + 1) * HALF])
            field.keep_pairs(part, secondc, seconde, at + k, second_lo + at + k)

def first_kernel(
    width_ref, sigma_ref, own, up3, down3, near_up, near_down, w_sigma, w_in, w_enc,
    state_ref, secondc, seconde,
    state, spread, firstc, firste, masks, f_in, f_enc,
):
    field = Field(width_ref[0], masks)
    form_in(w_in, f_in)
    form_pairs(w_enc, 128, f_enc)
    sigma, scale = levels(sigma_ref, 0)[:2]

    empty = jnp.zeros((4, 256), F32)
    held = {-3: (up3, 0), 3: (down3, 0)}
    for slot in range(3):
        held[3 * slot - 4] = (near_up, 128 + 32 * slot)
        held[3 * slot - 2] = (near_down, 128 + 32 * slot)
    state_lo = STEP_ROWS[0]["scaled"][0]
    for tile_off in range(-4, 4):
        if tile_off == 0:
            value = own[...]
        else:
            ref, begin = held[tile_off]
            value = ref[begin : begin + 16, :].astype(F32) + ref[begin + 16 : begin + 32, :].astype(F32)
        for r in range(4):
            rho = 4 * tile_off + r
            if rho >= state_lo:
                row = jnp.concatenate([value[4 * r : 4 * r + 4], empty], 0)
                at = 8 * (rho - state_lo)
                state[at : at + 8, :] = row * field.fine_ok(rho).astype(F32)

    rows = STEP_ROWS[0]
    out_lo, n_out = rows["out"]
    state_ref[...] = state[8 * (out_lo - state_lo) : 8 * (out_lo - state_lo + n_out), :]
    bias = 0.5 * embedding(w_sigma, sigma)
    encoder(field, rows, state, spread, scale, bias, f_in, f_enc, firstc, firste, secondc, seconde)


def second_kernel(
    width_ref, sigma_ref, state_in, secondc0, seconde0, near_up, near_down, cond_own, far_up, far_down,
    w_sigma, w_in, w_out, w_enc, w_down, w_mid, w_dec,
    out_ref,
    state, spread, firstc, firste, secondc1, seconde1, third, thirdl, thirdr, fourth, fourthl, fourthr,
    fifthc, fifthe, prod, picked, masks,
    f_in, f_out, f_enc, f_down, f_mid, f_dec, f_even, f_odd,
):
    field = Field(width_ref[0], masks)
    form_in(w_in, f_in)
    form_out(w_out, f_out)
    form_pairs(w_enc, 128, f_enc)
    form_down(w_down, f_down)
    form_mid(w_mid, f_mid)
    form_pairs(w_dec, 128, f_dec)
    form_up(w_dec, f_even, f_odd)

    empty = jnp.zeros((4, 256), F32)
    weave_j = lax.broadcasted_iota(jnp.int32, (256, 256), 0)
    weave_c = lax.broadcasted_iota(jnp.int32, (256, 256), 1)
    weave = (weave_c == 2 * (weave_j % HALF) + weave_j // HALF).astype(F32).astype(BF)
    repeat = (
        lax.broadcasted_iota(jnp.int32, (HALF, 64), 0) // 2 == lax.broadcasted_iota(jnp.int32, (HALF, 64), 1)
    ).astype(F32)
    repeat = (0.5 * repeat).astype(BF)
    conds = [
        (ref, r)
        for ref, n in ((far_up, 4), (near_up, 2), (cond_own, 2), (near_down, 2), (far_down, 4))
        for r in range(n)
    ]

    for step in range(2):
        rows = STEP_ROWS[step]
        sigma, scale, keep, mix, move = levels(sigma_ref, step)
        second_lo = rows["second"][0]
        third_lo, n_third = rows["third"]
        fourth_lo, n_fourth = rows["fourth"]
        fifth_lo, n_fifth = rows["fifth"]
        out_lo, n_out = rows["out"]

        secondc, seconde = (secondc0, seconde0) if step == 0 else (secondc1, seconde1)
        if step == 1:
            bias = 0.5 * embedding(w_sigma, sigma)
            encoder(field, rows, state, spread, scale, bias, f_in, f_enc, firstc, firste, secondc, seconde)

        for at, n in parts(n_third, BLOCKS[2]):
            begin = 2 * (third_lo + at) - 1 - second_lo
            x = jnp.concatenate(
                [stacked(secondc, begin + a, n, 2) for a in range(3)]
                + [
                    jnp.concatenate([seconde[begin + a + 2 * k][:, :128] for k in range(n)], 0)
                    for a in range(3)
                ],
                1,
            )
            y = dot_nt(x, f_down[...])
            for k in range(n):
                ref, r = conds[third_lo + at + k + 6]
                add = jnp.dot(repeat, ref[64 * r : 64 * r + 64, :], preferred_element_type=F32)
                part = silu_twice(y[k * HALF : (k + 1) * HALF] + add)
                field.keep_half(part, third, thirdl, thirdr, at + k, third_lo + at + k)

        for at, n in parts(n_fourth, BLOCKS[3]):
            x = jnp.concatenate(
                [stacked(ref, at + a, n) for a in range(3) for ref in (thirdl, third, thirdr)], 1
            )
            y = dot_nt(x, f_mid[...])
            for k in range(n):
                part = silu_twice(y[k * HALF : (k + 1) * HALF])
                field.keep_half(part, fourth, fourthl, fourthr, at + k, fourth_lo + at + k)

        for parity in range(2):
            for cut, n in parts((n_fifth - parity + 1) // 2, BLOCKS[4]):
                at = parity + 2 * cut
                rho = fifth_lo + at
                odd = rho % 2
                begin = rho - 1 - second_lo
                h = (rho - odd) // 2 - fourth_lo - (0 if odd else 1)
                x = jnp.concatenate(
                    [stacked(ref, begin + a, n, 2) for a in range(3) for ref in (secondc, seconde)], 1
                )
                z = jnp.concatenate(
                    [stacked(ref, h + a, n) for a in range(2) for ref in (fourthl, fourth, fourthr)], 1
                )
                y = dot_nt(x, f_dec[...]) + dot_nt(z, (f_odd if odd else f_even)[...])
                for k in range(n):
                    part = silu_twice(y[k * HALF : (k + 1) * HALF])
                    field.keep_pairs(part, fifthc, fifthe, at + 2 * k, fifth_lo + at + 2 * k)

        for at, n in parts(n_fifth, BLOCKS[5]):
            x = jnp.concatenate([stacked(fifthc, at, n), stacked(fifthe, at, n)], 1)
            prod[:, at * HALF : (at + n) * HALF] = dot_nt(f_out[...], x)
        for k in range(n_out):
            for p in range(2):
                picked[8 * k : 8 * k + 8, HALF * p : HALF * p + HALF] = sum(
                    prod[16 * a + 8 * p : 16 * a + 8 * p + 8, (k + a) * HALF : (k + a + 1) * HALF]
                    for a in range(3)
                )
        value = picked[0 : 8 * n_out, :]
        high = value.astype(BF)
        low = (value - high.astype(F32)).astype(BF)
        net = jnp.dot(high, weave, preferred_element_type=F32) + jnp.dot(low, weave, preferred_element_type=F32)
        if step == 0:
            now = state_in[...]
        else:
            skip = 8 * (out_lo - rows["scaled"][0])
            now = state[skip : skip + 8 * n_out, :]
        denoised = keep * now + mix * net
        now = now + move * (now - denoised)
        for k in range(n_out):
            if step == 0:
                mask = field.natural * field.fine_ok(out_lo + k).astype(F32)
                state[8 * k : 8 * k + 8, :] = jnp.concatenate([now[8 * k : 8 * k + 4] * mask, empty], 0)
            else:
                out_ref[:, k, :] = now[8 * k : 8 * k + 4] * field.natural


def turn(x, by):
    n = lax.axis_size("tile")
    return lax.ppermute(x, "tile", [(i, (i + by) % n) for i in range(n)])


VMEM = pl.BlockSpec(memory_space=pltpu.VMEM)
SMEM = pl.BlockSpec(memory_space=pltpu.SMEM)


LIMIT = 24


def limit(mib):
    return pltpu.CompilerParams(vmem_limit_bytes=mib << 20)


def rowbuf(n):
    return pltpu.VMEM((n, HALF, 256), BF)


def cost(passes):
    return pl.CostEstimate(flops=passes * 128 * 65536 * 2, bytes_accessed=1 << 20, transcendentals=0)


def first_call(*args):
    rows = STEP_ROWS[0]
    n = rows["scaled"][1]
    return pl.pallas_call(
        first_kernel,
        out_shape=[
            jax.ShapeDtypeStruct((rows["out"][1] * 8, 256), F32),
            *[jax.ShapeDtypeStruct((rows["second"][1], HALF, 256), BF)] * 2,
        ],
        in_specs=[SMEM, SMEM] + [VMEM] * 8,
        out_specs=[VMEM] * 3,
        scratch_shapes=[
            pltpu.VMEM((n * 8, 256), F32), pltpu.VMEM((n * 8, 512), F32),
            *[rowbuf(rows["first"][1])] * 2,
            pltpu.VMEM((3, HALF, 256), F32),
            pltpu.VMEM((96, 256), BF), pltpu.VMEM((256, 1536), BF),
        ],
        compiler_params=limit(16),
        cost_estimate=cost(200),
        name="first",
    )(*args)


def second_call(*args):
    rows, late = STEP_ROWS
    n = late["scaled"][1]
    return pl.pallas_call(
        second_kernel,
        out_shape=jax.ShapeDtypeStruct((4, 4, 256), F32),
        in_specs=[SMEM, SMEM] + [VMEM] * 15,
        out_specs=VMEM,
        scratch_shapes=[
            pltpu.VMEM((n * 8, 256), F32), pltpu.VMEM((n * 8, 512), F32),
            *[rowbuf(late["first"][1])] * 2, *[rowbuf(late["second"][1])] * 2,
            *[rowbuf(rows["third"][1])] * 3, *[rowbuf(rows["fourth"][1])] * 3, *[rowbuf(rows["fifth"][1])] * 2,
            pltpu.VMEM((48, rows["fifth"][1] * HALF), F32),
            pltpu.VMEM((rows["out"][1] * 8, 256), F32),
            pltpu.VMEM((3, HALF, 256), F32),
            *[
                pltpu.VMEM(shape, BF)
                for shape in (
                    (96, 256), (48, 512), (256, 1536), (256, 1152), (256, 2304),
                    (256, 1536), (256, 1536), (256, 1536),
                )
            ],
        ],
        compiler_params=limit(LIMIT),
        cost_estimate=cost(600),
        name="second",
    )(*args)


def encode_call(block_anchor, nest_width, sigmas, coarse_blocks, w_context, noise):
    chans = w_context.shape[1]
    cells = coarse_blocks.shape[1] // chans
    count = coarse_blocks.shape[0]
    tiles = coarse_blocks.shape[1] // 128
    return pl.pallas_call(
        encode_kernel,
        out_shape=[
            jax.ShapeDtypeStruct((8, 2 * cells, 256), BF),
            jax.ShapeDtypeStruct((16, 256), F32),
            jax.ShapeDtypeStruct((32, 256), BF),
        ],
        in_specs=[SMEM, SMEM, SMEM, VMEM, VMEM, VMEM],
        out_specs=[VMEM] * 3,
        scratch_shapes=[
            pltpu.VMEM((count + 8, cells, 256), F32),
            pltpu.VMEM((count * tiles + 64, 128), F32),
            pltpu.VMEM((2, 80, 128), F32),
        ],
        compiler_params=limit(56),
        cost_estimate=cost(100),
        name="encode",
    )(block_anchor, nest_width, sigmas, coarse_blocks, w_context.T, noise)


def per_device(
    coarse_blocks, block_anchor, nest_width, sigmas, noise,
    w_context, w_in, w_sigma, w_enc, w_down, w_mid, w_dec, w_out,
):
    partial, own, own_parts = encode_call(
        block_anchor, nest_width, sigmas, coarse_blocks, w_context, noise[0]
    )
    arrived = lax.all_to_all(partial, "band", 0, 0, tiled=True)

    up3 = turn(own_parts, 3)
    down3 = turn(own_parts, -3)
    arrived, up3, down3 = lax.optimization_barrier((arrived, up3, down3))

    cond = (jnp.sum(arrived.astype(F32), axis=0) * (1.0 / math.sqrt(K // 2))).astype(BF)
    parcel = jnp.concatenate([cond, up3, own_parts, down3], 0)
    near_up = turn(parcel, 1)
    near_down = turn(parcel, -1)
    far_up = turn(jnp.concatenate([near_up[:128], cond], 0), 2)
    far_down = turn(jnp.concatenate([cond, near_down[:128]], 0), -2)
    w_sigma = w_sigma.reshape(1, -1)
    w_in = w_in.transpose(0, 2, 1)
    fields = first_call(nest_width, sigmas, own, up3, down3, near_up, near_down, w_sigma, w_in, w_enc)
    out = second_call(
        nest_width, sigmas, *fields, near_up, near_down, cond, far_up, far_down,
        w_sigma, w_in, w_out, w_enc, w_down, w_mid, w_dec,
    )
    return out[None]


def solution(mesh):
    return jax.shard_map(
        per_device,
        mesh=mesh,
        in_specs=(
            P("band", None), P(), P("band"), P(), P("band", None, "tile", None),
            P(), P(), P(), P(), P(), P(), P(), P(),
        ),
        out_specs=P("band", None, "tile", None),
        check_vma=False,
    )
```

time: 75.7 us -> 77.1 us (1.018)
  the two profiles are of different devices: /device:TPU:2 before, /device:TPU:10 now
where the time goes in v6:
time: 77.1 us; the launch traced here: 76.7 us
  starting transfers between devices  34 us (44%)
  Pallas kernels  23.2 us (30%)
  waiting for transfers between devices  18.4 us (24%)
  between operations  0.87 us (1%)
    ppermute x6, starting transfers between devices, turn(): return lax.ppermute(x, 'tile', [(i, (i + by) % n) for i in range(n)])  29 us
    ppermute x6, waiting for transfers between devices, turn(): return lax.ppermute(x, 'tile', [(i, (i + by) % n) for i in range(n)])  18.4 us
    pallas_call x1, Pallas kernels, second_call(): pl.pallas_call(second_kernel, out_shape=jax.ShapeDtypeStruct((4, 4, 256),...  15 us
    all_to_all x1, starting transfers between devices, per_device(): arrived = lax.all_to_all(partial, 'band', 0, 0, tiled=True)  4.97 us
    pallas_call x1, Pallas kernels, first_call(): pl.pallas_call(first_kernel, out_shape=[jax.ShapeDtypeStruct((rows['out']...  4.57 us
    pallas_call x1, Pallas kernels, encode_call(): pl.pallas_call(encode_kernel, out_shape=[jax.ShapeDtypeStruct((8, 2 * cel...  3.66 us
  transfers between devices with their start and end apart: 7, of which 4 were waited for; matrix products, arithmetic and copies ran while one was open for 0% of the time, Pallas kernels for 6%

profile of v6, /device:TPU:10, one launch (start us, length us, event | category | flops | bytes accessed | tf_op | source)
XLA Modules:
  0.0 76.7 jit_solution(1802635906049147086)
XLA Ops:
  0.7 3.7 %encode.1 = (bf16[8,128,256]{2,1,0:T(8,128)(2,1)}, f32[16,256]{1,0:T(8,128)}, bf16[32,256]{1,0:T(8,128)(2,1)}) custom-call(s32[8,64]{1,0:T(8,128)} %anchor_ref.1, s32[1]{0:T(128)S(6)} %copy.14.width_ref, f32[3]{0:T(128)} %sigma_ref.5, bf16[64,4480]{1,0:T(8,128)(2,1)} %blocks_ref.1, bf16[70,256]{1,0:T(8,128)(2,1)} %bitcast.9, f32[4,4,256]{2,1,0:T(4,128)} %bitcast.10), custom_call_target="tpu_custom_call" | custom-call | flops 1677721600 | bytes 1048576 | tf_op jit(solution)/shard_map/encode/pallas_call | solution.py:507
  4.3 0.0 copy-start.6
  4.3 0.0 copy-start.7
  4.3 0.0 copy-start.8
  4.4 5.0 %all-to-all-start = ((bf16[8,128,256]{2,1,0:T(8,128)(2,1)}), bf16[8,128,256]{2,1,0:T(8,128)(2,1)S(1)}, u32[]{:S(2)}, u32[]{:S(2)}) async-start(bf16[8,128,256]{2,1,0:T(8,128)(2,1)} %get-tuple-element.15), calls=%async_computation | async-start | bytes 1048576 | tf_op jit(solution)/shard_map/all_to_all | solution.py:534
  9.3 14.5 %collective-permute-start.1 = (bf16[32,256]{1,0:T(8,128)(2,1)}, bf16[32,256]{1,0:T(8,128)(2,1)S(1)}, u32[]{:S(2)}, u32[]{:S(2)}) collective-permute-start(bf16[32,256]{1,0:T(8,128)(2,1)} %get-tuple-element.16), channel_id=1, source_target_pairs={{0,61},{1,62},{2,63},{3,0},{4,1},{5,2},{6,3},{7,4},{8,5},{9,6},{10... | collective-permute-start | bytes 49160 | tf_op jit(solution)/shard_map/ppermute | solution.py:428
  23.9 1.9 %collective-permute-start = (bf16[32,256]{1,0:T(8,128)(2,1)}, bf16[32,256]{1,0:T(8,128)(2,1)S(1)}, u32[]{:S(2)}, u32[]{:S(2)}) collective-permute-start(bf16[32,256]{1,0:T(8,128)(2,1)} %get-tuple-element.16), channel_id=1, source_target_pairs={{0,3},{1,4},{2,5},{3,6},{4,7},{5,8},{6,9},{7,10},{8,11},{9,12},{10... | collective-permute-start | bytes 49160 | tf_op jit(solution)/shard_map/ppermute | solution.py:428
  25.8 0.0 collective-permute-done.1.down3
  25.8 9.0 %collective-permute-done.up3 = bf16[32,256]{1,0:T(8,128)(2,1)S(1)} collective-permute-done((bf16[32,256]{1,0:T(8,128)(2,1)}, bf16[32,256]{1,0:T(8,128)(2,1)S(1)}, u32[]{:S(2)}, u32[]{:S(2)}) %collective-permute-start) | collective-permute-done | bytes 16416 | tf_op jit(solution)/shard_map/ppermute | solution.py:428
  34.8 0.0 all-to-all-done
  34.8 0.1 convert_reduce_fusion
  34.9 0.0 copy-done.9
  34.9 3.3 %collective-permute-start.3 = (bf16[224,256]{1,0:T(8,128)(2,1)S(1)}, bf16[224,256]{1,0:T(8,128)(2,1)S(1)}, u32[]{:S(2)}, u32[]{:S(2)}) collective-permute-start(bf16[224,256]{1,0:T(8,128)(2,1)S(1)} %pad_maximum_fusion.2), channel_id=1, source_target_pairs={{0,63},{1,0},{2,1},{3,2},{4,3},{5,4},{6,5},{7,6},{8,7},{9,8},{10,9... | collective-permute-start | bytes 344072 | tf_op jit(solution)/shard_map/ppermute | solution.py:428
  38.2 2.6 %collective-permute-start.2 = (bf16[224,256]{1,0:T(8,128)(2,1)S(1)}, bf16[224,256]{1,0:T(8,128)(2,1)S(1)}, u32[]{:S(2)}, u32[]{:S(2)}) collective-permute-start(bf16[224,256]{1,0:T(8,128)(2,1)S(1)} %pad_maximum_fusion.2), channel_id=1, source_target_pairs={{0,1},{1,2},{2,3},{3,4},{4,5},{5,6},{6,7},{7,8},{8,9},{9,10},{10,1... | collective-permute-start | bytes 344072 | tf_op jit(solution)/shard_map/ppermute | solution.py:428
  40.8 0.8 %collective-permute-done.3.near_down = bf16[224,256]{1,0:T(8,128)(2,1)S(1)} collective-permute-done((bf16[224,256]{1,0:T(8,128)(2,1)S(1)}, bf16[224,256]{1,0:T(8,128)(2,1)S(1)}, u32[]{:S(2)}, u32[]{:S(2)}) %collective-permute-start.3) | collective-permute-done | bytes 114720 | tf_op jit(solution)/shard_map/ppermute | solution.py:428
  41.6 3.3 %collective-permute-done.2.near_up = bf16[224,256]{1,0:T(8,128)(2,1)S(1)} collective-permute-done((bf16[224,256]{1,0:T(8,128)(2,1)S(1)}, bf16[224,256]{1,0:T(8,128)(2,1)S(1)}, u32[]{:S(2)}, u32[]{:S(2)}) %collective-permute-start.2) | collective-permute-done | bytes 114720 | tf_op jit(solution)/shard_map/ppermute | solution.py:428
  44.9 4.3 %collective-permute-start.5 = (bf16[256,256]{1,0:T(8,128)(2,1)S(1)}, bf16[256,256]{1,0:T(8,128)(2,1)S(1)}, u32[]{:S(2)}, u32[]{:S(2)}) collective-permute-start(bf16[256,256]{1,0:T(8,128)(2,1)S(1)} %get-tuple-element.23), channel_id=1, source_target_pairs={{0,62},{1,63},{2,0},{3,1},{4,2},{5,3},{6,4},{7,5},{8,6},{9,7},{10,... | collective-permute-start | bytes 393224 | tf_op jit(solution)/shard_map/ppermute | solution.py:428
  49.2 2.5 %collective-permute-start.4 = (bf16[256,256]{1,0:T(8,128)(2,1)S(1)}, bf16[256,256]{1,0:T(8,128)(2,1)S(1)}, u32[]{:S(2)}, u32[]{:S(2)}) collective-permute-start(bf16[256,256]{1,0:T(8,128)(2,1)S(1)} %get-tuple-element.24), channel_id=1, source_target_pairs={{0,2},{1,3},{2,4},{3,5},{4,6},{5,7},{6,8},{7,9},{8,10},{9,11},{10,... | collective-permute-start | bytes 393224 | tf_op jit(solution)/shard_map/ppermute | solution.py:428
  51.7 0.0 copy-done.3
  51.7 0.0 copy-done.4
  51.7 0.0 copy-done.6
  51.7 0.0 copy-done.7
  51.7 0.0 copy-done.8
  51.7 0.0 copy-start
  51.7 0.0 copy-start.1
  51.8 0.0 copy-start.2
  51.8 0.0 copy-start.5
  51.8 4.6 %first.1 = (f32[136,256]{1,0:T(8,128)S(1)}, bf16[27,128,256]{2,1,0:T(8,128)(2,1)S(1)}, bf16[27,128,256]{2,1,0:T(8,128)(2,1)S(1)}) custom-call(s32[1]{0:T(128)S(6)} %copy.14.width_ref, f32[3]{0:T(128)S(1)} %copy-done.6, f32[16,256]{1,0:T(8,128)S(1)} %copy-done.8, bf16[32,256]{1,0:T(8,128)(2,1)S(1)} %collective-permute-done.up3, ...), custom_call_target="tpu_custom_call" | custom-call | flops 3355443200 | bytes 1048576 | tf_op jit(solution)/shard_map/first/pallas_call | solution.py:453
  56.4 0.0 collective-permute-done.5.far_down
  56.4 5.3 %collective-permute-done.4.far_up = bf16[256,256]{1,0:T(8,128)(2,1)S(1)} collective-permute-done((bf16[256,256]{1,0:T(8,128)(2,1)S(1)}, bf16[256,256]{1,0:T(8,128)(2,1)S(1)}, u32[]{:S(2)}, u32[]{:S(2)}) %collective-permute-start.4) | collective-permute-done | bytes 131104 | tf_op jit(solution)/shard_map/ppermute | solution.py:428
  61.7 0.0 copy-done.1
  61.7 15.0 %second.1 = f32[4,4,256]{2,1,0:T(4,128)} custom-call(s32[1]{0:T(128)S(6)} %copy.14.width_ref, f32[3]{0:T(128)S(1)} %copy-done.6, f32[136,256]{1,0:T(8,128)S(1)} %get-tuple-element.20.state_in, bf16[27,128,256]{2,1,0:T(8,128)(2,1)S(1)} %get-tuple-element.21.secondc0, bf16[27,128,256]{2,1,0:T(8,128)(2,1)S(1)} %get-tuple-element.22.seconde0, ...), custom_call_target="tpu_custom_call" | custom-call | flops 10066329600 | bytes 1048576 | tf_op jit(solution)/shard_map/second/pallas_call | solution.py:476
  (11 shorter events, 0.1 us)
Async XLA Ops:
  4.3 30.6 %copy-start.9 = (bf16[32,256]{1,0:T(8,128)(2,1)S(1)}, bf16[32,256]{1,0:T(8,128)(2,1)}, u32[]{:S(2)}) copy-start(bf16[32,256]{1,0:T(8,128)(2,1)} %get-tuple-element.16) | copy-start | bytes 49156
  4.3 47.4 %copy-start.3 = (bf16[9,128,128]{2,1,0:T(8,128)(2,1)S(1)}, bf16[9,128,128]{2,1,0:T(8,128)(2,1)}, u32[]{:S(2)}) copy-start(bf16[9,128,128]{2,1,0:T(8,128)(2,1)} %w_enc.3) | copy-start | bytes 884740
  4.3 47.4 %copy-start.4 = (bf16[9,128,4]{1,2,0:T(4,128)(2,1)S(1)}, bf16[9,128,4]{1,2,0:T(4,128)(2,1)}, u32[]{:S(2)}) copy-start(bf16[9,128,4]{1,2,0:T(4,128)(2,1)} %param.19) | copy-start | bytes 27652
  4.3 47.4 %copy-start.6 = (f32[3]{0:T(128)S(1)}, f32[3]{0:T(128)}, u32[]{:S(2)}) copy-start(f32[3]{0:T(128)} %sigma_ref.5) | copy-start | bytes 40
  4.3 47.4 %copy-start.7 = (f32[128]{0:T(128)S(1)}, f32[128]{0:T(128)}, u32[]{:S(2)}) copy-start(f32[128]{0:T(128)} %param.20) | copy-start | bytes 1540
  4.3 47.4 %copy-start.8 = (f32[16,256]{1,0:T(8,128)S(1)}, f32[16,256]{1,0:T(8,128)}, u32[]{:S(2)}) copy-start(f32[16,256]{1,0:T(8,128)} %get-tuple-element.14.own) | copy-start | bytes 49156
  4.4 30.5 %all-to-all-start = ((bf16[8,128,256]{2,1,0:T(8,128)(2,1)}), bf16[8,128,256]{2,1,0:T(8,128)(2,1)S(1)}, u32[]{:S(2)}, u32[]{:S(2)}) async-start(bf16[8,128,256]{2,1,0:T(8,128)(2,1)} %get-tuple-element.15), calls=%async_computation | async-start | bytes 1048576 | tf_op jit(solution)/shard_map/all_to_all | solution.py:534
  9.3 16.5 %collective-permute-start.1 = (bf16[32,256]{1,0:T(8,128)(2,1)}, bf16[32,256]{1,0:T(8,128)(2,1)S(1)}, u32[]{:S(2)}, u32[]{:S(2)}) collective-permute-start(bf16[32,256]{1,0:T(8,128)(2,1)} %get-tuple-element.16), channel_id=1, source_target_pairs={{0,61},{1,62},{2,63},{3,0},{4,1},{5,2},{6,3},{7,4},{8,5},{9,6},{10... | collective-permute-start | bytes 49160 | tf_op jit(solution)/shard_map/ppermute | solution.py:428
  23.9 11.0 %collective-permute-start = (bf16[32,256]{1,0:T(8,128)(2,1)}, bf16[32,256]{1,0:T(8,128)(2,1)S(1)}, u32[]{:S(2)}, u32[]{:S(2)}) collective-permute-start(bf16[32,256]{1,0:T(8,128)(2,1)} %get-tuple-element.16), channel_id=1, source_target_pairs={{0,3},{1,4},{2,5},{3,6},{4,7},{5,8},{6,9},{7,10},{8,11},{9,12},{10... | collective-permute-start | bytes 49160 | tf_op jit(solution)/shard_map/ppermute | solution.py:428
  34.9 6.7 %collective-permute-start.3 = (bf16[224,256]{1,0:T(8,128)(2,1)S(1)}, bf16[224,256]{1,0:T(8,128)(2,1)S(1)}, u32[]{:S(2)}, u32[]{:S(2)}) collective-permute-start(bf16[224,256]{1,0:T(8,128)(2,1)S(1)} %pad_maximum_fusion.2), channel_id=1, source_target_pairs={{0,63},{1,0},{2,1},{3,2},{4,3},{5,4},{6,5},{7,6},{8,7},{9,8},{10,9... | collective-permute-start | bytes 344072 | tf_op jit(solution)/shard_map/ppermute | solution.py:428
  38.2 6.7 %collective-permute-start.2 = (bf16[224,256]{1,0:T(8,128)(2,1)S(1)}, bf16[224,256]{1,0:T(8,128)(2,1)S(1)}, u32[]{:S(2)}, u32[]{:S(2)}) collective-permute-start(bf16[224,256]{1,0:T(8,128)(2,1)S(1)} %pad_maximum_fusion.2), channel_id=1, source_target_pairs={{0,1},{1,2},{2,3},{3,4},{4,5},{5,6},{6,7},{7,8},{8,9},{9,10},{10,1... | collective-permute-start | bytes 344072 | tf_op jit(solution)/shard_map/ppermute | solution.py:428
  44.9 11.4 %collective-permute-start.5 = (bf16[256,256]{1,0:T(8,128)(2,1)S(1)}, bf16[256,256]{1,0:T(8,128)(2,1)S(1)}, u32[]{:S(2)}, u32[]{:S(2)}) collective-permute-start(bf16[256,256]{1,0:T(8,128)(2,1)S(1)} %get-tuple-element.23), channel_id=1, source_target_pairs={{0,62},{1,63},{2,0},{3,1},{4,2},{5,3},{6,4},{7,5},{8,6},{9,7},{10,... | collective-permute-start | bytes 393224 | tf_op jit(solution)/shard_map/ppermute | solution.py:428
  49.2 12.5 %collective-permute-start.4 = (bf16[256,256]{1,0:T(8,128)(2,1)S(1)}, bf16[256,256]{1,0:T(8,128)(2,1)S(1)}, u32[]{:S(2)}, u32[]{:S(2)}) collective-permute-start(bf16[256,256]{1,0:T(8,128)(2,1)S(1)} %get-tuple-element.24), channel_id=1, source_target_pairs={{0,2},{1,3},{2,4},{3,5},{4,6},{5,7},{6,8},{7,9},{8,10},{9,11},{10,... | collective-permute-start | bytes 393224 | tf_op jit(solution)/shard_map/ppermute | solution.py:428
  51.7 10.0 %copy-start = (bf16[9,256,256]{2,1,0:T(8,128)(2,1)S(1)}, bf16[9,256,256]{2,1,0:T(8,128)(2,1)}, u32[]{:S(2)}) copy-start(bf16[9,256,256]{2,1,0:T(8,128)(2,1)} %w_mid.1) | copy-start | bytes 3538948
  51.7 10.0 %copy-start.1 = (bf16[9,128,384]{2,1,0:T(8,128)(2,1)S(1)}, bf16[9,128,384]{2,1,0:T(8,128)(2,1)}, u32[]{:S(2)}) copy-start(bf16[9,128,384]{2,1,0:T(8,128)(2,1)} %w_dec.1) | copy-start | bytes 2654212
  51.8 9.9 %copy-start.2 = (bf16[9,256,128]{2,1,0:T(8,128)(2,1)S(1)}, bf16[9,256,128]{2,1,0:T(8,128)(2,1)}, u32[]{:S(2)}) copy-start(bf16[9,256,128]{2,1,0:T(8,128)(2,1)} %w_down.1) | copy-start | bytes 1769476
  51.8 9.9 %copy-start.5 = (bf16[9,4,128]{2,1,0:T(4,128)(2,1)S(1)}, bf16[9,4,128]{2,1,0:T(4,128)(2,1)}, u32[]{:S(2)}) copy-start(bf16[9,4,128]{2,1,0:T(4,128)(2,1)} %w_out.1) | copy-start | bytes 27652

commit v7 on v5

--- a/solution.py
+++ b/solution.py
@@ -17,13 +17,12 @@
 NT = (((1,), (1,)), ((), ()))
 TN = (((0,), (0,)), ((), ()))
 
-BLOCKS = (5, 5, 3, 2)
-SCALED = (-7, 17)
-FIRST = (-6, 15)
-SECOND = (-5, 13)
-THIRD = (-2, 6)
-FOURTH = (-1, 4)
-FIFTH = (-1, 6)
+BLOCKS = (5, 5, 3, 2, 5, 6)
+FIELDS = ("scaled", "first", "second", "third", "fourth", "fifth", "out")
+STEP_ROWS = (
+    dict(zip(FIELDS, ((-7, 21), (-6, 19), (-5, 17), (-2, 8), (-1, 6), (-1, 10), (0, 8)))),
+    dict(zip(FIELDS, ((-7, 17), (-6, 15), (-5, 13), (-2, 6), (-1, 4), (-1, 6), (0, 4)))),
+)
 
 
 def silu_twice(h):
@@ -43,7 +42,7 @@
 
 
 def encode_kernel(
-    anchor_ref, width_ref, sigma_ref, blocks_ref, w_ref, noise_ref, out_ref, state_ref, scaled_ref, enc_ref, flat, wide
+    anchor_ref, width_ref, sigma_ref, blocks_ref, w_ref, noise_ref, out_ref, state_ref, scaled_ref, parts_ref, enc_ref, flat, wide
 ):
     band = lax.axis_index("band")
     tile = lax.axis_index("tile")
@@ -66,6 +65,10 @@
         row = sigma * noise_ref[:, r, :] * natural
         state_ref[4 * r : 4 * r + 4, :] = row
         scaled_ref[4 * r : 4 * r + 4, :] = (row * scale).astype(BF)
+    state = state_ref[...]
+    high = state.astype(BF)
+    parts_ref[0:16, :] = high
+    parts_ref[16:32, :] = (state - high.astype(F32)).astype(BF)
 
     w = 0.5 * w_ref[...].astype(F32)
     for half in range(2):
@@ -125,31 +128,22 @@
     return own, rim
 
 
-def form_small(w_in, w_out, in_o, out_o):
-    half = jnp.asarray(0.5, BF)
-
-    def tall(ref, a, b):
-        if not 0 <= b <= 2:
-            return jnp.zeros((8, 128), F32)
-        return jnp.concatenate([ref[3 * a + b].astype(F32), jnp.zeros((4, 128), F32)], 0)
-
-    in_o[...] = jnp.concatenate(
-        [
-            jnp.concatenate([tall(w_in, a, q - p) for p in range(2)], 1)
-            for a in range(3)
-            for q in range(4)
-        ],
-        0,
-    ).astype(BF)
-    in_o[...] = in_o[...] * half
-    out_o[...] = jnp.concatenate(
-        [
-            jnp.concatenate([tall(w_out, a, q - p) for q in (1, 2, 0, 3)], 1)
-            for a in range(3)
-            for p in range(2)
-        ],
-        0,
-    ).astype(BF)
+def tall(ref, a, b):
+    if not 0 <= b <= 2:
+        return jnp.zeros((8, 128), F32)
+    return jnp.concatenate([ref[3 * a + b].astype(F32), jnp.zeros((4, 128), F32)], 0)
+
+
+def form_in(w, out):
+    taps = [jnp.concatenate([tall(w, a, q - p) for p in range(2)], 1) for a in range(3) for q in range(4)]
+    out[...] = (0.5 * jnp.concatenate(taps, 0)).astype(BF)
+
+
+def form_out(w, out):
+    taps = [
+        jnp.concatenate([tall(w, a, q - p) for q in (1, 2, 0, 3)], 1) for a in range(3) for p in range(2)
+    ]
+    out[...] = jnp.concatenate(taps, 0).astype(BF)
 
 
 def form_pairs(w, chans, out):
@@ -243,41 +237,22 @@
     return jnp.concatenate([ref[at + step * k] for k in range(n)], 0)
 
 
-def step_kernel(
-    step, width_ref, sigma_ref, own, halo, cond_up, cond_own, cond_down, weights, state_ref, scaled_ref,
-    scaled, spread, firstc, firste, secondc, seconde, third, thirdl, thirdr, fourth, fourthl, fourthr,
-    fifthc, fifthe, prod, picked, masks,
-    f_in, f_out, f_enc, f_down, f_mid, f_dec, f_even, f_odd,
-):
-    w_sigma, w_in, w_out, w_enc, w_down, w_mid, w_dec = weights
-    field = Field(width_ref[0], masks)
-    sigma, scale, keep, mix, move = levels(sigma_ref, step)
-
-    empty = jnp.zeros((4, 256), F32)
-    scaled_lo = SCALED[0]
-    for tile_off, ref, begin in halo:
-        value = ref[begin : begin + 16, :].astype(F32)
-        for r in range(4):
-            rho = 4 * tile_off + r
-            if scaled_lo <= rho < scaled_lo + SCALED[1]:
-                row = jnp.concatenate([value[4 * r : 4 * r + 4], empty], 0)
-                scaled[8 * (rho - scaled_lo) : 8 * (rho - scaled_lo) + 8, :] = row * field.fine_ok(rho).astype(F32)
-    states = [own[4 * r : 4 * r + 4, :] for r in range(4)]
-    for r in range(4):
-        row = jnp.concatenate([(states[r] * scale).astype(BF).astype(F32), empty], 0)
-        scaled[8 * (r - scaled_lo) : 8 * (r - scaled_lo) + 8, :] = row
-
-    form_small(w_in, w_out, f_in, f_out)
-
+def encoder(field, rows, scaled, spread, bias, f_in, f_enc, firstc, firste, secondc, seconde):
+    n_state = rows["scaled"][1]
+    first_lo, n_first = rows["first"]
+    second_lo, n_second = rows["second"]
     col = lax.broadcasted_iota(jnp.int32, (256, 512), 0)
     place = lax.broadcasted_iota(jnp.int32, (256, 512), 1)
     pick = (col == 2 * (place % 128) + place // 128 - 1).astype(F32).astype(BF)
-    spread[...] = jnp.dot(scaled[...].astype(BF), pick, preferred_element_type=F32)
-    bias = 0.5 * embedding(w_sigma, sigma)
-    for at, n in parts(FIRST[1], BLOCKS[0]):
+    spread[0 : 8 * n_state, :] = jnp.dot(scaled[...].astype(BF), pick, preferred_element_type=F32)
+    for at, n in parts(n_first, BLOCKS[0]):
         cols = [
             jnp.concatenate(
-                [spread[8 * (k + a) : 8 * (k + a) + 8, 128 * q : 128 * q + 128] for a in range(3) for q in range(4)],
+                [
+                    spread[8 * (k + a) : 8 * (k + a) + 8, 128 * q : 128 * q + 128]
+                    for a in range(3)
+                    for q in range(4)
+                ],
                 0,
             )
             for k in range(at, at + n)
@@ -286,90 +261,128 @@
         y = lax.dot_general(x, f_in[...], TN, preferred_element_type=F32)
         for k in range(n):
             part = silu_twice(y[k * HALF : (k + 1) * HALF] + bias)
-            field.keep_pairs(part, firstc, firste, at + k, FIRST[0] + at + k)
-
-    form_pairs(w_enc, 128, f_enc)
-    for at, n in parts(SECOND[1], BLOCKS[1]):
+            field.keep_pairs(part, firstc, firste, at + k, first_lo + at + k)
+
+    for at, n in parts(n_second, BLOCKS[1]):
         x = jnp.concatenate([stacked(ref, at + a, n) for a in range(3) for ref in (firstc, firste)], 1)
         y = dot_nt(x, f_enc[...])
         for k in range(n):
             part = silu_twice(y[k * HALF : (k + 1) * HALF])
-            field.keep_pairs(part, secondc, seconde, at + k, SECOND[0] + at + k)
-
+            field.keep_pairs(part, secondc, seconde, at + k, second_lo + at + k)
+
+def step_kernel(
+    step, width_ref, sigma_ref, own, halo, conds, weights, state_ref, scaled_ref,
+    state, spread, firstc, firste, secondc, seconde, third, thirdl, thirdr, fourth, fourthl, fourthr,
+    fifthc, fifthe, prod, picked, masks,
+    f_in, f_out, f_enc, f_down, f_mid, f_dec, f_even, f_odd,
+):
+    w_sigma, w_in, w_out, w_enc, w_down, w_mid, w_dec = weights
+    field = Field(width_ref[0], masks)
+    form_in(w_in, f_in)
+    form_out(w_out, f_out)
+    form_pairs(w_enc, 128, f_enc)
     form_down(w_down, f_down)
+    form_mid(w_mid, f_mid)
+    form_pairs(w_dec, 128, f_dec)
+    form_up(w_dec, f_even, f_odd)
+    rows = STEP_ROWS[step]
+    sigma, scale, keep, mix, move = levels(sigma_ref, step)
+    scaled_lo, n_scaled = rows["scaled"]
+    second_lo = rows["second"][0]
+    third_lo, n_third = rows["third"]
+    fourth_lo, n_fourth = rows["fourth"]
+    fifth_lo, n_fifth = rows["fifth"]
+    n_out = rows["out"][1]
+
+    empty = jnp.zeros((4, 256), F32)
+    pieces = [(rho, ref[begin : begin + 4 * n, :].astype(F32), n) for rho, n, ref, begin in halo]
+    pieces += [(rho, (value * scale).astype(BF).astype(F32), n) for rho, value, n in own]
+    for lo, value, n in pieces:
+        for r in range(n):
+            rho = lo + r
+            if scaled_lo <= rho < scaled_lo + n_scaled:
+                row = jnp.concatenate([value[4 * r : 4 * r + 4], empty], 0)
+                at = 8 * (rho - scaled_lo)
+                state[at : at + 8, :] = row * field.fine_ok(rho).astype(F32)
+    weave_j = lax.broadcasted_iota(jnp.int32, (256, 256), 0)
+    weave_c = lax.broadcasted_iota(jnp.int32, (256, 256), 1)
+    weave = (weave_c == 2 * (weave_j % HALF) + weave_j // HALF).astype(F32).astype(BF)
     repeat = (
         lax.broadcasted_iota(jnp.int32, (HALF, 64), 0) // 2 == lax.broadcasted_iota(jnp.int32, (HALF, 64), 1)
     ).astype(F32)
     repeat = (0.5 * repeat).astype(BF)
-    add = [
-        jnp.dot(repeat, ref[64 * r : 64 * r + 64, :], preferred_element_type=F32)
-        for ref in (cond_up, cond_own, cond_down)
-        for r in range(2)
-    ]
-    for at, n in parts(THIRD[1], BLOCKS[2]):
-        begin = 2 * (THIRD[0] + at) - 1 - SECOND[0]
+    bias = 0.5 * embedding(w_sigma, sigma)
+    encoder(field, rows, state, spread, bias, f_in, f_enc, firstc, firste, secondc, seconde)
+
+    for at, n in parts(n_third, BLOCKS[2]):
+        begin = 2 * (third_lo + at) - 1 - second_lo
         x = jnp.concatenate(
             [stacked(secondc, begin + a, n, 2) for a in range(3)]
-            + [jnp.concatenate([seconde[begin + a + 2 * k][:, :128] for k in range(n)], 0) for a in range(3)],
+            + [
+                jnp.concatenate([seconde[begin + a + 2 * k][:, :128] for k in range(n)], 0)
+                for a in range(3)
+            ],
             1,
         )
         y = dot_nt(x, f_down[...])
         for k in range(n):
-            part = silu_twice(y[k * HALF : (k + 1) * HALF] + add[at + k])
-            field.keep_half(part, third, thirdl, thirdr, at + k, THIRD[0] + at + k)
-
-    form_mid(w_mid, f_mid)
-    for at, n in parts(FOURTH[1], BLOCKS[3]):
+            ref, r = conds[at + k]
+            add = jnp.dot(repeat, ref[64 * r : 64 * r + 64, :], preferred_element_type=F32)
+            part = silu_twice(y[k * HALF : (k + 1) * HALF] + add)
+            field.keep_half(part, third, thirdl, thirdr, at + k, third_lo + at + k)
+
+    for at, n in parts(n_fourth, BLOCKS[3]):
         x = jnp.concatenate(
             [stacked(ref, at + a, n) for a in range(3) for ref in (thirdl, third, thirdr)], 1
         )
         y = dot_nt(x, f_mid[...])
         for k in range(n):
             part = silu_twice(y[k * HALF : (k + 1) * HALF])
-            field.keep_half(part, fourth, fourthl, fourthr, at + k, FOURTH[0] + at + k)
-
-    form_pairs(w_dec, 128, f_dec)
-    form_up(w_dec, f_even, f_odd)
-    for at in range(2):
-        rho = FIFTH[0] + at
-        odd = rho % 2
-        n = FIFTH[1] // 2
-        begin = rho - 1 - SECOND[0]
-        h = (rho - odd) // 2 - FOURTH[0] - (0 if odd else 1)
-        x = jnp.concatenate(
-            [stacked(ref, begin + a, n, 2) for a in range(3) for ref in (secondc, seconde)], 1
-        )
-        z = jnp.concatenate(
-            [stacked(ref, h + a, n) for a in range(2) for ref in (fourthl, fourth, fourthr)], 1
-        )
-        y = dot_nt(x, f_dec[...]) + dot_nt(z, (f_odd if odd else f_even)[...])
-        for k in range(n):
-            part = silu_twice(y[k * HALF : (k + 1) * HALF])
-            field.keep_pairs(part, fifthc, fifthe, at + 2 * k, FIFTH[0] + at + 2 * k)
-
-    n = FIFTH[1]
-    x = jnp.concatenate([stacked(fifthc, 0, n), stacked(fifthe, 0, n)], 1)
-    prod[...] = dot_nt(f_out[...], x)
-    for k in range(4):
+            field.keep_half(part, fourth, fourthl, fourthr, at + k, fourth_lo + at + k)
+
+    for parity in range(2):
+        for cut, n in parts((n_fifth - parity + 1) // 2, BLOCKS[4]):
+            at = parity + 2 * cut
+            rho = fifth_lo + at
+            odd = rho % 2
+            begin = rho - 1 - second_lo
+            h = (rho - odd) // 2 - fourth_lo - (0 if odd else 1)
+            x = jnp.concatenate(
+                [stacked(ref, begin + a, n, 2) for a in range(3) for ref in (secondc, seconde)], 1
+            )
+            z = jnp.concatenate(
+                [stacked(ref, h + a, n) for a in range(2) for ref in (fourthl, fourth, fourthr)], 1
+            )
+            y = dot_nt(x, f_dec[...]) + dot_nt(z, (f_odd if odd else f_even)[...])
+            for k in range(n):
+                part = silu_twice(y[k * HALF : (k + 1) * HALF])
+                field.keep_pairs(part, fifthc, fifthe, at + 2 * k, fifth_lo + at + 2 * k)
+
+    for at, n in parts(n_fifth, BLOCKS[5]):
+        x = jnp.concatenate([stacked(fifthc, at, n), stacked(fifthe, at, n)], 1)
+        prod[:, at * HALF : (at + n) * HALF] = dot_nt(f_out[...], x)
+    for k in range(n_out):
         for p in range(2):
             picked[8 * k : 8 * k + 8, HALF * p : HALF * p + HALF] = sum(
                 prod[16 * a + 8 * p : 16 * a + 8 * p + 8, (k + a) * HALF : (k + a + 1) * HALF]
                 for a in range(3)
             )
-    high = picked[...].astype(BF)
-    low = (picked[...] - high.astype(F32)).astype(BF)
-    weave_j = lax.broadcasted_iota(jnp.int32, (256, 256), 0)
-    weave_c = lax.broadcasted_iota(jnp.int32, (256, 256), 1)
-    weave = (weave_c == 2 * (weave_j % HALF) + weave_j // HALF).astype(F32).astype(BF)
+    value = picked[0 : 8 * n_out, :]
+    high = value.astype(BF)
+    low = (value - high.astype(F32)).astype(BF)
     net = jnp.dot(high, weave, preferred_element_type=F32) + jnp.dot(low, weave, preferred_element_type=F32)
-    for r in range(4):
-        denoised = keep * states[r] + mix * net[8 * r : 8 * r + 4]
-        now = (states[r] + move * (states[r] - denoised)) * field.natural
+    states = jnp.concatenate([value for _, value, _ in own], 0)
+    if step == 0:
+        next_scale = levels(sigma_ref, 1)[1]
+    for k in range(n_out):
+        now = states[4 * k : 4 * k + 4]
+        denoised = keep * now + mix * net[8 * k : 8 * k + 4]
+        now = (now + move * (now - denoised)) * (field.natural * field.fine_ok(k).astype(F32))
         if step == 0:
-            state_ref[4 * r : 4 * r + 4, :] = now
-            scaled_ref[4 * r : 4 * r + 4, :] = (now * levels(sigma_ref, 1)[1]).astype(BF)
+            state_ref[4 * k : 4 * k + 4, :] = now
+            scaled_ref[4 * k : 4 * k + 4, :] = (now * next_scale).astype(BF)
         else:
-            state_ref[:, r, :] = now
+            state_ref[:, k, :] = now
 
 
 def turn(x, by):
@@ -396,37 +409,51 @@
     return pl.CostEstimate(flops=passes * 128 * 65536 * 2, bytes_accessed=1 << 20, transcendentals=0)
 
 
-def step_call(step, width, sigmas, own, pieces, conds, weights):
-    distinct = list(conds)
-    for array, _ in pieces:
-        if not any(array is d for d in distinct):
-            distinct.append(array)
-    place = [next(i for i, d in enumerate(distinct) if d is array) for array, _ in pieces]
-    outs = [jax.ShapeDtypeStruct((16, 256), F32), jax.ShapeDtypeStruct((16, 256), BF)]
-    if step == 1:
+def step_call(step, arrays, width, sigmas, weights):
+    rows = STEP_ROWS[step]
+    n_arrays, n_weights = len(arrays), len(weights)
+    n_out = rows["out"][1]
+    if step == 0:
+        outs = [jax.ShapeDtypeStruct((4 * n_out, 256), F32), jax.ShapeDtypeStruct((4 * n_out, 256), BF)]
+    else:
         outs = [jax.ShapeDtypeStruct((4, 4, 256), F32)]
-    n_arrays, n_weights = len(distinct), len(weights)
-
-    def kernel(width_ref, sigma_ref, own_ref, *refs):
-        arrays, refs = refs[:n_arrays], refs[n_arrays:]
+
+    def kernel(width_ref, sigma_ref, *refs):
+        held, refs = refs[:n_arrays], refs[n_arrays:]
         weight_refs, refs = refs[:n_weights], refs[n_weights:]
         out_refs, refs = list(refs[: len(outs)]), refs[len(outs) :]
-        halo = [(off, arrays[place[i]], pieces[i][1]) for i, off in enumerate((-2, -1, 1, 2))]
+        near_up, near_down, cond, cond_far = held[:4]
+        conds = [(ref, r) for ref in (near_up, cond, near_down, cond_far) for r in range(2)]
+        if step == 0:
+            own_ref, two_down = held[4:]
+            below = near_down[128:144, :].astype(F32) + near_down[144:160, :].astype(F32)
+            own = [(0, own_ref[...], 4), (4, below, 4)]
+            halo = [(-8, 8, near_up, 128), (8, 4, two_down, 0), (12, 4, near_down, 160)]
+        else:
+            own_ref, up, down, top = held[4:]
+            own = [(0, own_ref[...], 8)]
+            second = lax.axis_index("tile") == 1
+            near = jnp.where(second, top[...].astype(F32), up[16:32, :].astype(F32))
+            halo = [(-8, 4, up, 0), (-4, 4, near, 0), (8, 4, down, 0)]
         step_kernel(
-            step, width_ref, sigma_ref, own_ref, halo, *arrays[:3], weight_refs,
-            *(out_refs + [None])[:2], *refs,
+            step, width_ref, sigma_ref, own, halo, conds, weight_refs, *(out_refs + [None])[:2], *refs
         )
 
     return pl.pallas_call(
         kernel,
         out_shape=outs,
-        in_specs=[SMEM, SMEM] + [VMEM] * (1 + n_arrays + n_weights),
+        in_specs=[SMEM, SMEM] + [VMEM] * (n_arrays + n_weights),
         out_specs=[VMEM] * len(outs),
         scratch_shapes=[
-            pltpu.VMEM((SCALED[1] * 8, 256), F32), pltpu.VMEM((SCALED[1] * 8, 512), F32),
-            rowbuf(FIRST[1]), rowbuf(FIRST[1]), rowbuf(SECOND[1]), rowbuf(SECOND[1]),
-            *[rowbuf(THIRD[1])] * 3, *[rowbuf(FOURTH[1])] * 3, *[rowbuf(FIFTH[1])] * 2,
-            pltpu.VMEM((48, FIFTH[1] * HALF), F32), pltpu.VMEM((32, 256), F32), pltpu.VMEM((3, HALF, 256), F32),
+            pltpu.VMEM((rows["scaled"][1] * 8, 256), F32), pltpu.VMEM((rows["scaled"][1] * 8, 512), F32),
+            *[
+                rowbuf(rows[name][1])
+                for name, n in (("first", 2), ("second", 2), ("third", 3), ("fourth", 3), ("fifth", 2))
+                for _ in range(n)
+            ],
+            pltpu.VMEM((48, rows["fifth"][1] * HALF), F32),
+            pltpu.VMEM((8 * n_out, 256), F32),
+            pltpu.VMEM((3, HALF, 256), F32),
             *[
                 pltpu.VMEM(shape, BF)
                 for shape in (
@@ -436,9 +463,9 @@
             ],
         ],
         compiler_params=limit(LIMIT),
-        cost_estimate=cost(240),
+        cost_estimate=cost(300),
         name="step" + str(step),
-    )(width, sigmas, own, *distinct, *weights)
+    )(width, sigmas, *arrays, *weights)
 
 
 def encode_call(block_anchor, nest_width, sigmas, coarse_blocks, w_context, noise):
@@ -452,9 +479,10 @@
             jax.ShapeDtypeStruct((8, 2 * cells, 256), BF),
             jax.ShapeDtypeStruct((16, 256), F32),
             jax.ShapeDtypeStruct((16, 256), BF),
+            jax.ShapeDtypeStruct((32, 256), BF),
         ],
         in_specs=[SMEM, SMEM, SMEM, VMEM, VMEM, VMEM],
-        out_specs=[VMEM] * 3,
+        out_specs=[VMEM] * 4,
         scratch_shapes=[
             pltpu.VMEM((count + 8, cells, 256), F32),
             pltpu.VMEM((count * tiles + 64, 128), F32),
@@ -470,22 +498,26 @@
     coarse_blocks, block_anchor, nest_width, sigmas, noise,
     w_context, w_in, w_sigma, w_enc, w_down, w_mid, w_dec, w_out,
 ):
-    partial, state, scaled = encode_call(block_anchor, nest_width, sigmas, coarse_blocks, w_context, noise[0])
+    partial, state, scaled, own_parts = encode_call(
+        block_anchor, nest_width, sigmas, coarse_blocks, w_context, noise[0]
+    )
     arrived = lax.all_to_all(partial, "band", 0, 0, tiled=True)
 
-    up = turn(scaled, 1)
-    down = turn(scaled, -1)
-    arrived, up, down = lax.optimization_barrier((arrived, up, down))
+    one_up = turn(scaled, 1)
+    two_down = turn(scaled, -2)
+    arrived, one_up, two_down = lax.optimization_barrier((arrived, one_up, two_down))
 
     cond = (jnp.sum(arrived.astype(F32), axis=0) * (1.0 / math.sqrt(K // 2))).astype(BF)
-    near_up = turn(jnp.concatenate([cond, up, scaled], 0), 1)
-    near_down = turn(jnp.concatenate([cond, scaled, down], 0), -1)
-    conds = (near_up, cond, near_down)
+    cond_far = turn(cond, -2)
+    near_up = turn(jnp.concatenate([cond, one_up, scaled], 0), 1)
+    near_down = turn(jnp.concatenate([cond, own_parts, two_down], 0), -1)
     weights = (w_sigma.reshape(1, -1), w_in.transpose(0, 2, 1), w_out, w_enc, w_down, w_mid, w_dec)
-    pieces = ((near_up, 128), (near_up, 144), (near_down, 128), (near_down, 144))
-    state, scaled = step_call(0, nest_width, sigmas, state, pieces, conds, weights)
-    pieces = tuple((turn(scaled, by), 0) for by in (2, 1, -1, -2))
-    (out,) = step_call(1, nest_width, sigmas, state, pieces, conds, weights)
+    conds = (near_up, near_down, cond, cond_far)
+    state, scaled = step_call(0, (*conds, state, two_down), nest_width, sigmas, weights)
+    up = turn(scaled, 2)
+    down = turn(scaled[16:], -1)
+    top = lax.ppermute(scaled[:16], "tile", [(0, 1)])
+    (out,) = step_call(1, (*conds, state, up, down, top), nest_width, sigmas, weights)
     return out[None]
 
 

time: 75.7 us -> 75.3 us (level)
  waiting for transfers between devices: 17.8 us -> 12.9 us
  Pallas kernels: 16.5 us -> 18.4 us
  starting transfers between devices: 39.2 us -> 41.1 us
    ppermute x8 -> x7, waiting for transfers between devices: 17.8 us -> 12.9 us  [turn(): return lax.ppermute(x, 'tile', [(i, (i + by) % n) for i in range(n)])]
    ppermute x0 -> x1, starting transfers between devices: none -> 3.29 us  [per_device(): top = lax.ppermute(scaled[:16], 'tile', [(0, 1)])]
    pallas_call x2, Pallas kernels: 12.8 us -> 14.6 us  [step_call(): pl.pallas_call(kernel, out_shape=outs, in_specs=[SMEM, SMEM] + [VMEM] * (...]
    ppermute x8 -> x7, starting transfers between devices: 29.7 us -> 28.4 us  [turn(): return lax.ppermute(x, 'tile', [(i, (i + by) % n) for i in range(n)])]
  transfers between devices with their start and end apart: 9 -> 9, of which waited for: 5 -> 3; matrix products, arithmetic and copies ran while one was open for 0% -> 1% of each run, Pallas kernels for 0% -> 0%
where the time goes in v7:
time: 75.3 us; the launch traced here: 74.8 us
  starting transfers between devices  41.1 us (55%)
  Pallas kernels  18.4 us (24%)
  waiting for transfers between devices  12.9 us (17%)
  other arithmetic  1.51 us (2%)
  between operations  0.89 us (1%)
    ppermute x7, starting transfers between devices, turn(): return lax.ppermute(x, 'tile', [(i, (i + by) % n) for i in range(n)])  28.4 us
    pallas_call x2, Pallas kernels, step_call(): pl.pallas_call(kernel, out_shape=outs, in_specs=[SMEM, SMEM] + [VMEM] * (...  14.6 us
    ppermute x7, waiting for transfers between devices, turn(): return lax.ppermute(x, 'tile', [(i, (i + by) % n) for i in range(n)])  12.9 us
    all_to_all x1, starting transfers between devices, per_device(): arrived = lax.all_to_all(partial, 'band', 0, 0, tiled=True)  9.45 us
    pallas_call x1, Pallas kernels, encode_call(): pl.pallas_call(encode_kernel, out_shape=[jax.ShapeDtypeStruct((8, 2 * cel...  3.72 us
    ppermute x1, starting transfers between devices, per_device(): top = lax.ppermute(scaled[:16], 'tile', [(0, 1)])  3.29 us
  transfers between devices with their start and end apart: 9, of which 3 were waited for; matrix products, arithmetic and copies ran while one was open for 1% of the time, Pallas kernels for 0%

profile of v7, /device:TPU:2, one launch (start us, length us, event | category | flops | bytes accessed | tf_op | source)
XLA Modules:
  0.0 74.8 jit_solution(10698718886809246911)
XLA Ops:
  0.7 0.0 copy-start.2
  0.7 0.0 copy-start.3
  0.7 3.7 %encode.1 = (bf16[8,128,256]{2,1,0:T(8,128)(2,1)}, f32[16,256]{1,0:T(8,128)}, bf16[16,256]{1,0:T(8,128)(2,1)}, bf16[32,256]{1,0:T(8,128)(2,1)}) custom-call(s32[8,64]{1,0:T(8,128)} %anchor_ref.1, s32[1]{0:T(128)S(6)} %copy.14.width_ref, f32[3]{0:T(128)} %sigma_ref.5, bf16[64,4480]{1,0:T(8,128)(2,1)} %blocks_ref.1, bf16[70,256]{1,0:T(8,128)(2,1)} %bitcast.9, ...), custom_call_target="tpu_custom_call" | custom-call | flops 1677721600 | bytes 1048576 | tf_op jit(solution)/shard_map/encode/pallas_call | solution.py:476
  4.4 0.0 copy-start.4
  4.4 0.0 copy-start.5
  4.4 0.0 copy-start.6
  4.4 0.0 copy-start.7
  4.5 0.0 copy-start.8
  4.5 9.5 %all-to-all-start = ((bf16[8,128,256]{2,1,0:T(8,128)(2,1)}), bf16[8,128,256]{2,1,0:T(8,128)(2,1)S(1)}, u32[]{:S(2)}, u32[]{:S(2)}) async-start(bf16[8,128,256]{2,1,0:T(8,128)(2,1)} %get-tuple-element.14), calls=%async_computation | async-start | bytes 1048576 | tf_op jit(solution)/shard_map/all_to_all | solution.py:504
  13.9 10.1 %collective-permute-start.1 = (bf16[16,256]{1,0:T(8,128)(2,1)}, bf16[16,256]{1,0:T(8,128)(2,1)S(1)}, u32[]{:S(2)}, u32[]{:S(2)}) collective-permute-start(bf16[16,256]{1,0:T(8,128)(2,1)} %get-tuple-element.15), channel_id=1, source_target_pairs={{0,62},{1,63},{2,0},{3,1},{4,2},{5,3},{6,4},{7,5},{8,6},{9,7},{10,... | collective-permute-start | bytes 24584 | tf_op jit(solution)/shard_map/ppermute | solution.py:390
  24.1 2.6 %collective-permute-start = (bf16[16,256]{1,0:T(8,128)(2,1)}, bf16[16,256]{1,0:T(8,128)(2,1)S(1)}, u32[]{:S(2)}, u32[]{:S(2)}) collective-permute-start(bf16[16,256]{1,0:T(8,128)(2,1)} %get-tuple-element.15), channel_id=1, source_target_pairs={{0,1},{1,2},{2,3},{3,4},{4,5},{5,6},{6,7},{7,8},{8,9},{9,10},{10,1... | collective-permute-start | bytes 24584 | tf_op jit(solution)/shard_map/ppermute | solution.py:390
  26.7 0.0 collective-permute-done.1.refs_5_
  26.7 6.5 %collective-permute-done = bf16[16,256]{1,0:T(8,128)(2,1)S(1)} collective-permute-done((bf16[16,256]{1,0:T(8,128)(2,1)}, bf16[16,256]{1,0:T(8,128)(2,1)S(1)}, u32[]{:S(2)}, u32[]{:S(2)}) %collective-permute-start) | collective-permute-done | bytes 8224 | tf_op jit(solution)/shard_map/ppermute | solution.py:390
  33.1 0.0 all-to-all-done
  33.2 0.1 convert_reduce_fusion
  33.2 0.7 pad_maximum_fusion
  34.0 1.9 %collective-permute-start.3 = (bf16[176,256]{1,0:T(8,128)(2,1)S(1)}, bf16[176,256]{1,0:T(8,128)(2,1)S(1)}, u32[]{:S(2)}, u32[]{:S(2)}) collective-permute-start(bf16[176,256]{1,0:T(8,128)(2,1)S(1)} %pad_maximum_fusion), channel_id=1, source_target_pairs={{0,63},{1,0},{2,1},{3,2},{4,3},{5,4},{6,5},{7,6},{8,7},{9,8},{10,9... | collective-permute-start | bytes 270344 | tf_op jit(solution)/shard_map/ppermute | solution.py:390
  35.9 0.7 pad_maximum_fusion.1
  36.6 3.9 %collective-permute-start.2 = (bf16[160,256]{1,0:T(8,128)(2,1)S(1)}, bf16[160,256]{1,0:T(8,128)(2,1)S(1)}, u32[]{:S(2)}, u32[]{:S(2)}) collective-permute-start(bf16[160,256]{1,0:T(8,128)(2,1)S(1)} %pad_maximum_fusion.1), channel_id=1, source_target_pairs={{0,1},{1,2},{2,3},{3,4},{4,5},{5,6},{6,7},{7,8},{8,9},{9,10},{10,1... | collective-permute-start | bytes 245768 | tf_op jit(solution)/shard_map/ppermute | solution.py:390
  40.5 1.9 %collective-permute-start.4 = (bf16[128,256]{1,0:T(8,128)(2,1)S(1)}, bf16[128,256]{1,0:T(8,128)(2,1)S(1)}, u32[]{:S(2)}, u32[]{:S(2)}) collective-permute-start(bf16[128,256]{1,0:T(8,128)(2,1)S(1)} %multiply_convert_fusion.refs_2_), channel_id=1, source_target_pairs={{0,62},{1,63},{2,0},{3,1},{4,2},{5,3},{6,4},{7,5},{8,6},{9,7},{10,... | collective-permute-start | bytes 196616 | tf_op jit(solution)/shard_map/ppermute | solution.py:390
  42.4 5.3 %collective-permute-done.4.refs_3_ = bf16[128,256]{1,0:T(8,128)(2,1)S(1)} collective-permute-done((bf16[128,256]{1,0:T(8,128)(2,1)S(1)}, bf16[128,256]{1,0:T(8,128)(2,1)S(1)}, u32[]{:S(2)}, u32[]{:S(2)}) %collective-permute-start.4) | collective-permute-done | bytes 65568 | tf_op jit(solution)/shard_map/ppermute | solution.py:390
  47.7 0.0 collective-permute-done.2.refs_0_
  47.7 0.0 collective-permute-done.3.refs_1_
  47.7 0.0 copy-done.2
  47.8 7.8 %step0.1 = (f32[32,256]{1,0:T(8,128)S(1)}, bf16[32,256]{1,0:T(8,128)(2,1)S(1)}) custom-call(s32[1]{0:T(128)S(6)} %copy.14.width_ref, f32[3]{0:T(128)S(1)} %copy-done.6, bf16[160,256]{1,0:T(8,128)(2,1)S(1)} %collective-permute-done.2.refs_0_, bf16[176,256]{1,0:T(8,128)(2,1)S(1)} %collective-permute-done.3.refs_1_, ...), custom_call_target="tpu_custom_call" | custom-call | flops 5033164800 | bytes 1048576 | tf_op jit(solution)/shard_map/step0/pallas_call | solution.py:442
  55.6 1.9 %collective-permute-start.5 = (bf16[32,256]{1,0:T(8,128)(2,1)S(1)}, bf16[32,256]{1,0:T(8,128)(2,1)S(1)}, u32[]{:S(2)}, u32[]{:S(2)}) collective-permute-start(bf16[32,256]{1,0:T(8,128)(2,1)S(1)} %get-tuple-element.22), channel_id=1, source_target_pairs={{0,2},{1,3},{2,4},{3,5},{4,6},{5,7},{6,8},{7,9},{8,10},{9,11},{10,... | collective-permute-start | bytes 49160 | tf_op jit(solution)/shard_map/ppermute | solution.py:390
  57.6 3.3 %collective-permute-start.7 = (bf16[16,256]{1,0:T(8,128)(2,1)S(1)}, bf16[16,256]{1,0:T(8,128)(2,1)S(1)}, u32[]{:S(2)}, u32[]{:S(2)}) collective-permute-start(bf16[16,256]{1,0:T(8,128)(2,1)S(1)} %get-tuple-element.23), channel_id=1, source_target_pairs={{0,1},{64,65},{128,129},{192,193},{256,257},{320,321},{384,385},{4... | collective-permute-start | bytes 24584 | tf_op jit(solution)/shard_map/ppermute | solution.py:519
  60.9 6.0 %collective-permute-start.6 = (bf16[16,256]{1,0:T(8,128)(2,1)S(1)}, bf16[16,256]{1,0:T(8,128)(2,1)S(1)}, u32[]{:S(2)}, u32[]{:S(2)}) collective-permute-start(bf16[16,256]{1,0:T(8,128)(2,1)S(1)} %get-tuple-element.24), channel_id=1, source_target_pairs={{0,63},{1,0},{2,1},{3,2},{4,3},{5,4},{6,5},{7,6},{8,7},{9,8},{10,9... | collective-permute-start | bytes 24584 | tf_op jit(solution)/shard_map/ppermute | solution.py:390
  66.8 0.0 collective-permute-done.7.refs_7_
  66.8 1.2 %collective-permute-done.6.refs_6_ = bf16[16,256]{1,0:T(8,128)(2,1)S(1)} collective-permute-done((bf16[16,256]{1,0:T(8,128)(2,1)S(1)}, bf16[16,256]{1,0:T(8,128)(2,1)S(1)}, u32[]{:S(2)}, u32[]{:S(2)}) %collective-permute-start.6) | collective-permute-done | bytes 8224 | tf_op jit(solution)/shard_map/ppermute | solution.py:390
  68.0 0.0 collective-permute-done.5.refs_5_
  68.0 6.8 %step1.1 = f32[4,4,256]{2,1,0:T(4,128)} custom-call(s32[1]{0:T(128)S(6)} %copy.14.width_ref, f32[3]{0:T(128)S(1)} %copy-done.6, bf16[160,256]{1,0:T(8,128)(2,1)S(1)} %collective-permute-done.2.refs_0_, bf16[176,256]{1,0:T(8,128)(2,1)S(1)} %collective-permute-done.3.refs_1_, bf16[128,256]{1,0:T(8,128)(2,1)S(1)} %multiply_convert_fusion.refs_2_, ...), custom_call_target="tpu_custom_call" | custom-call | flops 5033164800 | bytes 1048576 | tf_op jit(solution)/shard_map/step1/pallas_call | solution.py:442
  (12 shorter events, 0.0 us)
Async XLA Ops:
  0.7 47.1 %copy-start.2 = (bf16[9,256,128]{2,1,0:T(8,128)(2,1)S(1)}, bf16[9,256,128]{2,1,0:T(8,128)(2,1)}, u32[]{:S(2)}) copy-start(bf16[9,256,128]{2,1,0:T(8,128)(2,1)} %refs_12_.3) | copy-start | bytes 1769476
  0.7 47.1 %copy-start.3 = (bf16[9,128,128]{2,1,0:T(8,128)(2,1)S(1)}, bf16[9,128,128]{2,1,0:T(8,128)(2,1)}, u32[]{:S(2)}) copy-start(bf16[9,128,128]{2,1,0:T(8,128)(2,1)} %refs_11_.3) | copy-start | bytes 884740
  4.4 43.3 %copy-start = (bf16[9,256,256]{2,1,0:T(8,128)(2,1)S(1)}, bf16[9,256,256]{2,1,0:T(8,128)(2,1)}, u32[]{:S(2)}) copy-start(bf16[9,256,256]{2,1,0:T(8,128)(2,1)} %refs_13_.1) | copy-start | bytes 3538948
  4.4 43.4 %copy-start.1 = (bf16[9,128,384]{2,1,0:T(8,128)(2,1)S(1)}, bf16[9,128,384]{2,1,0:T(8,128)(2,1)}, u32[]{:S(2)}) copy-start(bf16[9,128,384]{2,1,0:T(8,128)(2,1)} %refs_14_.1) | copy-start | bytes 2654212
  4.4 43.4 %copy-start.4 = (bf16[9,128,4]{1,2,0:T(4,128)(2,1)S(1)}, bf16[9,128,4]{1,2,0:T(4,128)(2,1)}, u32[]{:S(2)}) copy-start(bf16[9,128,4]{1,2,0:T(4,128)(2,1)} %param.19) | copy-start | bytes 27652
  4.4 43.4 %copy-start.5 = (bf16[9,4,128]{2,1,0:T(4,128)(2,1)S(1)}, bf16[9,4,128]{2,1,0:T(4,128)(2,1)}, u32[]{:S(2)}) copy-start(bf16[9,4,128]{2,1,0:T(4,128)(2,1)} %refs_10_.3) | copy-start | bytes 27652
  4.4 43.4 %copy-start.6 = (f32[3]{0:T(128)S(1)}, f32[3]{0:T(128)}, u32[]{:S(2)}) copy-start(f32[3]{0:T(128)} %sigma_ref.5) | copy-start | bytes 40
  4.4 43.4 %copy-start.7 = (f32[128]{0:T(128)S(1)}, f32[128]{0:T(128)}, u32[]{:S(2)}) copy-start(f32[128]{0:T(128)} %param.20) | copy-start | bytes 1540
  4.5 43.4 %copy-start.8 = (f32[16,256]{1,0:T(8,128)S(1)}, f32[16,256]{1,0:T(8,128)}, u32[]{:S(2)}) copy-start(f32[16,256]{1,0:T(8,128)} %get-tuple-element.20.refs_4_) | copy-start | bytes 49156
  4.5 28.7 %all-to-all-start = ((bf16[8,128,256]{2,1,0:T(8,128)(2,1)}), bf16[8,128,256]{2,1,0:T(8,128)(2,1)S(1)}, u32[]{:S(2)}, u32[]{:S(2)}) async-start(bf16[8,128,256]{2,1,0:T(8,128)(2,1)} %get-tuple-element.14), calls=%async_computation | async-start | bytes 1048576 | tf_op jit(solution)/shard_map/all_to_all | solution.py:504
  13.9 12.7 %collective-permute-start.1 = (bf16[16,256]{1,0:T(8,128)(2,1)}, bf16[16,256]{1,0:T(8,128)(2,1)S(1)}, u32[]{:S(2)}, u32[]{:S(2)}) collective-permute-start(bf16[16,256]{1,0:T(8,128)(2,1)} %get-tuple-element.15), channel_id=1, source_target_pairs={{0,62},{1,63},{2,0},{3,1},{4,2},{5,3},{6,4},{7,5},{8,6},{9,7},{10,... | collective-permute-start | bytes 24584 | tf_op jit(solution)/shard_map/ppermute | solution.py:390
  24.1 9.1 %collective-permute-start = (bf16[16,256]{1,0:T(8,128)(2,1)}, bf16[16,256]{1,0:T(8,128)(2,1)S(1)}, u32[]{:S(2)}, u32[]{:S(2)}) collective-permute-start(bf16[16,256]{1,0:T(8,128)(2,1)} %get-tuple-element.15), channel_id=1, source_target_pairs={{0,1},{1,2},{2,3},{3,4},{4,5},{5,6},{6,7},{7,8},{8,9},{9,10},{10,1... | collective-permute-start | bytes 24584 | tf_op jit(solution)/shard_map/ppermute | solution.py:390
  34.0 13.8 %collective-permute-start.3 = (bf16[176,256]{1,0:T(8,128)(2,1)S(1)}, bf16[176,256]{1,0:T(8,128)(2,1)S(1)}, u32[]{:S(2)}, u32[]{:S(2)}) collective-permute-start(bf16[176,256]{1,0:T(8,128)(2,1)S(1)} %pad_maximum_fusion), channel_id=1, source_target_pairs={{0,63},{1,0},{2,1},{3,2},{4,3},{5,4},{6,5},{7,6},{8,7},{9,8},{10,9... | collective-permute-start | bytes 270344 | tf_op jit(solution)/shard_map/ppermute | solution.py:390
  36.6 11.1 %collective-permute-start.2 = (bf16[160,256]{1,0:T(8,128)(2,1)S(1)}, bf16[160,256]{1,0:T(8,128)(2,1)S(1)}, u32[]{:S(2)}, u32[]{:S(2)}) collective-permute-start(bf16[160,256]{1,0:T(8,128)(2,1)S(1)} %pad_maximum_fusion.1), channel_id=1, source_target_pairs={{0,1},{1,2},{2,3},{3,4},{4,5},{5,6},{6,7},{7,8},{8,9},{9,10},{10,1... | collective-permute-start | bytes 245768 | tf_op jit(solution)/shard_map/ppermute | solution.py:390
  40.5 7.2 %collective-permute-start.4 = (bf16[128,256]{1,0:T(8,128)(2,1)S(1)}, bf16[128,256]{1,0:T(8,128)(2,1)S(1)}, u32[]{:S(2)}, u32[]{:S(2)}) collective-permute-start(bf16[128,256]{1,0:T(8,128)(2,1)S(1)} %multiply_convert_fusion.refs_2_), channel_id=1, source_target_pairs={{0,62},{1,63},{2,0},{3,1},{4,2},{5,3},{6,4},{7,5},{8,6},{9,7},{10,... | collective-permute-start | bytes 196616 | tf_op jit(solution)/shard_map/ppermute | solution.py:390
  55.6 12.4 %collective-permute-start.5 = (bf16[32,256]{1,0:T(8,128)(2,1)S(1)}, bf16[32,256]{1,0:T(8,128)(2,1)S(1)}, u32[]{:S(2)}, u32[]{:S(2)}) collective-permute-start(bf16[32,256]{1,0:T(8,128)(2,1)S(1)} %get-tuple-element.22), channel_id=1, source_target_pairs={{0,2},{1,3},{2,4},{3,5},{4,6},{5,7},{6,8},{7,9},{8,10},{9,11},{10,... | collective-permute-start | bytes 49160 | tf_op jit(solution)/shard_map/ppermute | solution.py:390
  57.6 9.3 %collective-permute-start.7 = (bf16[16,256]{1,0:T(8,128)(2,1)S(1)}, bf16[16,256]{1,0:T(8,128)(2,1)S(1)}, u32[]{:S(2)}, u32[]{:S(2)}) collective-permute-start(bf16[16,256]{1,0:T(8,128)(2,1)S(1)} %get-tuple-element.23), channel_id=1, source_target_pairs={{0,1},{64,65},{128,129},{192,193},{256,257},{320,321},{384,385},{4... | collective-permute-start | bytes 24584 | tf_op jit(solution)/shard_map/ppermute | solution.py:519
  60.9 7.1 %collective-permute-start.6 = (bf16[16,256]{1,0:T(8,128)(2,1)S(1)}, bf16[16,256]{1,0:T(8,128)(2,1)S(1)}, u32[]{:S(2)}, u32[]{:S(2)}) collective-permute-start(bf16[16,256]{1,0:T(8,128)(2,1)S(1)} %get-tuple-element.24), channel_id=1, source_target_pairs={{0,63},{1,0},{2,1},{3,2},{4,3},{5,4},{6,5},{7,6},{8,7},{9,8},{10,9... | collective-permute-start | bytes 24584 | tf_op jit(solution)/shard_map/ppermute | solution.py:390

commit v8 on v7

--- a/solution.py
+++ b/solution.py
@@ -17,7 +17,7 @@
 NT = (((1,), (1,)), ((), ()))
 TN = (((0,), (0,)), ((), ()))
 
-BLOCKS = (5, 5, 3, 2, 5, 6)
+BLOCKS = ((5, 5, 3, 2, 5, 6), (4, 4, 4, 3, 3, 5))
 FIELDS = ("scaled", "first", "second", "third", "fourth", "fifth", "out")
 STEP_ROWS = (
     dict(zip(FIELDS, ((-7, 21), (-6, 19), (-5, 17), (-2, 8), (-1, 6), (-1, 10), (0, 8)))),
@@ -237,7 +237,7 @@
     return jnp.concatenate([ref[at + step * k] for k in range(n)], 0)
 
 
-def encoder(field, rows, scaled, spread, bias, f_in, f_enc, firstc, firste, secondc, seconde):
+def encoder(field, rows, blocks, scaled, spread, bias, f_in, f_enc, firstc, firste, secondc, seconde):
     n_state = rows["scaled"][1]
     first_lo, n_first = rows["first"]
     second_lo, n_second = rows["second"]
@@ -245,7 +245,7 @@
     place = lax.broadcasted_iota(jnp.int32, (256, 512), 1)
     pick = (col == 2 * (place % 128) + place // 128 - 1).astype(F32).astype(BF)
     spread[0 : 8 * n_state, :] = jnp.dot(scaled[...].astype(BF), pick, preferred_element_type=F32)
-    for at, n in parts(n_first, BLOCKS[0]):
+    for at, n in parts(n_first, blocks[0]):
         cols = [
             jnp.concatenate(
                 [
@@ -263,7 +263,7 @@
             part = silu_twice(y[k * HALF : (k + 1) * HALF] + bias)
             field.keep_pairs(part, firstc, firste, at + k, first_lo + at + k)
 
-    for at, n in parts(n_second, BLOCKS[1]):
+    for at, n in parts(n_second, blocks[1]):
         x = jnp.concatenate([stacked(ref, at + a, n) for a in range(3) for ref in (firstc, firste)], 1)
         y = dot_nt(x, f_enc[...])
         for k in range(n):
@@ -312,9 +312,9 @@
     ).astype(F32)
     repeat = (0.5 * repeat).astype(BF)
     bias = 0.5 * embedding(w_sigma, sigma)
-    encoder(field, rows, state, spread, bias, f_in, f_enc, firstc, firste, secondc, seconde)
-
-    for at, n in parts(n_third, BLOCKS[2]):
+    encoder(field, rows, BLOCKS[step], state, spread, bias, f_in, f_enc, firstc, firste, secondc, seconde)
+
+    for at, n in parts(n_third, BLOCKS[step][2]):
         begin = 2 * (third_lo + at) - 1 - second_lo
         x = jnp.concatenate(
             [stacked(secondc, begin + a, n, 2) for a in range(3)]
@@ -331,7 +331,7 @@
             part = silu_twice(y[k * HALF : (k + 1) * HALF] + add)
             field.keep_half(part, third, thirdl, thirdr, at + k, third_lo + at + k)
 
-    for at, n in parts(n_fourth, BLOCKS[3]):
+    for at, n in parts(n_fourth, BLOCKS[step][3]):
         x = jnp.concatenate(
             [stacked(ref, at + a, n) for a in range(3) for ref in (thirdl, third, thirdr)], 1
         )
@@ -341,7 +341,7 @@
             field.keep_half(part, fourth, fourthl, fourthr, at + k, fourth_lo + at + k)
 
     for parity in range(2):
-        for cut, n in parts((n_fifth - parity + 1) // 2, BLOCKS[4]):
+        for cut, n in parts((n_fifth - parity + 1) // 2, BLOCKS[step][4]):
             at = parity + 2 * cut
             rho = fifth_lo + at
             odd = rho % 2
@@ -358,7 +358,7 @@
                 part = silu_twice(y[k * HALF : (k + 1) * HALF])
                 field.keep_pairs(part, fifthc, fifthe, at + 2 * k, fifth_lo + at + 2 * k)
 
-    for at, n in parts(n_fifth, BLOCKS[5]):
+    for at, n in parts(n_fifth, BLOCKS[step][5]):
         x = jnp.concatenate([stacked(fifthc, at, n), stacked(fifthe, at, n)], 1)
         prod[:, at * HALF : (at + n) * HALF] = dot_nt(f_out[...], x)
     for k in range(n_out):
@@ -383,6 +383,32 @@
             scaled_ref[4 * k : 4 * k + 4, :] = (now * next_scale).astype(BF)
         else:
             state_ref[:, k, :] = now
+
+
+def pack_kernel(arrived, above, scaled, own_parts, below, cond, to_below, to_above):
+    for at in range(0, 128, 32):
+        total = arrived[0, at : at + 32, :].astype(F32)
+        for k in range(1, 8):
+            total = total + arrived[k, at : at + 32, :].astype(F32)
+        total = (total * (1.0 / math.sqrt(K // 2))).astype(BF)
+        for ref in (cond, to_below, to_above):
+            ref[at : at + 32, :] = total
+    to_below[128:144, :] = above[...]
+    to_below[144:160, :] = scaled[...]
+    to_above[128:160, :] = own_parts[...]
+    to_above[160:176, :] = below[...]
+
+
+def pack_call(*args):
+    return pl.pallas_call(
+        pack_kernel,
+        out_shape=[jax.ShapeDtypeStruct((n, 256), BF) for n in (128, 160, 176)],
+        in_specs=[VMEM] * 5,
+        out_specs=[VMEM] * 3,
+        compiler_params=limit(4),
+        cost_estimate=cost(4),
+        name="pack",
+    )(*args)
 
 
 def turn(x, by):
@@ -507,10 +533,10 @@
     two_down = turn(scaled, -2)
     arrived, one_up, two_down = lax.optimization_barrier((arrived, one_up, two_down))
 
-    cond = (jnp.sum(arrived.astype(F32), axis=0) * (1.0 / math.sqrt(K // 2))).astype(BF)
+    cond, to_below, to_above = pack_call(arrived, one_up, scaled, own_parts, two_down)
+    near_up = turn(to_below, 1)
+    near_down = turn(to_above, -1)
     cond_far = turn(cond, -2)
-    near_up = turn(jnp.concatenate([cond, one_up, scaled], 0), 1)
-    near_down = turn(jnp.concatenate([cond, own_parts, two_down], 0), -1)
     weights = (w_sigma.reshape(1, -1), w_in.transpose(0, 2, 1), w_out, w_enc, w_down, w_mid, w_dec)
     conds = (near_up, near_down, cond, cond_far)
     state, scaled = step_call(0, (*conds, state, two_down), nest_width, sigmas, weights)

time: 75.3 us -> 75 us (level)
  other arithmetic: 1.51 us -> 0 us
  local copies, waits for them, and re-layouts: 0.05 us -> 1.46 us
    concatenate x2 -> x0, other arithmetic: 1.43 us -> none  [the longest x1 0.73 us: per_device(): near_down = turn(jnp.concatenate([cond, own_parts, two_down], 0), -1)]
    unnamed x18 -> x22, local copies, waits for them, and re-layouts: 0.05 us -> 1.46 us
  transfers between devices with their start and end apart: 9 -> 9, of which waited for: 3 -> 3; matrix products, arithmetic and copies ran while one was open for 1% -> 0% of each run, Pallas kernels for 0% -> 0%
where the time goes in v8:
time: 75 us; the launch traced here: 74.5 us
  starting transfers between devices  41.1 us (55%)
  Pallas kernels  18.1 us (24%)
  waiting for transfers between devices  12.9 us (17%)
  local copies, waits for them, and re-layouts  1.46 us (2%)
  between operations  0.88 us (1%)
    ppermute x7, starting transfers between devices, turn(): return lax.ppermute(x, 'tile', [(i, (i + by) % n) for i in range(n)])  28.4 us
    pallas_call x2, Pallas kernels, step_call(): pl.pallas_call(kernel, out_shape=outs, in_specs=[SMEM, SMEM] + [VMEM] * (...  14.3 us
    ppermute x7, waiting for transfers between devices, turn(): return lax.ppermute(x, 'tile', [(i, (i + by) % n) for i in range(n)])  12.9 us
    all_to_all x1, starting transfers between devices, per_device(): arrived = lax.all_to_all(partial, 'band', 0, 0, tiled=True)  9.45 us
    pallas_call x1, Pallas kernels, encode_call(): pl.pallas_call(encode_kernel, out_shape=[jax.ShapeDtypeStruct((8, 2 * cel...  3.79 us
    ppermute x1, starting transfers between devices, per_device(): top = lax.ppermute(scaled[:16], 'tile', [(0, 1)])  3.29 us
  transfers between devices with their start and end apart: 9, of which 3 were waited for; matrix products, arithmetic and copies ran while one was open for 0% of the time, Pallas kernels for 0%

profile of v8, /device:TPU:2, one launch (start us, length us, event | category | flops | bytes accessed | tf_op | source)
XLA Modules:
  0.0 74.5 jit_solution(18377710882716381697)
XLA Ops:
  0.7 0.0 copy-start.2
  0.7 0.0 copy-start.4
  0.7 0.0 copy-start.5
  0.7 3.8 %encode.1 = (bf16[8,128,256]{2,1,0:T(8,128)(2,1)}, f32[16,256]{1,0:T(8,128)}, bf16[16,256]{1,0:T(8,128)(2,1)}, bf16[32,256]{1,0:T(8,128)(2,1)}) custom-call(s32[8,64]{1,0:T(8,128)} %anchor_ref.1, s32[1]{0:T(128)S(6)} %copy.14.width_ref, f32[3]{0:T(128)} %sigma_ref.5, bf16[64,4480]{1,0:T(8,128)(2,1)} %blocks_ref.1, bf16[70,256]{1,0:T(8,128)(2,1)} %bitcast.9, ...), custom_call_target="tpu_custom_call" | custom-call | flops 1677721600 | bytes 1048576 | tf_op jit(solution)/shard_map/encode/pallas_call | solution.py:502
  4.5 0.0 copy-start.7
  4.5 0.0 copy-start.8
  4.5 0.0 copy-start.9
  4.5 0.0 copy-start.10
  4.5 9.5 %all-to-all-start = ((bf16[8,128,256]{2,1,0:T(8,128)(2,1)}), bf16[8,128,256]{2,1,0:T(8,128)(2,1)S(1)}, u32[]{:S(2)}, u32[]{:S(2)}) async-start(bf16[8,128,256]{2,1,0:T(8,128)(2,1)} %get-tuple-element.17), calls=%async_computation | async-start | bytes 1048576 | tf_op jit(solution)/shard_map/all_to_all | solution.py:530
  14.0 10.1 %collective-permute-start.1 = (bf16[16,256]{1,0:T(8,128)(2,1)}, bf16[16,256]{1,0:T(8,128)(2,1)S(1)}, u32[]{:S(2)}, u32[]{:S(2)}) collective-permute-start(bf16[16,256]{1,0:T(8,128)(2,1)} %get-tuple-element.18.scaled), channel_id=1, source_target_pairs={{0,62},{1,63},{2,0},{3,1},{4,2},{5,3},{6,4},{7,5},{8,6},{9,7},{10,... | collective-permute-start | bytes 24584 | tf_op jit(solution)/shard_map/ppermute | solution.py:416
  24.1 2.6 %collective-permute-start = (bf16[16,256]{1,0:T(8,128)(2,1)}, bf16[16,256]{1,0:T(8,128)(2,1)S(1)}, u32[]{:S(2)}, u32[]{:S(2)}) collective-permute-start(bf16[16,256]{1,0:T(8,128)(2,1)} %get-tuple-element.18.scaled), channel_id=1, source_target_pairs={{0,1},{1,2},{2,3},{3,4},{4,5},{5,6},{6,7},{7,8},{8,9},{9,10},{10,1... | collective-permute-start | bytes 24584 | tf_op jit(solution)/shard_map/ppermute | solution.py:416
  26.7 0.0 collective-permute-done.1.below.refs_5_
  26.8 6.5 %collective-permute-done.above = bf16[16,256]{1,0:T(8,128)(2,1)S(1)} collective-permute-done((bf16[16,256]{1,0:T(8,128)(2,1)}, bf16[16,256]{1,0:T(8,128)(2,1)S(1)}, u32[]{:S(2)}, u32[]{:S(2)}) %collective-permute-start) | collective-permute-done | bytes 8224 | tf_op jit(solution)/shard_map/ppermute | solution.py:416
  33.2 0.0 all-to-all-done.arrived
  33.2 0.7 copy-done
  33.9 0.7 copy-done.1
  34.6 0.1 pack.1
  34.7 1.9 %collective-permute-start.3 = (bf16[176,256]{1,0:T(8,128)(2,1)S(1)}, bf16[176,256]{1,0:T(8,128)(2,1)S(1)}, u32[]{:S(2)}, u32[]{:S(2)}) collective-permute-start(bf16[176,256]{1,0:T(8,128)(2,1)S(1)} %get-tuple-element.24), channel_id=1, source_target_pairs={{0,63},{1,0},{2,1},{3,2},{4,3},{5,4},{6,5},{7,6},{8,7},{9,8},{10,9... | collective-permute-start | bytes 270344 | tf_op jit(solution)/shard_map/ppermute | solution.py:416
  36.6 3.9 %collective-permute-start.2 = (bf16[160,256]{1,0:T(8,128)(2,1)S(1)}, bf16[160,256]{1,0:T(8,128)(2,1)S(1)}, u32[]{:S(2)}, u32[]{:S(2)}) collective-permute-start(bf16[160,256]{1,0:T(8,128)(2,1)S(1)} %get-tuple-element.23), channel_id=1, source_target_pairs={{0,1},{1,2},{2,3},{3,4},{4,5},{5,6},{6,7},{7,8},{8,9},{9,10},{10,1... | collective-permute-start | bytes 245768 | tf_op jit(solution)/shard_map/ppermute | solution.py:416
  40.6 1.9 %collective-permute-start.4 = (bf16[128,256]{1,0:T(8,128)(2,1)S(1)}, bf16[128,256]{1,0:T(8,128)(2,1)S(1)}, u32[]{:S(2)}, u32[]{:S(2)}) collective-permute-start(bf16[128,256]{1,0:T(8,128)(2,1)S(1)} %get-tuple-element.25.refs_2_), channel_id=1, source_target_pairs={{0,62},{1,63},{2,0},{3,1},{4,2},{5,3},{6,4},{7,5},{8,6},{9,7},{10,... | collective-permute-start | bytes 196616 | tf_op jit(solution)/shard_map/ppermute | solution.py:416
  42.5 5.3 %collective-permute-done.4.refs_3_ = bf16[128,256]{1,0:T(8,128)(2,1)S(1)} collective-permute-done((bf16[128,256]{1,0:T(8,128)(2,1)S(1)}, bf16[128,256]{1,0:T(8,128)(2,1)S(1)}, u32[]{:S(2)}, u32[]{:S(2)}) %collective-permute-start.4) | collective-permute-done | bytes 65568 | tf_op jit(solution)/shard_map/ppermute | solution.py:416
  47.8 0.0 collective-permute-done.2.refs_0_
  47.8 0.0 collective-permute-done.3.refs_1_
  47.8 0.0 copy-done.2
  47.9 7.8 %step0.1 = (f32[32,256]{1,0:T(8,128)S(1)}, bf16[32,256]{1,0:T(8,128)(2,1)S(1)}) custom-call(s32[1]{0:T(128)S(6)} %copy.14.width_ref, f32[3]{0:T(128)S(1)} %copy-done.8, bf16[160,256]{1,0:T(8,128)(2,1)S(1)} %collective-permute-done.2.refs_0_, bf16[176,256]{1,0:T(8,128)(2,1)S(1)} %collective-permute-done.3.refs_1_, ...), custom_call_target="tpu_custom_call" | custom-call | flops 5033164800 | bytes 1048576 | tf_op jit(solution)/shard_map/step0/pallas_call | solution.py:468
  55.7 1.9 %collective-permute-start.5 = (bf16[32,256]{1,0:T(8,128)(2,1)S(1)}, bf16[32,256]{1,0:T(8,128)(2,1)S(1)}, u32[]{:S(2)}, u32[]{:S(2)}) collective-permute-start(bf16[32,256]{1,0:T(8,128)(2,1)S(1)} %get-tuple-element.28), channel_id=1, source_target_pairs={{0,2},{1,3},{2,4},{3,5},{4,6},{5,7},{6,8},{7,9},{8,10},{9,11},{10,... | collective-permute-start | bytes 49160 | tf_op jit(solution)/shard_map/ppermute | solution.py:416
  57.6 3.3 %collective-permute-start.7 = (bf16[16,256]{1,0:T(8,128)(2,1)S(1)}, bf16[16,256]{1,0:T(8,128)(2,1)S(1)}, u32[]{:S(2)}, u32[]{:S(2)}) collective-permute-start(bf16[16,256]{1,0:T(8,128)(2,1)S(1)} %get-tuple-element.29), channel_id=1, source_target_pairs={{0,1},{64,65},{128,129},{192,193},{256,257},{320,321},{384,385},{4... | collective-permute-start | bytes 24584 | tf_op jit(solution)/shard_map/ppermute | solution.py:545
  60.9 6.0 %collective-permute-start.6 = (bf16[16,256]{1,0:T(8,128)(2,1)S(1)}, bf16[16,256]{1,0:T(8,128)(2,1)S(1)}, u32[]{:S(2)}, u32[]{:S(2)}) collective-permute-start(bf16[16,256]{1,0:T(8,128)(2,1)S(1)} %get-tuple-element.30), channel_id=1, source_target_pairs={{0,63},{1,0},{2,1},{3,2},{4,3},{5,4},{6,5},{7,6},{8,7},{9,8},{10,9... | collective-permute-start | bytes 24584 | tf_op jit(solution)/shard_map/ppermute | solution.py:416
  66.9 0.0 collective-permute-done.7.refs_7_
  66.9 1.2 %collective-permute-done.6.refs_6_ = bf16[16,256]{1,0:T(8,128)(2,1)S(1)} collective-permute-done((bf16[16,256]{1,0:T(8,128)(2,1)S(1)}, bf16[16,256]{1,0:T(8,128)(2,1)S(1)}, u32[]{:S(2)}, u32[]{:S(2)}) %collective-permute-start.6) | collective-permute-done | bytes 8224 | tf_op jit(solution)/shard_map/ppermute | solution.py:416
  68.0 0.0 collective-permute-done.5.refs_5_
  68.1 6.5 %step1.1 = f32[4,4,256]{2,1,0:T(4,128)} custom-call(s32[1]{0:T(128)S(6)} %copy.14.width_ref, f32[3]{0:T(128)S(1)} %copy-done.8, bf16[160,256]{1,0:T(8,128)(2,1)S(1)} %collective-permute-done.2.refs_0_, bf16[176,256]{1,0:T(8,128)(2,1)S(1)} %collective-permute-done.3.refs_1_, bf16[128,256]{1,0:T(8,128)(2,1)S(1)} %get-tuple-element.25.refs_2_, ...), custom_call_target="tpu_custom_call" | custom-call | flops 5033164800 | bytes 1048576 | tf_op jit(solution)/shard_map/step1/pallas_call | solution.py:468
  (13 shorter events, 0.0 us)
Async XLA Ops:
  0.7 47.1 %copy-start.2 = (bf16[9,256,256]{2,1,0:T(8,128)(2,1)S(1)}, bf16[9,256,256]{2,1,0:T(8,128)(2,1)}, u32[]{:S(2)}) copy-start(bf16[9,256,256]{2,1,0:T(8,128)(2,1)} %refs_13_.1) | copy-start | bytes 3538948
  0.7 47.1 %copy-start.4 = (bf16[9,256,128]{2,1,0:T(8,128)(2,1)S(1)}, bf16[9,256,128]{2,1,0:T(8,128)(2,1)}, u32[]{:S(2)}) copy-start(bf16[9,256,128]{2,1,0:T(8,128)(2,1)} %refs_12_.3) | copy-start | bytes 1769476
  0.7 47.1 %copy-start.5 = (bf16[9,128,128]{2,1,0:T(8,128)(2,1)S(1)}, bf16[9,128,128]{2,1,0:T(8,128)(2,1)}, u32[]{:S(2)}) copy-start(bf16[9,128,128]{2,1,0:T(8,128)(2,1)} %refs_11_.3) | copy-start | bytes 884740
  4.5 43.3 %copy-start.3 = (bf16[9,128,384]{2,1,0:T(8,128)(2,1)S(1)}, bf16[9,128,384]{2,1,0:T(8,128)(2,1)}, u32[]{:S(2)}) copy-start(bf16[9,128,384]{2,1,0:T(8,128)(2,1)} %refs_14_.1) | copy-start | bytes 2654212
  4.5 43.4 %copy-start.6 = (bf16[9,128,4]{1,2,0:T(4,128)(2,1)S(1)}, bf16[9,128,4]{1,2,0:T(4,128)(2,1)}, u32[]{:S(2)}) copy-start(bf16[9,128,4]{1,2,0:T(4,128)(2,1)} %param.19) | copy-start | bytes 27652
  4.5 43.4 %copy-start.7 = (bf16[9,4,128]{2,1,0:T(4,128)(2,1)S(1)}, bf16[9,4,128]{2,1,0:T(4,128)(2,1)}, u32[]{:S(2)}) copy-start(bf16[9,4,128]{2,1,0:T(4,128)(2,1)} %refs_10_.3) | copy-start | bytes 27652
  4.5 43.4 %copy-start.8 = (f32[3]{0:T(128)S(1)}, f32[3]{0:T(128)}, u32[]{:S(2)}) copy-start(f32[3]{0:T(128)} %sigma_ref.5) | copy-start | bytes 40
  4.5 43.3 %copy-start.9 = (f32[128]{0:T(128)S(1)}, f32[128]{0:T(128)}, u32[]{:S(2)}) copy-start(f32[128]{0:T(128)} %param.20) | copy-start | bytes 1540
  4.5 43.3 %copy-start.10 = (f32[16,256]{1,0:T(8,128)S(1)}, f32[16,256]{1,0:T(8,128)}, u32[]{:S(2)}) copy-start(f32[16,256]{1,0:T(8,128)} %get-tuple-element.26.refs_4_) | copy-start | bytes 49156
  4.5 28.7 %all-to-all-start = ((bf16[8,128,256]{2,1,0:T(8,128)(2,1)}), bf16[8,128,256]{2,1,0:T(8,128)(2,1)S(1)}, u32[]{:S(2)}, u32[]{:S(2)}) async-start(bf16[8,128,256]{2,1,0:T(8,128)(2,1)} %get-tuple-element.17), calls=%async_computation | async-start | bytes 1048576 | tf_op jit(solution)/shard_map/all_to_all | solution.py:530
  14.0 12.8 %collective-permute-start.1 = (bf16[16,256]{1,0:T(8,128)(2,1)}, bf16[16,256]{1,0:T(8,128)(2,1)S(1)}, u32[]{:S(2)}, u32[]{:S(2)}) collective-permute-start(bf16[16,256]{1,0:T(8,128)(2,1)} %get-tuple-element.18.scaled), channel_id=1, source_target_pairs={{0,62},{1,63},{2,0},{3,1},{4,2},{5,3},{6,4},{7,5},{8,6},{9,7},{10,... | collective-permute-start | bytes 24584 | tf_op jit(solution)/shard_map/ppermute | solution.py:416
  24.1 9.1 %collective-permute-start = (bf16[16,256]{1,0:T(8,128)(2,1)}, bf16[16,256]{1,0:T(8,128)(2,1)S(1)}, u32[]{:S(2)}, u32[]{:S(2)}) collective-permute-start(bf16[16,256]{1,0:T(8,128)(2,1)} %get-tuple-element.18.scaled), channel_id=1, source_target_pairs={{0,1},{1,2},{2,3},{3,4},{4,5},{5,6},{6,7},{7,8},{8,9},{9,10},{10,1... | collective-permute-start | bytes 24584 | tf_op jit(solution)/shard_map/ppermute | solution.py:416
  33.2 0.7 copy-start
  33.9 0.7 copy-start.1
  34.7 13.1 %collective-permute-start.3 = (bf16[176,256]{1,0:T(8,128)(2,1)S(1)}, bf16[176,256]{1,0:T(8,128)(2,1)S(1)}, u32[]{:S(2)}, u32[]{:S(2)}) collective-permute-start(bf16[176,256]{1,0:T(8,128)(2,1)S(1)} %get-tuple-element.24), channel_id=1, source_target_pairs={{0,63},{1,0},{2,1},{3,2},{4,3},{5,4},{6,5},{7,6},{8,7},{9,8},{10,9... | collective-permute-start | bytes 270344 | tf_op jit(solution)/shard_map/ppermute | solution.py:416
  36.6 11.1 %collective-permute-start.2 = (bf16[160,256]{1,0:T(8,128)(2,1)S(1)}, bf16[160,256]{1,0:T(8,128)(2,1)S(1)}, u32[]{:S(2)}, u32[]{:S(2)}) collective-permute-start(bf16[160,256]{1,0:T(8,128)(2,1)S(1)} %get-tuple-element.23), channel_id=1, source_target_pairs={{0,1},{1,2},{2,3},{3,4},{4,5},{5,6},{6,7},{7,8},{8,9},{9,10},{10,1... | collective-permute-start | bytes 245768 | tf_op jit(solution)/shard_map/ppermute | solution.py:416
  40.6 7.2 %collective-permute-start.4 = (bf16[128,256]{1,0:T(8,128)(2,1)S(1)}, bf16[128,256]{1,0:T(8,128)(2,1)S(1)}, u32[]{:S(2)}, u32[]{:S(2)}) collective-permute-start(bf16[128,256]{1,0:T(8,128)(2,1)S(1)} %get-tuple-element.25.refs_2_), channel_id=1, source_target_pairs={{0,62},{1,63},{2,0},{3,1},{4,2},{5,3},{6,4},{7,5},{8,6},{9,7},{10,... | collective-permute-start | bytes 196616 | tf_op jit(solution)/shard_map/ppermute | solution.py:416
  55.7 12.4 %collective-permute-start.5 = (bf16[32,256]{1,0:T(8,128)(2,1)S(1)}, bf16[32,256]{1,0:T(8,128)(2,1)S(1)}, u32[]{:S(2)}, u32[]{:S(2)}) collective-permute-start(bf16[32,256]{1,0:T(8,128)(2,1)S(1)} %get-tuple-element.28), channel_id=1, source_target_pairs={{0,2},{1,3},{2,4},{3,5},{4,6},{5,7},{6,8},{7,9},{8,10},{9,11},{10,... | collective-permute-start | bytes 49160 | tf_op jit(solution)/shard_map/ppermute | solution.py:416
  57.6 9.3 %collective-permute-start.7 = (bf16[16,256]{1,0:T(8,128)(2,1)S(1)}, bf16[16,256]{1,0:T(8,128)(2,1)S(1)}, u32[]{:S(2)}, u32[]{:S(2)}) collective-permute-start(bf16[16,256]{1,0:T(8,128)(2,1)S(1)} %get-tuple-element.29), channel_id=1, source_target_pairs={{0,1},{64,65},{128,129},{192,193},{256,257},{320,321},{384,385},{4... | collective-permute-start | bytes 24584 | tf_op jit(solution)/shard_map/ppermute | solution.py:545
  60.9 7.1 %collective-permute-start.6 = (bf16[16,256]{1,0:T(8,128)(2,1)S(1)}, bf16[16,256]{1,0:T(8,128)(2,1)S(1)}, u32[]{:S(2)}, u32[]{:S(2)}) collective-permute-start(bf16[16,256]{1,0:T(8,128)(2,1)S(1)} %get-tuple-element.30), channel_id=1, source_target_pairs={{0,63},{1,0},{2,1},{3,2},{4,3},{5,4},{6,5},{7,6},{8,7},{9,8},{10,9... | collective-permute-start | bytes 24584 | tf_op jit(solution)/shard_map/ppermute | solution.py:416

commit v9 on v8

--- a/solution.py
+++ b/solution.py
@@ -385,6 +385,11 @@
             state_ref[:, k, :] = now
 
 
+def hold_kernel(scaled, own_parts, scaled_out, parts_out):
+    scaled_out[...] = scaled[...]
+    parts_out[...] = own_parts[...]
+
+
 def pack_kernel(arrived, above, scaled, own_parts, below, cond, to_below, to_above):
     for at in range(0, 128, 32):
         total = arrived[0, at : at + 32, :].astype(F32)
@@ -399,15 +404,15 @@
     to_above[160:176, :] = below[...]
 
 
-def pack_call(*args):
+def small_call(kernel, name, sizes, *args):
     return pl.pallas_call(
-        pack_kernel,
-        out_shape=[jax.ShapeDtypeStruct((n, 256), BF) for n in (128, 160, 176)],
-        in_specs=[VMEM] * 5,
-        out_specs=[VMEM] * 3,
+        kernel,
+        out_shape=[jax.ShapeDtypeStruct((n, 256), BF) for n in sizes],
+        in_specs=[VMEM] * len(args),
+        out_specs=[VMEM] * len(sizes),
         compiler_params=limit(4),
         cost_estimate=cost(4),
-        name="pack",
+        name=name,
     )(*args)
 
 
@@ -531,9 +536,14 @@
 
     one_up = turn(scaled, 1)
     two_down = turn(scaled, -2)
-    arrived, one_up, two_down = lax.optimization_barrier((arrived, one_up, two_down))
-
-    cond, to_below, to_above = pack_call(arrived, one_up, scaled, own_parts, two_down)
+    scaled, own_parts = small_call(hold_kernel, "hold", (16, 32), scaled, own_parts)
+    arrived, one_up, two_down, scaled, own_parts = lax.optimization_barrier(
+        (arrived, one_up, two_down, scaled, own_parts)
+    )
+
+    cond, to_below, to_above = small_call(
+        pack_kernel, "pack", (128, 160, 176), arrived, one_up, scaled, own_parts, two_down
+    )
     near_up = turn(to_below, 1)
     near_down = turn(to_above, -1)
     cond_far = turn(cond, -2)

time: 75 us -> 74.5 us (level)
  waiting for transfers between devices: 12.9 us -> 11.6 us
    ppermute x7, waiting for transfers between devices: 12.9 us -> 11.6 us  [turn(): return lax.ppermute(x, 'tile', [(i, (i + by) % n) for i in range(n)])]
where the time goes in v9:
time: 74.5 us; the launch traced here: 73.9 us
  starting transfers between devices  41 us (55%)
  Pallas kernels  18.2 us (24%)
  waiting for transfers between devices  11.6 us (16%)
  local copies, waits for them, and re-layouts  2.17 us (3%)
  between operations  0.88 us (1%)
    ppermute x7, starting transfers between devices, turn(): return lax.ppermute(x, 'tile', [(i, (i + by) % n) for i in range(n)])  28.4 us
    pallas_call x2, Pallas kernels, step_call(): pl.pallas_call(kernel, out_shape=outs, in_specs=[SMEM, SMEM] + [VMEM] * (...  14.4 us
    ppermute x7, waiting for transfers between devices, turn(): return lax.ppermute(x, 'tile', [(i, (i + by) % n) for i in range(n)])  11.6 us
    all_to_all x1, starting transfers between devices, per_device(): arrived = lax.all_to_all(partial, 'band', 0, 0, tiled=True)  9.45 us
    pallas_call x1, Pallas kernels, encode_call(): pl.pallas_call(encode_kernel, out_shape=[jax.ShapeDtypeStruct((8, 2 * cel...  3.74 us
    ppermute x1, starting transfers between devices, per_device(): top = lax.ppermute(scaled[:16], 'tile', [(0, 1)])  3.19 us
    unnamed x22, local copies, waits for them, and re-layouts  2.17 us
  transfers between devices with their start and end apart: 9, of which 3 were waited for; matrix products, arithmetic and copies ran while one was open for 0% of the time, Pallas kernels for 0%

profile of v9, /device:TPU:2, one launch (start us, length us, event | category | flops | bytes accessed | tf_op | source)
XLA Modules:
  0.0 73.9 jit_solution(6758950496467514434)
XLA Ops:
  0.7 0.0 copy-start.1
  0.7 0.0 copy-start.3
  0.7 0.0 copy-start.7
  0.7 0.0 copy-start.8
  0.7 3.7 %encode.1 = (bf16[8,128,256]{2,1,0:T(8,128)(2,1)}, f32[16,256]{1,0:T(8,128)}, bf16[16,256]{1,0:T(8,128)(2,1)}, bf16[32,256]{1,0:T(8,128)(2,1)}) custom-call(s32[8,64]{1,0:T(8,128)} %anchor_ref.1, s32[1]{0:T(128)S(6)} %copy.14.width_ref, f32[3]{0:T(128)} %sigma_ref.5, bf16[64,4480]{1,0:T(8,128)(2,1)} %blocks_ref.1, bf16[70,256]{1,0:T(8,128)(2,1)} %bitcast.9, ...), custom_call_target="tpu_custom_call" | custom-call | flops 1677721600 | bytes 1048576 | tf_op jit(solution)/shard_map/encode/pallas_call | solution.py:507
  4.4 0.0 copy-start.4
  4.5 0.0 copy-start.5
  4.5 9.5 %all-to-all-start = ((bf16[8,128,256]{2,1,0:T(8,128)(2,1)}), bf16[8,128,256]{2,1,0:T(8,128)(2,1)S(1)}, u32[]{:S(2)}, u32[]{:S(2)}) async-start(bf16[8,128,256]{2,1,0:T(8,128)(2,1)} %get-tuple-element.21), calls=%async_computation | async-start | bytes 1048576 | tf_op jit(solution)/shard_map/all_to_all | solution.py:535
  13.9 10.1 %collective-permute-start.1 = (bf16[16,256]{1,0:T(8,128)(2,1)}, bf16[16,256]{1,0:T(8,128)(2,1)S(1)}, u32[]{:S(2)}, u32[]{:S(2)}) collective-permute-start(bf16[16,256]{1,0:T(8,128)(2,1)} %get-tuple-element.22.scaled), channel_id=1, source_target_pairs={{0,62},{1,63},{2,0},{3,1},{4,2},{5,3},{6,4},{7,5},{8,6},{9,7},{10,... | collective-permute-start | bytes 24584 | tf_op jit(solution)/shard_map/ppermute | solution.py:421
  24.1 2.6 %collective-permute-start = (bf16[16,256]{1,0:T(8,128)(2,1)}, bf16[16,256]{1,0:T(8,128)(2,1)S(1)}, u32[]{:S(2)}, u32[]{:S(2)}) collective-permute-start(bf16[16,256]{1,0:T(8,128)(2,1)} %get-tuple-element.22.scaled), channel_id=1, source_target_pairs={{0,1},{1,2},{2,3},{3,4},{4,5},{5,6},{6,7},{7,8},{8,9},{9,10},{10,1... | collective-permute-start | bytes 24584 | tf_op jit(solution)/shard_map/ppermute | solution.py:421
  26.7 0.7 copy-done.6
  27.4 0.7 copy-done.9
  28.1 0.0 collective-permute-done.1.below.refs_5_
  28.1 5.0 %collective-permute-done.above = bf16[16,256]{1,0:T(8,128)(2,1)S(1)} collective-permute-done((bf16[16,256]{1,0:T(8,128)(2,1)}, bf16[16,256]{1,0:T(8,128)(2,1)S(1)}, u32[]{:S(2)}, u32[]{:S(2)}) %collective-permute-start) | collective-permute-done | bytes 8224 | tf_op jit(solution)/shard_map/ppermute | solution.py:421
  33.2 0.0 all-to-all-done.arrived
  33.2 0.1 pack.1
  33.2 1.9 %collective-permute-start.3 = (bf16[176,256]{1,0:T(8,128)(2,1)S(1)}, bf16[176,256]{1,0:T(8,128)(2,1)S(1)}, u32[]{:S(2)}, u32[]{:S(2)}) collective-permute-start(bf16[176,256]{1,0:T(8,128)(2,1)S(1)} %get-tuple-element.32), channel_id=1, source_target_pairs={{0,63},{1,0},{2,1},{3,2},{4,3},{5,4},{6,5},{7,6},{8,7},{9,8},{10,9... | collective-permute-start | bytes 270344 | tf_op jit(solution)/shard_map/ppermute | solution.py:421
  35.2 3.9 %collective-permute-start.2 = (bf16[160,256]{1,0:T(8,128)(2,1)S(1)}, bf16[160,256]{1,0:T(8,128)(2,1)S(1)}, u32[]{:S(2)}, u32[]{:S(2)}) collective-permute-start(bf16[160,256]{1,0:T(8,128)(2,1)S(1)} %get-tuple-element.31), channel_id=1, source_target_pairs={{0,1},{1,2},{2,3},{3,4},{4,5},{5,6},{6,7},{7,8},{8,9},{9,10},{10,1... | collective-permute-start | bytes 245768 | tf_op jit(solution)/shard_map/ppermute | solution.py:421
  39.1 1.9 %collective-permute-start.4 = (bf16[128,256]{1,0:T(8,128)(2,1)S(1)}, bf16[128,256]{1,0:T(8,128)(2,1)S(1)}, u32[]{:S(2)}, u32[]{:S(2)}) collective-permute-start(bf16[128,256]{1,0:T(8,128)(2,1)S(1)} %get-tuple-element.33.refs_2_), channel_id=1, source_target_pairs={{0,62},{1,63},{2,0},{3,1},{4,2},{5,3},{6,4},{7,5},{8,6},{9,7},{10,... | collective-permute-start | bytes 196616 | tf_op jit(solution)/shard_map/ppermute | solution.py:421
  41.0 5.4 %collective-permute-done.4.refs_3_ = bf16[128,256]{1,0:T(8,128)(2,1)S(1)} collective-permute-done((bf16[128,256]{1,0:T(8,128)(2,1)S(1)}, bf16[128,256]{1,0:T(8,128)(2,1)S(1)}, u32[]{:S(2)}, u32[]{:S(2)}) %collective-permute-start.4) | collective-permute-done | bytes 65568 | tf_op jit(solution)/shard_map/ppermute | solution.py:421
  46.4 0.0 collective-permute-done.2.refs_0_
  46.4 0.0 collective-permute-done.3.refs_1_
  46.5 0.0 copy-start.10
  46.5 0.7 copy-done.10
  47.2 7.9 %step0.1 = (f32[32,256]{1,0:T(8,128)S(1)}, bf16[32,256]{1,0:T(8,128)(2,1)S(1)}) custom-call(s32[1]{0:T(128)S(6)} %copy.14.width_ref, f32[3]{0:T(128)S(1)} %copy-done.7, bf16[160,256]{1,0:T(8,128)(2,1)S(1)} %collective-permute-done.2.refs_0_, bf16[176,256]{1,0:T(8,128)(2,1)S(1)} %collective-permute-done.3.refs_1_, ...), custom_call_target="tpu_custom_call" | custom-call | flops 5033164800 | bytes 1048576 | tf_op jit(solution)/shard_map/step0/pallas_call | solution.py:473
  55.1 1.9 %collective-permute-start.5 = (bf16[32,256]{1,0:T(8,128)(2,1)S(1)}, bf16[32,256]{1,0:T(8,128)(2,1)S(1)}, u32[]{:S(2)}, u32[]{:S(2)}) collective-permute-start(bf16[32,256]{1,0:T(8,128)(2,1)S(1)} %get-tuple-element.36), channel_id=1, source_target_pairs={{0,2},{1,3},{2,4},{3,5},{4,6},{5,7},{6,8},{7,9},{8,10},{9,11},{10,... | collective-permute-start | bytes 49160 | tf_op jit(solution)/shard_map/ppermute | solution.py:421
  57.0 3.2 %collective-permute-start.7 = (bf16[16,256]{1,0:T(8,128)(2,1)S(1)}, bf16[16,256]{1,0:T(8,128)(2,1)S(1)}, u32[]{:S(2)}, u32[]{:S(2)}) collective-permute-start(bf16[16,256]{1,0:T(8,128)(2,1)S(1)} %get-tuple-element.37), channel_id=1, source_target_pairs={{0,1},{64,65},{128,129},{192,193},{256,257},{320,321},{384,385},{4... | collective-permute-start | bytes 24584 | tf_op jit(solution)/shard_map/ppermute | solution.py:555
  60.2 6.0 %collective-permute-start.6 = (bf16[16,256]{1,0:T(8,128)(2,1)S(1)}, bf16[16,256]{1,0:T(8,128)(2,1)S(1)}, u32[]{:S(2)}, u32[]{:S(2)}) collective-permute-start(bf16[16,256]{1,0:T(8,128)(2,1)S(1)} %get-tuple-element.38), channel_id=1, source_target_pairs={{0,63},{1,0},{2,1},{3,2},{4,3},{5,4},{6,5},{7,6},{8,7},{9,8},{10,9... | collective-permute-start | bytes 24584 | tf_op jit(solution)/shard_map/ppermute | solution.py:421
  66.2 0.0 collective-permute-done.7.refs_7_
  66.2 1.2 %collective-permute-done.6.refs_6_ = bf16[16,256]{1,0:T(8,128)(2,1)S(1)} collective-permute-done((bf16[16,256]{1,0:T(8,128)(2,1)S(1)}, bf16[16,256]{1,0:T(8,128)(2,1)S(1)}, u32[]{:S(2)}, u32[]{:S(2)}) %collective-permute-start.6) | collective-permute-done | bytes 8224 | tf_op jit(solution)/shard_map/ppermute | solution.py:421
  67.3 0.0 collective-permute-done.5.refs_5_
  67.3 6.5 %step1.1 = f32[4,4,256]{2,1,0:T(4,128)} custom-call(s32[1]{0:T(128)S(6)} %copy.14.width_ref, f32[3]{0:T(128)S(1)} %copy-done.7, bf16[160,256]{1,0:T(8,128)(2,1)S(1)} %collective-permute-done.2.refs_0_, bf16[176,256]{1,0:T(8,128)(2,1)S(1)} %collective-permute-done.3.refs_1_, bf16[128,256]{1,0:T(8,128)(2,1)S(1)} %get-tuple-element.33.refs_2_, ...), custom_call_target="tpu_custom_call" | custom-call | flops 5033164800 | bytes 1048576 | tf_op jit(solution)/shard_map/step1/pallas_call | solution.py:473
  (14 shorter events, 0.0 us)
Async XLA Ops:
  0.7 45.8 %copy-start.1 = (bf16[9,128,384]{2,1,0:T(8,128)(2,1)S(1)}, bf16[9,128,384]{2,1,0:T(8,128)(2,1)}, u32[]{:S(2)}) copy-start(bf16[9,128,384]{2,1,0:T(8,128)(2,1)} %refs_14_.1) | copy-start | bytes 2654212
  0.7 45.8 %copy-start.3 = (bf16[9,128,128]{2,1,0:T(8,128)(2,1)S(1)}, bf16[9,128,128]{2,1,0:T(8,128)(2,1)}, u32[]{:S(2)}) copy-start(bf16[9,128,128]{2,1,0:T(8,128)(2,1)} %refs_11_.3) | copy-start | bytes 884740
  0.7 45.8 %copy-start.7 = (f32[3]{0:T(128)S(1)}, f32[3]{0:T(128)}, u32[]{:S(2)}) copy-start(f32[3]{0:T(128)} %sigma_ref.5) | copy-start | bytes 40
  0.7 45.8 %copy-start.8 = (f32[128]{0:T(128)S(1)}, f32[128]{0:T(128)}, u32[]{:S(2)}) copy-start(f32[128]{0:T(128)} %param.20) | copy-start | bytes 1540
  4.4 42.0 %copy-start = (bf16[9,256,256]{2,1,0:T(8,128)(2,1)S(1)}, bf16[9,256,256]{2,1,0:T(8,128)(2,1)}, u32[]{:S(2)}) copy-start(bf16[9,256,256]{2,1,0:T(8,128)(2,1)} %refs_13_.1) | copy-start | bytes 3538948
  4.4 42.0 %copy-start.2 = (bf16[9,256,128]{2,1,0:T(8,128)(2,1)S(1)}, bf16[9,256,128]{2,1,0:T(8,128)(2,1)}, u32[]{:S(2)}) copy-start(bf16[9,256,128]{2,1,0:T(8,128)(2,1)} %refs_12_.3) | copy-start | bytes 1769476
  4.4 42.0 %copy-start.4 = (bf16[9,128,4]{1,2,0:T(4,128)(2,1)S(1)}, bf16[9,128,4]{1,2,0:T(4,128)(2,1)}, u32[]{:S(2)}) copy-start(bf16[9,128,4]{1,2,0:T(4,128)(2,1)} %param.19) | copy-start | bytes 27652
  4.5 42.0 %copy-start.5 = (bf16[9,4,128]{2,1,0:T(4,128)(2,1)S(1)}, bf16[9,4,128]{2,1,0:T(4,128)(2,1)}, u32[]{:S(2)}) copy-start(bf16[9,4,128]{2,1,0:T(4,128)(2,1)} %refs_10_.3) | copy-start | bytes 27652
  4.5 28.7 %all-to-all-start = ((bf16[8,128,256]{2,1,0:T(8,128)(2,1)}), bf16[8,128,256]{2,1,0:T(8,128)(2,1)S(1)}, u32[]{:S(2)}, u32[]{:S(2)}) async-start(bf16[8,128,256]{2,1,0:T(8,128)(2,1)} %get-tuple-element.21), calls=%async_computation | async-start | bytes 1048576 | tf_op jit(solution)/shard_map/all_to_all | solution.py:535
  13.9 14.2 %collective-permute-start.1 = (bf16[16,256]{1,0:T(8,128)(2,1)}, bf16[16,256]{1,0:T(8,128)(2,1)S(1)}, u32[]{:S(2)}, u32[]{:S(2)}) collective-permute-start(bf16[16,256]{1,0:T(8,128)(2,1)} %get-tuple-element.22.scaled), channel_id=1, source_target_pairs={{0,62},{1,63},{2,0},{3,1},{4,2},{5,3},{6,4},{7,5},{8,6},{9,7},{10,... | collective-permute-start | bytes 24584 | tf_op jit(solution)/shard_map/ppermute | solution.py:421
  24.1 9.1 %collective-permute-start = (bf16[16,256]{1,0:T(8,128)(2,1)}, bf16[16,256]{1,0:T(8,128)(2,1)S(1)}, u32[]{:S(2)}, u32[]{:S(2)}) collective-permute-start(bf16[16,256]{1,0:T(8,128)(2,1)} %get-tuple-element.22.scaled), channel_id=1, source_target_pairs={{0,1},{1,2},{2,3},{3,4},{4,5},{5,6},{6,7},{7,8},{8,9},{9,10},{10,1... | collective-permute-start | bytes 24584 | tf_op jit(solution)/shard_map/ppermute | solution.py:421
  26.7 0.7 copy-start.6
  27.4 0.7 copy-start.9
  33.2 13.2 %collective-permute-start.3 = (bf16[176,256]{1,0:T(8,128)(2,1)S(1)}, bf16[176,256]{1,0:T(8,128)(2,1)S(1)}, u32[]{:S(2)}, u32[]{:S(2)}) collective-permute-start(bf16[176,256]{1,0:T(8,128)(2,1)S(1)} %get-tuple-element.32), channel_id=1, source_target_pairs={{0,63},{1,0},{2,1},{3,2},{4,3},{5,4},{6,5},{7,6},{8,7},{9,8},{10,9... | collective-permute-start | bytes 270344 | tf_op jit(solution)/shard_map/ppermute | solution.py:421
  35.2 11.2 %collective-permute-start.2 = (bf16[160,256]{1,0:T(8,128)(2,1)S(1)}, bf16[160,256]{1,0:T(8,128)(2,1)S(1)}, u32[]{:S(2)}, u32[]{:S(2)}) collective-permute-start(bf16[160,256]{1,0:T(8,128)(2,1)S(1)} %get-tuple-element.31), channel_id=1, source_target_pairs={{0,1},{1,2},{2,3},{3,4},{4,5},{5,6},{6,7},{7,8},{8,9},{9,10},{10,1... | collective-permute-start | bytes 245768 | tf_op jit(solution)/shard_map/ppermute | solution.py:421
  39.1 7.3 %collective-permute-start.4 = (bf16[128,256]{1,0:T(8,128)(2,1)S(1)}, bf16[128,256]{1,0:T(8,128)(2,1)S(1)}, u32[]{:S(2)}, u32[]{:S(2)}) collective-permute-start(bf16[128,256]{1,0:T(8,128)(2,1)S(1)} %get-tuple-element.33.refs_2_), channel_id=1, source_target_pairs={{0,62},{1,63},{2,0},{3,1},{4,2},{5,3},{6,4},{7,5},{8,6},{9,7},{10,... | collective-permute-start | bytes 196616 | tf_op jit(solution)/shard_map/ppermute | solution.py:421
  46.5 0.7 copy-start.10
  55.1 12.3 %collective-permute-start.5 = (bf16[32,256]{1,0:T(8,128)(2,1)S(1)}, bf16[32,256]{1,0:T(8,128)(2,1)S(1)}, u32[]{:S(2)}, u32[]{:S(2)}) collective-permute-start(bf16[32,256]{1,0:T(8,128)(2,1)S(1)} %get-tuple-element.36), channel_id=1, source_target_pairs={{0,2},{1,3},{2,4},{3,5},{4,6},{5,7},{6,8},{7,9},{8,10},{9,11},{10,... | collective-permute-start | bytes 49160 | tf_op jit(solution)/shard_map/ppermute | solution.py:421
  57.0 9.2 %collective-permute-start.7 = (bf16[16,256]{1,0:T(8,128)(2,1)S(1)}, bf16[16,256]{1,0:T(8,128)(2,1)S(1)}, u32[]{:S(2)}, u32[]{:S(2)}) collective-permute-start(bf16[16,256]{1,0:T(8,128)(2,1)S(1)} %get-tuple-element.37), channel_id=1, source_target_pairs={{0,1},{64,65},{128,129},{192,193},{256,257},{320,321},{384,385},{4... | collective-permute-start | bytes 24584 | tf_op jit(solution)/shard_map/ppermute | solution.py:555
  60.2 7.1 %collective-permute-start.6 = (bf16[16,256]{1,0:T(8,128)(2,1)S(1)}, bf16[16,256]{1,0:T(8,128)(2,1)S(1)}, u32[]{:S(2)}, u32[]{:S(2)}) collective-permute-start(bf16[16,256]{1,0:T(8,128)(2,1)S(1)} %get-tuple-element.38), channel_id=1, source_target_pairs={{0,63},{1,0},{2,1},{3,2},{4,3},{5,4},{6,5},{7,6},{8,7},{9,8},{10,9... | collective-permute-start | bytes 24584 | tf_op jit(solution)/shard_map/ppermute | solution.py:421
